TPU v7x, 512 devices: a whole 4x8x8 slice. The times are simulated.
512 devices in a mesh: dp: 32 (over x, z), tensor: 4 (over y_lo), group: 4 (over y_hi, core).
Axes of the slice: x: 4, y: 8 (y_hi: 2, y_lo: 4; y = y_hi * 4 + y_lo), z: 8, core: 2. Of those that a mesh axis runs over, the one named last changes fastest.
Arguments:
- image_in: bfloat16 [128, 256, 1408], P(('dp', 'group')), may hold values from -6 to 6
- enc_gain: float32 [1408], replicated, may hold values from 0.1 to 1.9
- enc_up: bfloat16 [1408, 4096], P('group', 'tensor'), may hold values from -0.15625 to 0.15625
- enc_down: bfloat16 [4096, 1408], P('tensor', 'group'), may hold values from -0.09375 to 0.09375
- text_in: bfloat16 [128, 128, 2048], P('dp', ('tensor', 'group')), may hold values from -6 to 6
- query_gain: float32 [2048], replicated, may hold values from 0.5 to 2
- w_query: bfloat16 [2048, 2048], P(None, ('tensor', 'group')), may hold values from -0.125 to 0.125
- w_key: bfloat16 [1408, 2048], P(None, ('tensor', 'group')), may hold values from -0.15625 to 0.15625
- w_value: bfloat16 [1408, 2048], P(None, ('tensor', 'group')), may hold values from -0.15625 to 0.15625
- w_out: bfloat16 [2048, 2048], P(('tensor', 'group')), may hold values from -0.125 to 0.125
- cotangent: bfloat16 [128, 128, 2048], P('dp', ('tensor', 'group')), may hold values from -6 to 6
Outputs:
- image_grad: bfloat16 [128, 256, 1408], P(('dp', 'group'))
- key_grad: float32 [1408, 2048], P('dp', ('tensor', 'group'))
- value_grad: float32 [1408, 2048], P('dp', ('tensor', 'group'))
All inputs are finite; a program needn't handle non-finite values.
Results may differ from a plain program's by a relative error of at most 0.035.
Values may be sent and summed in bfloat16 or wider, within the bound.
No kernel may reach another device: no remote copies, remote signals or barrier semaphores. Data moves between devices by JAX's collectives and lax.ppermute only.
A program may use at most 64 MiB of HBM per device.

v0:
```python
import jax
import jax.numpy as jnp
from jax import lax
from jax.sharding import PartitionSpec as P

HEAD_DIM = 128


EPSILON = 1e-06


def layer_norm(values, gain):
    floats = values.astype(jnp.float32)
    centre = jnp.mean(floats, axis=-1, keepdims=True)
    spread = jnp.mean(jnp.square(floats - centre), axis=-1, keepdims=True)
    inverse = lax.rsqrt(spread + EPSILON)
    normal = (floats - centre) * inverse
    return (normal * gain, normal, inverse)


def gelu_tanh(values):
    return jax.nn.gelu(values, approximate=True)


def local(
    image_in,
    enc_gain,
    enc_up,
    enc_down,
    text_in,
    query_gain,
    w_query,
    w_key,
    w_value,
    w_out,
    cotangent,
):
    images, patches, width = image_in.shape
    up_full, down_full = (
        lax.all_gather(enc_up, "group", axis=0, tiled=True),
        lax.all_gather(enc_down, "group", axis=1, tiled=True),
    )
    flat_in = image_in.reshape(images * patches, width)
    scaled, normal, inverse = layer_norm(flat_in, enc_gain)
    normed = scaled.astype(jnp.bfloat16)
    pre_act = jnp.dot(normed, up_full, preferred_element_type=jnp.float32)
    activated = gelu_tanh(pre_act).astype(jnp.bfloat16)
    branch_part = jnp.dot(activated, down_full, preferred_element_type=jnp.float32)
    branch = lax.psum(branch_part.astype(jnp.bfloat16), "tensor").astype(jnp.float32)
    encoded = (
        (flat_in.astype(jnp.float32) + branch).astype(jnp.bfloat16).reshape(images, patches, width)
    )
    encoded_all = lax.all_gather(encoded, "group", axis=0, tiled=True)
    block_images = encoded_all.shape[0]
    text_all, cot_all = (
        lax.all_gather(text_in, ("tensor", "group"), axis=1, tiled=True),
        lax.all_gather(cotangent, ("tensor", "group"), axis=1, tiled=True),
    )
    text_len = text_all.shape[1]
    dec_width = text_all.shape[2]
    head_cols = w_query.shape[1]
    heads_here = head_cols // HEAD_DIM
    text_scaled, text_normal, text_inverse = layer_norm(text_all, query_gain)
    text_normed = text_scaled.astype(jnp.bfloat16)
    query = (
        jnp.dot(text_normed.reshape(-1, dec_width), w_query, preferred_element_type=jnp.float32)
        * HEAD_DIM ** (-0.5)
    ).astype(jnp.bfloat16)
    query = query.reshape(block_images, text_len, heads_here, HEAD_DIM)
    pair_weight = jnp.concatenate([w_key, w_value], axis=1)
    key_value = jnp.dot(
        encoded_all.reshape(-1, width), pair_weight, preferred_element_type=jnp.float32
    ).astype(jnp.bfloat16)
    key_value = key_value.reshape(block_images, patches, 2, heads_here, HEAD_DIM)
    keys = key_value[:, :, 0]
    values = key_value[:, :, 1]
    d_attn = lax.dot_general(
        cot_all.reshape(-1, dec_width),
        w_out,
        (((1,), (1,)), ((), ())),
        preferred_element_type=jnp.float32,
    ).astype(jnp.bfloat16)
    d_attn = d_attn.reshape(block_images, text_len, heads_here, HEAD_DIM)
    scores = jnp.einsum("ithe,iphe->ihtp", query, keys, preferred_element_type=jnp.float32)
    top = jnp.max(scores, axis=-1, keepdims=True)
    expo = jnp.exp(scores - top)
    probs = expo / jnp.sum(expo, axis=-1, keepdims=True)
    d_probs = jnp.einsum("ithe,iphe->ihtp", d_attn, values, preferred_element_type=jnp.float32)
    d_scores = (probs * (d_probs - jnp.sum(probs * d_probs, axis=-1, keepdims=True))).astype(
        jnp.bfloat16
    )
    probs_low = probs.astype(jnp.bfloat16)
    d_keys = jnp.einsum(
        "ihtp,ithe->iphe", d_scores, query, preferred_element_type=jnp.float32
    ).astype(jnp.bfloat16)
    d_values = jnp.einsum(
        "ihtp,ithe->iphe", probs_low, d_attn, preferred_element_type=jnp.float32
    ).astype(jnp.bfloat16)
    d_pair = jnp.stack([d_keys, d_values], axis=2).reshape(block_images, patches, 2 * head_cols)
    weight_term = jnp.einsum("ipd,ipc->dc", encoded_all, d_pair, preferred_element_type=jnp.float32)
    weight_sum = lax.psum_scatter(
        weight_term.astype(jnp.bfloat16), "dp", scatter_dimension=0, tiled=True
    ).astype(jnp.float32)
    key_grad = weight_sum[:, :head_cols]
    value_grad = weight_sum[:, head_cols:]
    tensor_count = lax.axis_size("tensor")
    token_blocks = d_pair.reshape(
        block_images, tensor_count, patches // tensor_count, 2 * head_cols
    )
    term = jnp.einsum(
        "itpc,dc->tipd", token_blocks, pair_weight, preferred_element_type=jnp.float32
    )
    term = term.reshape(tensor_count * block_images, patches // tensor_count, width)
    own_block = lax.psum_scatter(
        term.astype(jnp.bfloat16), ("tensor", "group"), scatter_dimension=0, tiled=True
    )
    d_encoded = lax.all_gather(own_block, "tensor", axis=1, tiled=True)
    flat_grad = d_encoded.reshape(images * patches, width)
    d_act = lax.dot_general(
        flat_grad, down_full, (((1,), (1,)), ((), ())), preferred_element_type=jnp.float32
    )
    d_pre = jax.vjp(gelu_tanh, pre_act)[1](d_act)[0].astype(jnp.bfloat16)
    d_norm_part = lax.dot_general(
        d_pre, up_full, (((1,), (1,)), ((), ())), preferred_element_type=jnp.float32
    )
    d_normed = lax.psum(d_norm_part.astype(jnp.bfloat16), "tensor").astype(jnp.float32)
    scaled_grad = d_normed * enc_gain
    d_input = inverse * (
        scaled_grad
        - jnp.mean(scaled_grad, axis=-1, keepdims=True)
        - normal * jnp.mean(scaled_grad * normal, axis=-1, keepdims=True)
    )
    image_grad = (
        (flat_grad.astype(jnp.float32) + d_input)
        .astype(jnp.bfloat16)
        .reshape(images, patches, width)
    )
    return (image_grad, key_grad, value_grad)


def solution(mesh):
    in_specs = (
        P(("dp", "group"), None, None),
        P(),
        P("group", "tensor"),
        P("tensor", "group"),
        P("dp", ("tensor", "group"), None),
        P(),
        P(None, ("tensor", "group")),
        P(None, ("tensor", "group")),
        P(None, ("tensor", "group")),
        P(("tensor", "group"), None),
        P("dp", ("tensor", "group"), None),
    )
    out_specs = (
        P(("dp", "group"), None, None),
        P("dp", ("tensor", "group")),
        P("dp", ("tensor", "group")),
    )
    return jax.shard_map(local, mesh=mesh, in_specs=in_specs, out_specs=out_specs, check_vma=False)
```

profile of v0, /device:TPU:56, one launch (start us, length us, event | category | flops | bytes accessed | tf_op | source)
XLA Modules:
  0.0 590.6 jit_solution(2485152381775829591)
XLA Ops:
  8.0 0.0 copy-start
  8.0 0.0 all-gather.9.cloned.1.call-start
  8.1 0.7 all-gather.9.cloned.1.call-update
  8.8 0.0 all-gather.11.cloned.1.call-start
  8.8 0.7 all-gather.11.cloned.1.call-update
  9.5 0.0 all-reduce.5.cloned.1.call-start
  9.6 1.3 convert_reduce_fusion.1
  10.9 0.3 fusion.22
  11.2 51.1 %all-gather.9.cloned.1.call-done = bf16[1408,1024]{1,0:T(8,128)(2,1)} async-done(((bf16[352,1024]{1,0:T(8,128)(2,1)}), bf16[1408,1024]{1,0:T(8,128)(2,1)}) %all-gather.9.cloned.1.call-update) | async-done | bytes 2883600 | tf_op jit(solution)/shard_map/all_gather | solution.py:40
  62.3 2.8 fusion.38
  65.2 50.2 %all-gather.11.cloned.1.call-done = bf16[1024,1408]{0,1:T(8,128)(2,1)} async-done(((bf16[1024,352]{0,1:T(8,128)(2,1)}), bf16[1024,1408]{0,1:T(8,128)(2,1)}) %all-gather.11.cloned.1.call-update) | async-done | bytes 2883600 | tf_op jit(solution)/shard_map/all_gather | solution.py:41
  115.4 3.8 convolution_convert_fusion.2
  119.2 0.0 all-reduce.5.cloned.1.call-update
  119.2 0.0 copy-start.4
  119.2 0.0 all-gather.7.cloned.1.call-start
  119.2 0.5 all-gather.7.cloned.1.call-update
  119.8 0.0 all-gather.13.cloned.1.call-start
  119.8 0.5 all-gather.13.cloned.1.call-update
  120.4 0.0 all-gather.15.cloned.1.call-start
  120.4 78.1 %all-reduce.5.cloned.1.call-done = bf16[256,1408]{1,0:T(8,128)(2,1)} async-done(((bf16[256,1408]{1,0:T(8,128)(2,1)}), bf16[256,1408]{1,0:T(8,128)(2,1)}) %all-reduce.5.cloned.1.call-update) | async-done | bytes 720912 | tf_op jit(solution)/shard_map/psum | solution.py:49
  198.6 2.1 fusion.23
  200.7 0.0 all-gather.15.cloned.1.call-update
  200.7 0.0 reduce-scatter.4.cloned.1.call-start
  200.8 0.8 constant_dynamic-update-slice_fusion.1
  201.6 0.8 constant_dynamic-update-slice_fusion
  202.3 14.6 %all-gather.7.cloned.1.call-done = bf16[4,128,2048]{2,1,0:T(8,128)(2,1)} async-done(((bf16[4,8,2048]{2,1,0:T(8,128)(2,1)}), bf16[4,128,2048]{2,1,0:T(8,128)(2,1)}) %all-gather.7.cloned.1.call-update) | async-done | bytes 2097168 | tf_op jit(solution)/shard_map/all_gather | solution.py:56
  217.0 2.1 convert_reduce_fusion
  219.1 0.1 copy-done.1
  219.2 0.7 fusion.4
  219.9 83.8 %all-gather.13.cloned.1.call-done = bf16[4,128,2048]{2,1,0:T(8,128)(2,1)} async-done(((bf16[4,8,2048]{2,1,0:T(8,128)(2,1)}), bf16[4,128,2048]{2,1,0:T(8,128)(2,1)}) %all-gather.13.cloned.1.call-update) | async-done | bytes 2097168 | tf_op jit(solution)/shard_map/all_gather | solution.py:57
  303.7 2.3 convolution_convert_fusion.6
  306.1 0.0 copy-start.7
  306.1 0.7 fusion.6
  306.8 0.3 copy-done.7
  307.1 0.7 fusion.29
  307.8 48.0 %all-gather.15.cloned.1.call-done = bf16[1024,1408]{1,0:T(8,128)(2,1)} async-done(((bf16[256,1408]{1,0:T(8,128)(2,1)}), bf16[1024,1408]{1,0:T(8,128)(2,1)}) %all-gather.15.cloned.1.call-update) | async-done | bytes 2883600 | tf_op jit(solution)/shard_map/all_gather | solution.py:53
  355.9 3.0 convolution_convert_fusion.3
  358.8 0.1 reshape.127
  358.9 0.7 fusion.74
  359.7 0.4 fusion.76
  360.1 0.3 fusion.28
  360.4 0.3 multiply_reduce_fusion
  360.8 0.4 fusion.27
  361.2 0.1 pad_maximum_fusion
  361.2 0.4 copy.33
  361.7 0.3 reshape_reshape.3
  362.0 2.1 fusion.7
  364.1 1.9 copy.34
  366.1 0.0 reduce-scatter.4.cloned.1.call-update
  366.1 0.0 all-reduce.7.cloned.1.call-start
  366.2 2.8 fusion.8
  369.0 96.2 %reduce-scatter.4.cloned.1.call-done = bf16[1,64,1408]{2,1,0:T(8,128)(2,1)} async-done(((bf16[16,64,1408]{2,1,0:T(8,128)(2,1)}), bf16[1,64,1408]{2,1,0:T(8,128)(2,1)}) %reduce-scatter.4.cloned.1.call-update) | async-done | bytes 180240 | tf_op jit(solution)/shard_map/reduce_scatter | solution.py:114
  465.2 21.1 %all_gather.23 = bf16[1,256,1408]{2,1,0:T(8,128)(2,1)S(1)} all-gather(bf16[1,64,1408]{2,1,0:T(8,128)(2,1)} %reduce-scatter.4.cloned.1.call-done), channel_id=1, replica_groups=mesh['dp'=32,'tensor'=4,'group'=4] {'tensor'}, dimensions={1}, use_global_device_ids=true | all-gather | bytes 901120 | tf_op jit(solution)/shard_map/all_gather | solution.py:117
  486.3 6.1 %convolution_convert_fusion.1 = bf16[256,1408]{1,0:T(8,128)(2,1)} fusion(bf16[1408,1024]{1,0:T(8,128)(2,1)} %all-gather.9.cloned.1.call-done, f32[256,1024]{1,0:T(8,128)} %copy-done.8, bf16[1024,1408]{0,1:T(8,128)(2,1)} %all-gather.11.cloned.1.call-done, bf16[1,256,1408]{2,1,0:T(8,128)(2,1)S(1)} %all_gather.23), kind=kOutput, calls=%fused_computation.11 | convolution fusion | flops 1481998336 | bytes 8257536 | tf_op jit(solution)/shard_map/dot_general | solution.py:123
  492.4 0.0 all-reduce.7.cloned.1.call-update
  492.4 79.6 %fusion = bf16[48,256]{1,0:T(8,128)(2,1)S(1)} fusion(bf16[1408,256]{1,0:T(8,128)(2,1)S(1)} %fusion.8), kind=kCustom, calls=%all-reduce-scatter | all-reduce-scatter fusion | flops 393217 | bytes 747520
  572.0 1.3 collective-permute-start.1
  573.3 1.3 collective-permute-start
  574.6 1.3 collective-permute-start.2
  575.9 1.3 dynamic-slice.4
  577.8 0.5 concatenate.4
  578.4 0.6 fusion.75
  579.0 1.6 fusion.24
  580.6 2.6 fusion.37
  (25 shorter events, 0.1 us)
Async XLA Ops:
  8.0 295.7 %copy-start = (bf16[128,2048]{1,0:T(8,128)(2,1)S(1)}, bf16[128,2048]{1,0:T(8,128)(2,1)}, u32[]{:S(2)}) copy-start(bf16[128,2048]{1,0:T(8,128)(2,1)} %param.20) | copy-start | bytes 1572868
  8.0 2.8 copy-start.2
  8.0 54.3 %copy-start.5 = (f32[1408]{0:T(1024)S(1)}, f32[1408]{0:T(1024)}, u32[]{:S(2)}) copy-start(f32[1408]{0:T(1024)} %param.12) | copy-start | bytes 16900
  8.0 54.3 %all-gather.9.cloned.1.call-start = ((), (), s32[]{:S(2)}) async-start(), calls=%async_computation.2 | async-start | bytes 3604480 | tf_op jit(solution)/shard_map/all_gather | solution.py:40
  8.8 106.6 %all-gather.11.cloned.1.call-start = ((), (), s32[]{:S(2)}) async-start(), calls=%async_computation.3 | async-start | bytes 3604480 | tf_op jit(solution)/shard_map/all_gather | solution.py:41
  9.5 189.0 %all-reduce.5.cloned.1.call-start = ((), (), s32[]{:S(2)}) async-start(), calls=%async_computation.4 | async-start | bytes 1441792 | tf_op jit(solution)/shard_map/psum | solution.py:49
  65.2 50.2 %copy-start.8 = (f32[256,1024]{1,0:T(8,128)}, f32[256,1024]{1,0:T(8,128)S(1)}, u32[]{:S(2)}) copy-start(f32[256,1024]{1,0:T(8,128)S(1)} %fusion.38) | copy-start | bytes 3145732
  119.2 81.6 %copy-start.3 = (bf16[1408,128]{1,0:T(8,128)(2,1)S(1)}, bf16[1408,128]{1,0:T(8,128)(2,1)}, u32[]{:S(2)}) copy-start(bf16[1408,128]{1,0:T(8,128)(2,1)} %param.18) | copy-start | bytes 1081348
  119.2 82.4 %copy-start.4 = (bf16[1408,128]{1,0:T(8,128)(2,1)S(1)}, bf16[1408,128]{1,0:T(8,128)(2,1)}, u32[]{:S(2)}) copy-start(bf16[1408,128]{1,0:T(8,128)(2,1)} %param.19) | copy-start | bytes 1081348
  119.2 97.8 %all-gather.7.cloned.1.call-start = ((), (), s32[]{:S(2)}) async-start(), calls=%async_computation.1 | async-start | bytes 2228224 | tf_op jit(solution)/shard_map/all_gather | solution.py:56
  119.8 184.0 %all-gather.13.cloned.1.call-start = ((), (), s32[]{:S(2)}) async-start(), calls=%async_computation.5 | async-start | bytes 2228224 | tf_op jit(solution)/shard_map/all_gather | solution.py:57
  120.4 235.5 %all-gather.15.cloned.1.call-start = ((), (), s32[]{:S(2)}) async-start(), calls=%async_computation.8 | async-start | bytes 3604480 | tf_op jit(solution)/shard_map/all_gather | solution.py:53
  200.7 264.4 %reduce-scatter.4.cloned.1.call-start = ((), (), s32[]{:S(2)}) async-start(), calls=%async_computation.6 | async-start | bytes 3063808 | tf_op jit(solution)/shard_map/reduce_scatter | solution.py:114
  217.0 2.2 copy-start.1
  219.2 86.9 %copy-start.6 = (f32[2048]{0:T(1024)S(1)}, f32[2048]{0:T(1024)}, u32[]{:S(2)}) copy-start(f32[2048]{0:T(1024)} %param.16) | copy-start | bytes 24580
  306.1 1.0 copy-start.7
  366.1 212.9 %all-reduce.7.cloned.1.call-start = ((), (), s32[]{:S(2)}) async-start(), calls=%async_computation.7 | async-start | bytes 1441792 | tf_op jit(solution)/shard_map/psum | solution.py:126
  572.0 5.8 collective-permute-start.1
  573.3 4.6 collective-permute-start
  574.6 3.2 collective-permute-start.2
Sparse Core Ops, SparseCore 0:
  11.0 51.2 all-gather.8
  64.4 50.9 all-gather.10
  119.3 79.2 all-reduce.4
  492.5 60.1 all-reduce.6
Sparse Core Ops, SparseCore 1:
  121.7 95.2 all-gather.6
  218.9 84.7 all-gather.12
  306.3 49.5 all-gather.14
  366.2 98.9 reduce-scatter.3
where the time goes:
time: 594 us; the launch traced here: 591 us
  waiting for transfers between devices  425 us (72%)
  blocking collectives  101 us (17%)
  matrix products  25.1 us (4%)
  between operations  16.4 us (3%)
  other arithmetic  11.5 us (2%)
  local copies, waits for them, and re-layouts  8.03 us (1%)
    reduce_scatter x1, waiting for transfers between devices, local(): lax.psum_scatter(term.astype(jnp.bfloat16), ('tensor', 'group'), scatter_...  96.2 us
    all_gather x1, waiting for transfers between devices, local(): lax.all_gather(cotangent, ('tensor', 'group'), axis=1, tiled=True)  83.8 us
    unnamed x1, blocking collectives  79.6 us
    psum x1, waiting for transfers between devices, local(): lax.psum(branch_part.astype(jnp.bfloat16), 'tensor').astype(jnp.float32)  78.1 us
    all_gather x1, waiting for transfers between devices, local(): lax.all_gather(enc_up, 'group', axis=0, tiled=True)  51.1 us
    all_gather x1, waiting for transfers between devices, local(): lax.all_gather(enc_down, 'group', axis=1, tiled=True)  50.2 us
    all_gather x1, waiting for transfers between devices, local(): encoded_all = lax.all_gather(encoded, 'group', axis=0, tiled=True)  48 us
    all_gather x1, blocking collectives, local(): d_encoded = lax.all_gather(own_block, 'tensor', axis=1, tiled=True)  21.1 us
  transfers between devices with their start and end apart: 11, of which 7 were waited for; matrix products, arithmetic and copies ran while one was open for 17% of the time, Pallas kernels for 0%

commit v1 on v0

v1 whole, which is shorter than its diff:
```python
import jax
import jax.numpy as jnp
from jax import lax
from jax.sharding import Mesh, PartitionSpec as P

HEAD_DIM = 128
EPSILON = 1e-06
BF = jnp.bfloat16
F32 = jnp.float32


def layer_norm(values, gain):
    floats = values.astype(F32)
    centre = jnp.mean(floats, axis=-1, keepdims=True)
    spread = jnp.mean(jnp.square(floats - centre), axis=-1, keepdims=True)
    inverse = lax.rsqrt(spread + EPSILON)
    normal = (floats - centre) * inverse
    return (normal * gain, normal, inverse)


def gelu_tanh(values):
    return jax.nn.gelu(values, approximate=True)


def shift(value, axis, by):
    size = lax.axis_size(axis)
    return lax.ppermute(value, axis, [(i, (i + by) % size) for i in range(size)])


def swap(value, axis, bit=1):
    size = lax.axis_size(axis)
    return lax.ppermute(value, axis, [(i, i ^ bit) for i in range(size)])


def rows_at(value, start, size):
    return lax.dynamic_slice_in_dim(value, start, size, axis=0)


def put(buffer, block, start):
    return lax.dynamic_update_slice_in_dim(buffer, block, start, axis=0)


def far_block(own, axis):
    quarter = own.shape[0] // 4
    mine = lax.rem(lax.axis_index(axis), 4)
    piece = swap(rows_at(own, mine * quarter, quarter), "yh")
    pieces = [piece, shift(piece, axis, -1), shift(piece, axis, 2), shift(piece, axis, 1)]
    block = jnp.zeros_like(own)
    for offset, part in enumerate(pieces):
        block = put(block, part, lax.rem(mine + offset, 4) * quarter)
    return block


def group_blocks(own, axis):
    far = far_block(own, axis)
    return own, far, swap(own, "core"), swap(far, "core")


def stacked(blocks, group):
    own, far, near, far_near = blocks
    rows = own.shape[0]
    buffer = jnp.zeros((4 * rows, own.shape[1]), own.dtype)
    buffer = put(buffer, own, group * rows)
    buffer = put(buffer, near, (group ^ 1) * rows)
    buffer = put(buffer, far, (group ^ 2) * rows)
    return put(buffer, far_near, (group ^ 3) * rows)


def scatter_sum(partial, axis):
    size = lax.axis_size(axis)
    rows = partial.shape[0] // size
    here = lax.axis_index(axis)
    total = rows_at(partial, here * rows, rows).astype(F32)
    for by in range(1, size):
        block = rows_at(partial, lax.rem(here + by, size) * rows, rows)
        total = total + shift(block, axis, by).astype(F32)
    return total


def gather_rows(block, axis):
    size = lax.axis_size(axis)
    rows = block.shape[0]
    here = lax.axis_index(axis)
    whole = jnp.zeros((size * rows,) + block.shape[1:], block.dtype)
    whole = put(whole, block, here * rows)
    for by in range(1, size):
        whole = put(whole, shift(block, axis, by), lax.rem(here - by + size, size) * rows)
    return whole


def halved(partial, axis, bit):
    half = partial.shape[0] // 2
    side = (lax.axis_index(axis) // bit) % 2
    sent = rows_at(partial, (1 - side) * half, half).astype(BF)
    return rows_at(partial, side * half, half) + swap(sent, axis, bit).astype(F32)


def local(
    image_in, enc_gain, enc_up, enc_down, text_in, query_gain, w_query, w_key, w_value, w_out, cotangent
):
    _, patches, width = image_in.shape
    group = lax.axis_index("yh") * 2 + lax.axis_index("core")
    tensor = lax.axis_index("tensor")
    flat_in = image_in.reshape(patches, width)

    up = stacked(group_blocks(enc_up, "x"), group)
    down = stacked(group_blocks(enc_down.T, "z"), group)
    packed = jnp.concatenate([w_key, w_value, w_query, w_out.T], axis=0)
    heads = group_blocks(packed, "x")
    dec = w_query.shape[0]
    pair_weight = jnp.concatenate(
        [part for block in heads for part in (block[:width], block[width : 2 * width])], axis=1
    )
    query_weight = jnp.concatenate([block[2 * width : 2 * width + dec] for block in heads], axis=1)
    out_weight = jnp.concatenate([block[2 * width + dec :] for block in heads], axis=1)

    text_normed = layer_norm(text_in, query_gain)[0].astype(BF)
    both = jnp.stack([text_normed, cotangent], axis=1)
    per = 2 * text_in.shape[1] * dec
    rows = text_in.shape[1]
    group_rows = []
    for other in range(4):
        block = lax.dynamic_index_in_dim(both, group ^ other, axis=0, keepdims=False)
        if other:
            pairs = [(i, i ^ other) for i in range(4)]
            block = lax.ppermute(block, ("yh", "core"), pairs)
        group_rows.append(block)
    caption = jnp.concatenate(group_rows, axis=1).reshape(2, 4 * rows, dec)
    caption = gather_rows(caption.reshape(1, 2, 4 * rows, dec), "tensor")
    text_mine = caption[:, 0].reshape(-1, dec)
    cot_mine = caption[:, 1].reshape(-1, dec)

    scaled, _, _ = layer_norm(flat_in, enc_gain)
    normed = scaled.astype(BF)
    pre_act = jnp.dot(normed, up, preferred_element_type=F32)
    activated = gelu_tanh(pre_act).astype(BF)
    branch_part = lax.dot_general(
        activated, down, (((1,), (1,)), ((), ())), preferred_element_type=F32
    ).astype(BF)
    own_rows = patches // lax.axis_size("tensor")
    in_rows = rows_at(flat_in, tensor * own_rows, own_rows)
    encoded_rows = (in_rows.astype(F32) + scatter_sum(branch_part, "tensor")).astype(BF)
    encoded = gather_rows(encoded_rows, "tensor")

    query = (
        jnp.dot(text_mine, query_weight, preferred_element_type=F32) * HEAD_DIM ** (-0.5)
    ).astype(BF)
    d_attn = jnp.dot(cot_mine, out_weight, preferred_element_type=F32).astype(BF)
    query = query.reshape(-1, 4, HEAD_DIM)
    d_attn = d_attn.reshape(-1, 4, HEAD_DIM)
    key_value = jnp.dot(encoded, pair_weight, preferred_element_type=F32).astype(BF)
    key_value = key_value.reshape(patches, 4, 2, HEAD_DIM)
    keys, values = key_value[:, :, 0], key_value[:, :, 1]
    scores = jnp.einsum("the,phe->htp", query, keys, preferred_element_type=F32)
    top = jnp.max(scores, axis=-1, keepdims=True)
    expo = jnp.exp(scores - top)
    probs = expo / jnp.sum(expo, axis=-1, keepdims=True)
    d_probs = jnp.einsum("the,phe->htp", d_attn, values, preferred_element_type=F32)
    d_scores = (probs * (d_probs - jnp.sum(probs * d_probs, axis=-1, keepdims=True))).astype(BF)
    probs_low = probs.astype(BF)
    d_keys = jnp.einsum("htp,the->phe", d_scores, query, preferred_element_type=F32).astype(BF)
    d_values = jnp.einsum("htp,the->phe", probs_low, d_attn, preferred_element_type=F32).astype(BF)
    d_pair = jnp.stack([d_keys, d_values], axis=2).reshape(patches, 8 * HEAD_DIM)

    term = lax.dot_general(
        d_pair, pair_weight, (((1,), (1,)), ((), ())), preferred_element_type=F32
    ).astype(BF)
    grad_rows = scatter_sum(term, "tensor").astype(BF)
    flat_grad = gather_rows(grad_rows, "tensor")

    pair_cols = 2 * HEAD_DIM
    keep = lax.dot_general(
        encoded, d_pair[:, : 2 * pair_cols], (((0,), (0,)), ((), ())), preferred_element_type=F32
    )
    give = lax.dot_general(
        encoded, d_pair[:, 2 * pair_cols :], (((0,), (0,)), ((), ())), preferred_element_type=F32
    ).astype(BF)
    sums = (keep + swap(give, "core").astype(F32)).astype(BF)
    sums = scatter_sum(sums, "x")
    sums = sums[:, :pair_cols] + swap(sums[:, pair_cols:].astype(BF), "yh").astype(F32)
    sums = sums.reshape(8, -1, pair_cols)
    for bit in (4, 2, 1):
        sums = halved(sums, "z", bit)
    sums = sums[0]
    key_grad, value_grad = sums[:, :HEAD_DIM], sums[:, HEAD_DIM:]

    d_act = jnp.dot(flat_grad, down, preferred_element_type=F32)
    d_pre = jax.vjp(gelu_tanh, pre_act)[1](d_act)[0].astype(BF)
    d_norm_part = lax.dot_general(
        d_pre, up, (((1,), (1,)), ((), ())), preferred_element_type=F32
    ).astype(BF)
    d_normed = scatter_sum(d_norm_part, "tensor")
    _, normal, inverse = layer_norm(in_rows, enc_gain)
    scaled_grad = d_normed * enc_gain
    d_input = inverse * (
        scaled_grad
        - jnp.mean(scaled_grad, axis=-1, keepdims=True)
        - normal * jnp.mean(scaled_grad * normal, axis=-1, keepdims=True)
    )
    image_rows = (grad_rows.astype(F32) + d_input).astype(BF)
    image_grad = gather_rows(image_rows, "tensor").reshape(1, patches, width)
    return (image_grad, key_grad, value_grad)


def solution(mesh):
    fine = Mesh(mesh.devices.reshape(4, 8, 4, 2, 2), ("x", "z", "tensor", "yh", "core"))
    dp, group, heads = ("x", "z"), ("yh", "core"), ("tensor", "yh", "core")
    in_specs = (
        P(dp + group, None, None),
        P(),
        P(group, "tensor"),
        P("tensor", group),
        P(dp, heads, None),
        P(),
        P(None, heads),
        P(None, heads),
        P(None, heads),
        P(heads, None),
        P(dp, heads, None),
    )
    out_specs = (P(dp + group, None, None), P(dp, heads), P(dp, heads))
    return jax.shard_map(local, mesh=fine, in_specs=in_specs, out_specs=out_specs, check_vma=False)
```

time: 594 us -> 409 us (0.69)
  waiting for transfers between devices: 425 us -> 124 us
  starting transfers between devices: 4.2 us -> 166 us
  blocking collectives: 101 us -> 0 us
  local copies, waits for them, and re-layouts: 8.03 us -> 75.6 us
  between operations: 16.4 us -> 2.19 us
    all_gather x5 -> x0, waiting for transfers between devices: 248 us -> none  [the longest x1 83.8 us: local(): lax.all_gather(cotangent, ('tensor', 'group'), axis=1, tiled=True)]
    ppermute x0 -> x50, starting transfers between devices: none -> 166 us  [the longest x33 109 us: shift(): lax.ppermute(value, axis, [(i, (i + by) % size) for i in range(size)])]
    ppermute x0 -> x50, waiting for transfers between devices: none -> 124 us  [the longest x33 109 us: shift(): lax.ppermute(value, axis, [(i, (i + by) % size) for i in range(size)])]
    reduce_scatter x1 -> x0, waiting for transfers between devices: 96.2 us -> none  [local(): lax.psum_scatter(term.astype(jnp.bfloat16), ('tensor', 'group'), scatter_...]
    unnamed x1 -> x0, blocking collectives: 79.6 us -> none
    psum x2 -> x0, waiting for transfers between devices: 78.1 us -> none  [the longest x1 78.1 us: local(): lax.psum(branch_part.astype(jnp.bfloat16), 'tensor').astype(jnp.float32)]
    dynamic_update_slice x0 -> x31, local copies, waits for them, and re-layouts: none -> 45.8 us  [put(): return lax.dynamic_update_slice_in_dim(buffer, block, start, axis=0)]
    all_gather x1 -> x0, blocking collectives: 21.1 us -> none  [local(): d_encoded = lax.all_gather(own_block, 'tensor', axis=1, tiled=True)]
  transfers between devices with their start and end apart: 11 -> 50, of which waited for: 7 -> 20; matrix products, arithmetic and copies ran while one was open for 17% -> 21% of each run, Pallas kernels for 0% -> 0%
where the time goes in v1:
time: 409 us; the launch traced here: 402 us
  starting transfers between devices  166 us (41%)
  waiting for transfers between devices  124 us (30%)
  local copies, waits for them, and re-layouts  75.6 us (18%)
  matrix products  22.9 us (6%)
  other arithmetic  11.5 us (3%)
    ppermute x33, starting transfers between devices, shift(): lax.ppermute(value, axis, [(i, (i + by) % size) for i in range(size)])  109 us
    ppermute x33, waiting for transfers between devices, shift(): lax.ppermute(value, axis, [(i, (i + by) % size) for i in range(size)])  109 us
    dynamic_update_slice x31, local copies, waits for them, and re-layouts, put(): return lax.dynamic_update_slice_in_dim(buffer, block, start, axis=0)  45.8 us
    ppermute x14, starting transfers between devices, swap(): return lax.ppermute(value, axis, [(i, i ^ bit) for i in range(size)])  44.9 us
    ppermute x14, waiting for transfers between devices, swap(): return lax.ppermute(value, axis, [(i, i ^ bit) for i in range(size)])  15.5 us
    unnamed x50, local copies, waits for them, and re-layouts  11.7 us
    ppermute x3, starting transfers between devices, local(): block = lax.ppermute(block, ('yh', 'core'), pairs)  11.5 us
  transfers between devices with their start and end apart: 50, of which 20 were waited for; matrix products, arithmetic and copies ran while one was open for 21% of the time, Pallas kernels for 0%

profile of v1, /device:TPU:56, one launch (start us, length us, event | category | flops | bytes accessed | tf_op | source)
XLA Modules:
  0.0 402.0 jit_solution(9167686232248720338)
XLA Ops:
  7.4 4.7 %collective-permute-start.1 = (bf16[2,8,2048]{2,1,0:T(8,128)(2,1)}, bf16[2,8,2048]{2,1,0:T(8,128)(2,1)S(1)}, u32[]{:S(2)}, u32[]{:S(2)}) collective-permute-start(bf16[2,8,2048]{2,1,0:T(8,128)(2,1)} %get-tuple-element.36), channel_id=1, source_target_pairs={{0,2},{1,3},{2,0},{3,1},{4,6},{5,7},{6,4},{7,5},{8,10},{9,11},{10,... | collective-permute-start | bytes 196616 | tf_op jit(solution)/shard_map/ppermute | solution.py:126
  12.1 4.9 %collective-permute-start.2 = (bf16[2,8,2048]{2,1,0:T(8,128)(2,1)S(1)}, bf16[2,8,2048]{2,1,0:T(8,128)(2,1)S(1)}, u32[]{:S(2)}, u32[]{:S(2)}) collective-permute-start(bf16[2,8,2048]{2,1,0:T(8,128)(2,1)S(1)} %get-tuple-element.37), channel_id=1, source_target_pairs={{0,3},{1,2},{2,1},{3,0},{4,7},{5,6},{6,5},{7,4},{8,11},{9,10},{10,... | collective-permute-start | bytes 196616 | tf_op jit(solution)/shard_map/ppermute | solution.py:126
  18.6 4.7 %collective-permute-start.19 = (bf16[88,1024]{1,0:T(8,128)(2,1)}, bf16[88,1024]{1,0:T(8,128)(2,1)}, u32[]{:S(2)}, u32[]{:S(2)}) collective-permute-start(bf16[88,1024]{1,0:T(8,128)(2,1)} %dynamic-slice_bitcast_fusion), channel_id=1, source_target_pairs={{0,2},{2,0},{1,3},{3,1},{4,6},{6,4},{5,7},{7,5},{8,10},{10,8},{9,1... | collective-permute-start | bytes 540680 | tf_op jit(solution)/shard_map/ppermute | solution.py:32
  31.5 2.1 constant_dynamic-update-slice_fusion.17
  37.8 5.0 %collective-permute-start.13 = (bf16[88,1024]{1,0:T(8,128)(2,1)S(1)}, bf16[88,1024]{1,0:T(8,128)(2,1)S(1)}, u32[]{:S(2)}, u32[]{:S(2)}) collective-permute-start(bf16[88,1024]{1,0:T(8,128)(2,1)S(1)} %constant_dynamic-slice_fusion.12), channel_id=1, source_target_pairs={{0,2},{2,0},{1,3},{3,1},{4,6},{6,4},{5,7},{7,5},{8,10},{10,8},{9,1... | collective-permute-start | bytes 540680 | tf_op jit(solution)/shard_map/ppermute | solution.py:32
  42.8 2.1 collective-permute-start.18
  44.9 4.8 %collective-permute-start.3 = (bf16[1,2,32,2048]{3,2,1,0:T(8,128)(2,1)S(1)}, bf16[1,2,32,2048]{3,2,1,0:T(8,128)(2,1)S(1)}, u32[]{:S(2)}, u32[]{:S(2)}) collective-permute-start(bf16[1,2,32,2048]{3,2,1,0:T(8,128)(2,1)S(1)} %maximum_bitcast_fusion), channel_id=1, source_target_pairs={{0,4},{4,8},{8,12},{12,0},{1,5},{5,9},{9,13},{13,1},{2,6},{6,10},{... | collective-permute-start | bytes 786440 | tf_op jit(solution)/shard_map/ppermute | solution.py:27
  49.9 7.5 %collective-permute-start.6 = (bf16[1728,128]{0,1:T(8,128)(2,1)S(1)}, bf16[1728,128]{0,1:T(8,128)(2,1)}, u32[]{:S(2)}, u32[]{:S(2)}) collective-permute-start(bf16[1728,128]{0,1:T(8,128)(2,1)S(1)} %constant_dynamic-slice_fusion.13), channel_id=1, source_target_pairs={{0,2},{2,0},{1,3},{3,1},{4,6},{6,4},{5,7},{7,5},{8,10},{10,8},{9,1... | collective-permute-start | bytes 1327112 | tf_op jit(solution)/shard_map/ppermute | solution.py:32
  62.0 2.5 collective-permute-start.5
  64.5 32.0 %collective-permute-done.4 = bf16[1,2,32,2048]{3,2,1,0:T(8,128)(2,1)S(1)} collective-permute-done((bf16[1,2,32,2048]{3,2,1,0:T(8,128)(2,1)S(1)}, bf16[1,2,32,2048]{3,2,1,0:T(8,128)(2,1)S(1)}, u32[]{:S(2)}, u32[]{:S(2)}) %collective-permute-start.4) | collective-permute-done | bytes 262176 | tf_op jit(solution)/shard_map/ppermute | solution.py:27
  96.5 6.2 %collective-permute-start.21 = (bf16[88,1024]{1,0:T(8,128)(2,1)}, bf16[88,1024]{1,0:T(8,128)(2,1)S(1)}, u32[]{:S(2)}, u32[]{:S(2)}) collective-permute-start(bf16[88,1024]{1,0:T(8,128)(2,1)} %collective-permute-done.19), channel_id=1, source_target_pairs={{0,32},{16,48},{32,64},{48,80},{64,96},{80,112},{96,0},{112,16},{1... | collective-permute-start | bytes 540680 | tf_op jit(solution)/shard_map/ppermute | solution.py:27
  102.7 6.8 %collective-permute-start.20 = (bf16[88,1024]{1,0:T(8,128)(2,1)}, bf16[88,1024]{1,0:T(8,128)(2,1)S(1)}, u32[]{:S(2)}, u32[]{:S(2)}) collective-permute-start(bf16[88,1024]{1,0:T(8,128)(2,1)} %collective-permute-done.19), channel_id=1, source_target_pairs={{0,112},{16,0},{32,16},{48,32},{64,48},{80,64},{96,80},{112,96},{1... | collective-permute-start | bytes 540680 | tf_op jit(solution)/shard_map/ppermute | solution.py:27
  110.5 3.2 collective-permute-done.20
  113.8 3.3 collective-permute-start.22
  117.2 4.7 %collective-permute-start.14 = (bf16[88,1024]{1,0:T(8,128)(2,1)S(1)}, bf16[88,1024]{1,0:T(8,128)(2,1)S(1)}, u32[]{:S(2)}, u32[]{:S(2)}) collective-permute-start(bf16[88,1024]{1,0:T(8,128)(2,1)S(1)} %collective-permute-done.13), channel_id=1, source_target_pairs={{0,384},{128,0},{256,128},{384,256},{1,385},{129,1},{257,129},{385... | collective-permute-start | bytes 540680 | tf_op jit(solution)/shard_map/ppermute | solution.py:27
  123.4 4.9 %collective-permute-start.15 = (bf16[88,1024]{1,0:T(8,128)(2,1)S(1)}, bf16[88,1024]{1,0:T(8,128)(2,1)S(1)}, u32[]{:S(2)}, u32[]{:S(2)}) collective-permute-start(bf16[88,1024]{1,0:T(8,128)(2,1)S(1)} %collective-permute-done.13), channel_id=1, source_target_pairs={{0,256},{128,384},{256,0},{384,128},{1,257},{129,385},{257,1},{385... | collective-permute-start | bytes 540680 | tf_op jit(solution)/shard_map/ppermute | solution.py:27
  128.4 2.5 collective-permute-start.16
  133.8 2.6 collective-permute-start.9
  136.4 5.3 %collective-permute-start.8 = (bf16[1728,128]{0,1:T(8,128)(2,1)}, bf16[1728,128]{0,1:T(8,128)(2,1)}, u32[]{:S(2)}, u32[]{:S(2)}) collective-permute-start(bf16[1728,128]{0,1:T(8,128)(2,1)} %collective-permute-done.6), channel_id=1, source_target_pairs={{0,256},{128,384},{256,0},{384,128},{1,257},{129,385},{257,1},{385... | collective-permute-start | bytes 1327112 | tf_op jit(solution)/shard_map/ppermute | solution.py:27
  141.6 4.5 %collective-permute-start.7 = (bf16[1728,128]{0,1:T(8,128)(2,1)}, bf16[1728,128]{0,1:T(8,128)(2,1)}, u32[]{:S(2)}, u32[]{:S(2)}) collective-permute-start(bf16[1728,128]{0,1:T(8,128)(2,1)} %collective-permute-done.6), channel_id=1, source_target_pairs={{0,384},{128,0},{256,128},{384,256},{1,385},{129,1},{257,129},{385... | collective-permute-start | bytes 1327112 | tf_op jit(solution)/shard_map/ppermute | solution.py:27
  147.0 6.1 %dynamic_update_slice.116 = bf16[6912,128]{0,1:T(8,128)(2,1)S(1)} dynamic-update-slice(bf16[6912,128]{0,1:T(8,128)(2,1)S(1)} %broadcast_in_dim.5, bf16[1728,128]{0,1:T(8,128)(2,1)} %collective-permute-done.6, s32[]{:T(128)S(6)} %select_n.181, s32[]{:T(128)} %constant.163.clone.1) | dynamic-update-slice | bytes 884740 | tf_op jit(solution)/shard_map/dynamic_update_slice | solution.py:40
  155.1 2.0 constant_dynamic-update-slice_fusion.16
  157.1 2.4 collective-permute-start.17
  159.5 2.1 constant_dynamic-update-slice_fusion.24
  161.6 2.3 constant_dynamic-update-slice_fusion.11
  165.9 6.9 %dynamic_update_slice.117 = bf16[6912,128]{0,1:T(8,128)(2,1)S(1)} dynamic-update-slice(bf16[6912,128]{0,1:T(8,128)(2,1)S(1)} %dynamic_update_slice.116, bf16[1728,128]{0,1:T(8,128)(2,1)} %collective-permute-done.7, s32[]{:T(128)S(6)} %select_n.182, s32[]{:T(128)} %constant.163.clone.1) | dynamic-update-slice | bytes 884740 | tf_op jit(solution)/shard_map/dynamic_update_slice | solution.py:40
  172.8 6.1 %dynamic_update_slice.118 = bf16[6912,128]{0,1:T(8,128)(2,1)S(1)} dynamic-update-slice(bf16[6912,128]{0,1:T(8,128)(2,1)S(1)} %dynamic_update_slice.117, bf16[1728,128]{0,1:T(8,128)(2,1)} %collective-permute-done.8, s32[]{:T(128)S(6)} %select_n.183, s32[]{:T(128)} %constant.163.clone.1) | dynamic-update-slice | bytes 884740 | tf_op jit(solution)/shard_map/dynamic_update_slice | solution.py:40
  179.0 6.6 %dynamic_update_slice.119 = bf16[6912,128]{0,1:T(8,128)(2,1)S(1)} dynamic-update-slice(bf16[6912,128]{0,1:T(8,128)(2,1)S(1)} %dynamic_update_slice.118, bf16[1728,128]{0,1:T(8,128)(2,1)} %collective-permute-done.9, s32[]{:T(128)S(6)} %select_n.184, s32[]{:T(128)} %constant.163.clone.1) | dynamic-update-slice | bytes 884740 | tf_op jit(solution)/shard_map/dynamic_update_slice | solution.py:40
  186.4 2.4 collective-permute-start.11
  190.9 2.8 fusion.44
  193.7 2.4 constant_dynamic-update-slice_fusion.10
  196.2 2.9 convolution_convert_fusion.3
  201.1 3.9 collective-permute-start.26
  207.7 2.9 collective-permute-done.24
  212.3 6.7 %collective-permute-done.25 = bf16[64,1408]{1,0:T(8,128)(2,1)S(1)} collective-permute-done((bf16[64,1408]{1,0:T(8,128)(2,1)S(1)}, bf16[64,1408]{1,0:T(8,128)(2,1)S(1)}, u32[]{:S(2)}, u32[]{:S(2)}) %collective-permute-start.25) | collective-permute-done | bytes 180256 | tf_op jit(solution)/shard_map/ppermute | solution.py:27
  219.2 4.1 %collective-permute-start.27 = (bf16[64,1408]{1,0:T(8,128)(2,1)S(1)}, bf16[64,1408]{1,0:T(8,128)(2,1)S(1)}, u32[]{:S(2)}, u32[]{:S(2)}) collective-permute-start(bf16[64,1408]{1,0:T(8,128)(2,1)S(1)} %get-tuple-element.11), channel_id=1, source_target_pairs={{0,4},{4,8},{8,12},{12,0},{1,5},{5,9},{9,13},{13,1},{2,6},{6,10},{... | collective-permute-start | bytes 540680 | tf_op jit(solution)/shard_map/ppermute | solution.py:27
  226.0 2.7 collective-permute-start.29
  228.7 11.4 %collective-permute-done.28 = bf16[64,1408]{1,0:T(8,128)(2,1)S(1)} collective-permute-done((bf16[64,1408]{1,0:T(8,128)(2,1)S(1)}, bf16[64,1408]{1,0:T(8,128)(2,1)S(1)}, u32[]{:S(2)}, u32[]{:S(2)}) %collective-permute-start.28) | collective-permute-done | bytes 180256 | tf_op jit(solution)/shard_map/ppermute | solution.py:27
  243.8 2.1 fusion.109
  249.3 2.0 fusion.34
  255.0 2.8 convolution_convert_fusion.4
  264.6 3.8 collective-permute-start.32
  268.4 4.1 %collective-permute-start.31 = (bf16[64,1408]{1,0:T(8,128)(2,1)S(1)}, bf16[64,1408]{1,0:T(8,128)(2,1)}, u32[]{:S(2)}, u32[]{:S(2)}) collective-permute-start(bf16[64,1408]{1,0:T(8,128)(2,1)S(1)} %get-tuple-element.28), channel_id=1, source_target_pairs={{0,8},{4,12},{8,0},{12,4},{1,9},{5,13},{9,1},{13,5},{2,10},{6,14},... | collective-permute-start | bytes 540680 | tf_op jit(solution)/shard_map/ppermute | solution.py:27
  272.9 4.7 %collective-permute-done.32 = bf16[64,1408]{1,0:T(8,128)(2,1)} collective-permute-done((bf16[64,1408]{1,0:T(8,128)(2,1)S(1)}, bf16[64,1408]{1,0:T(8,128)(2,1)}, u32[]{:S(2)}, u32[]{:S(2)}) %collective-permute-start.32) | collective-permute-done | bytes 180256 | tf_op jit(solution)/shard_map/ppermute | solution.py:27
  277.6 6.6 %collective-permute-done.31 = bf16[64,1408]{1,0:T(8,128)(2,1)} collective-permute-done((bf16[64,1408]{1,0:T(8,128)(2,1)S(1)}, bf16[64,1408]{1,0:T(8,128)(2,1)}, u32[]{:S(2)}, u32[]{:S(2)}) %collective-permute-start.31) | collective-permute-done | bytes 180256 | tf_op jit(solution)/shard_map/ppermute | solution.py:27
  286.8 2.5 collective-permute-start.33
  293.8 3.4 collective-permute-start.35
  297.8 11.5 %collective-permute-done.34 = bf16[64,1408]{1,0:T(8,128)(2,1)S(1)} collective-permute-done((bf16[64,1408]{1,0:T(8,128)(2,1)S(1)}, bf16[64,1408]{1,0:T(8,128)(2,1)S(1)}, u32[]{:S(2)}, u32[]{:S(2)}) %collective-permute-start.34) | collective-permute-done | bytes 180256 | tf_op jit(solution)/shard_map/ppermute | solution.py:27
  310.7 6.3 %convolution_convert_fusion.1 = bf16[256,1408]{1,0:T(8,128)(2,1)} fusion(bf16[1408,1024]{1,0:T(8,128)(2,1)} %constant_dynamic-update-slice_fusion.18, f32[256,1024]{1,0:T(8,128)} %copy-done.19, bf16[256,1408]{1,0:T(8,128)(2,1)} %constant_dynamic-update-slice_fusion.2, bf16[1408,1024]{1,0:T(8,128)(2,1)} %constant_dynamic-update-slice_fusion.10), kind=kOutput, calls=%fused_computation.4 | convolution fusion | flops 1481998336 | bytes 8257536 | tf_op jit(solution)/shard_map/dot_general | solution.py:189
  320.1 3.9 collective-permute-start.38
  326.0 2.9 collective-permute-done.36
  328.9 2.5 collective-permute-done.38
  331.4 6.3 %collective-permute-done.37 = bf16[64,1408]{1,0:T(8,128)(2,1)S(1)} collective-permute-done((bf16[64,1408]{1,0:T(8,128)(2,1)S(1)}, bf16[64,1408]{1,0:T(8,128)(2,1)S(1)}, u32[]{:S(2)}, u32[]{:S(2)}) %collective-permute-start.37) | collective-permute-done | bytes 180256 | tf_op jit(solution)/shard_map/ppermute | solution.py:27
  342.9 5.1 %collective-permute-start.45 = (bf16[352,512]{1,0:T(8,128)(2,1)S(1)}, bf16[352,512]{1,0:T(8,128)(2,1)S(1)}, u32[]{:S(2)}, u32[]{:S(2)}) collective-permute-start(bf16[352,512]{1,0:T(8,128)(2,1)S(1)} %get-tuple-element.19), channel_id=1, source_target_pairs={{0,384},{128,0},{256,128},{384,256},{1,385},{129,1},{257,129},{385... | collective-permute-start | bytes 1081352 | tf_op jit(solution)/shard_map/ppermute | solution.py:27
  350.0 12.1 %collective-permute-done.43 = bf16[352,512]{1,0:T(8,128)(2,1)S(1)} collective-permute-done((bf16[352,512]{1,0:T(8,128)(2,1)S(1)}, bf16[352,512]{1,0:T(8,128)(2,1)S(1)}, u32[]{:S(2)}, u32[]{:S(2)}) %collective-permute-start.43) | collective-permute-done | bytes 360480 | tf_op jit(solution)/shard_map/ppermute | solution.py:27
  363.6 2.5 collective-permute-start.46
  368.3 4.1 %collective-permute-start.39 = (bf16[64,1408]{1,0:T(8,128)(2,1)S(1)}, bf16[64,1408]{1,0:T(8,128)(2,1)S(1)}, u32[]{:S(2)}, u32[]{:S(2)}) collective-permute-start(bf16[64,1408]{1,0:T(8,128)(2,1)S(1)} %get-tuple-element.6), channel_id=1, source_target_pairs={{0,4},{4,8},{8,12},{12,0},{1,5},{5,9},{9,13},{13,1},{2,6},{6,10},{... | collective-permute-start | bytes 540680 | tf_op jit(solution)/shard_map/ppermute | solution.py:27
  372.4 2.5 collective-permute-start.41
  374.9 2.2 collective-permute-done.46
  377.2 4.8 %collective-permute-start.47 = (bf16[4,44,256]{2,1,0:T(8,128)(2,1)S(1)}, bf16[4,44,256]{2,1,0:T(8,128)(2,1)S(1)}, u32[]{:S(2)}, u32[]{:S(2)}) collective-permute-start(bf16[4,44,256]{2,1,0:T(8,128)(2,1)S(1)} %dynamic-slice_convert_fusion), channel_id=1, source_target_pairs={{0,64},{16,80},{32,96},{48,112},{64,0},{80,16},{96,32},{112,48},{1... | collective-permute-start | bytes 270344 | tf_op jit(solution)/shard_map/ppermute | solution.py:32
  382.0 6.7 %collective-permute-done.47 = bf16[4,44,256]{2,1,0:T(8,128)(2,1)S(1)} collective-permute-done((bf16[4,44,256]{2,1,0:T(8,128)(2,1)S(1)}, bf16[4,44,256]{2,1,0:T(8,128)(2,1)S(1)}, u32[]{:S(2)}, u32[]{:S(2)}) %collective-permute-start.47) | collective-permute-done | bytes 90144 | tf_op jit(solution)/shard_map/ppermute | solution.py:32
  388.8 4.0 collective-permute-start.48
  392.8 2.8 collective-permute-done.48
  397.7 3.7 collective-permute-done.49
  (191 shorter events, 92.9 us)
Async XLA Ops:
  0.6 27.1 %copy-start = (bf16[1,256,1408]{2,1,0:T(8,128)(2,1)S(1)}, bf16[1,256,1408]{2,1,0:T(8,128)(2,1)}, u32[]{:S(2)}) copy-start(bf16[1,256,1408]{2,1,0:T(8,128)(2,1)} %param.11) | copy-start | bytes 2162692
  0.6 27.5 %copy-start.15 = (bf16[1408,128]{1,0:T(8,128)(2,1)S(1)}, bf16[1408,128]{1,0:T(8,128)(2,1)}, u32[]{:S(2)}) copy-start(bf16[1408,128]{1,0:T(8,128)(2,1)} %param.18) | copy-start | bytes 1081348
  0.7 27.7 %copy-start.16 = (bf16[1408,128]{1,0:T(8,128)(2,1)S(1)}, bf16[1408,128]{1,0:T(8,128)(2,1)}, u32[]{:S(2)}) copy-start(bf16[1408,128]{1,0:T(8,128)(2,1)} %param.19) | copy-start | bytes 1081348
  0.7 27.9 %copy-start.11 = (bf16[2048,128]{1,0:T(8,128)(2,1)S(1)}, bf16[2048,128]{1,0:T(8,128)(2,1)}, u32[]{:S(2)}) copy-start(bf16[2048,128]{1,0:T(8,128)(2,1)} %param.17) | copy-start | bytes 1572868
  5.5 32.3 %collective-permute-start = (bf16[2,8,2048]{2,1,0:T(8,128)(2,1)}, bf16[2,8,2048]{2,1,0:T(8,128)(2,1)S(1)}, u32[]{:S(2)}, u32[]{:S(2)}) collective-permute-start(bf16[2,8,2048]{2,1,0:T(8,128)(2,1)} %get-tuple-element.35), channel_id=1, source_target_pairs={{0,1},{1,0},{2,3},{3,2},{4,5},{5,4},{6,7},{7,6},{8,9},{9,8},{10,11... | collective-permute-start | bytes 196616 | tf_op jit(solution)/shard_map/ppermute | solution.py:126
  7.4 35.4 %collective-permute-start.1 = (bf16[2,8,2048]{2,1,0:T(8,128)(2,1)}, bf16[2,8,2048]{2,1,0:T(8,128)(2,1)S(1)}, u32[]{:S(2)}, u32[]{:S(2)}) collective-permute-start(bf16[2,8,2048]{2,1,0:T(8,128)(2,1)} %get-tuple-element.36), channel_id=1, source_target_pairs={{0,2},{1,3},{2,0},{3,1},{4,6},{5,7},{6,4},{7,5},{8,10},{9,11},{10,... | collective-permute-start | bytes 196616 | tf_op jit(solution)/shard_map/ppermute | solution.py:126
  12.1 32.8 %collective-permute-start.2 = (bf16[2,8,2048]{2,1,0:T(8,128)(2,1)S(1)}, bf16[2,8,2048]{2,1,0:T(8,128)(2,1)S(1)}, u32[]{:S(2)}, u32[]{:S(2)}) collective-permute-start(bf16[2,8,2048]{2,1,0:T(8,128)(2,1)S(1)} %get-tuple-element.37), channel_id=1, source_target_pairs={{0,3},{1,2},{2,1},{3,0},{4,7},{5,6},{6,5},{7,4},{8,11},{9,10},{10,... | collective-permute-start | bytes 196616 | tf_op jit(solution)/shard_map/ppermute | solution.py:126
  18.6 31.3 %collective-permute-start.19 = (bf16[88,1024]{1,0:T(8,128)(2,1)}, bf16[88,1024]{1,0:T(8,128)(2,1)}, u32[]{:S(2)}, u32[]{:S(2)}) collective-permute-start(bf16[88,1024]{1,0:T(8,128)(2,1)} %dynamic-slice_bitcast_fusion), channel_id=1, source_target_pairs={{0,2},{2,0},{1,3},{3,1},{4,6},{6,4},{5,7},{7,5},{8,10},{10,8},{9,1... | collective-permute-start | bytes 540680 | tf_op jit(solution)/shard_map/ppermute | solution.py:32
  23.3 133.8 %collective-permute-start.12 = (bf16[352,1024]{1,0:T(8,128)(2,1)}, bf16[352,1024]{1,0:T(8,128)(2,1)}, u32[]{:S(2)}, u32[]{:S(2)}) collective-permute-start(bf16[352,1024]{1,0:T(8,128)(2,1)} %param.13), channel_id=1, source_target_pairs={{0,1},{1,0},{2,3},{3,2},{4,5},{5,4},{6,7},{7,6},{8,9},{9,8},{10,11... | collective-permute-start | bytes 2162696 | tf_op jit(solution)/shard_map/ppermute | solution.py:32
  28.8 8.6 %copy-start.2 = (bf16[2048,128]{0,1:T(8,128)(2,1)}, bf16[2048,128]{0,1:T(8,128)(2,1)S(1)}, u32[]{:S(2)}) copy-start(bf16[2048,128]{0,1:T(8,128)(2,1)S(1)} %copy.29) | copy-start | bytes 1572868
  31.5 4.1 %copy-start.5 = (bf16[352,1024]{1,0:T(8,128)(2,1)S(1)}, bf16[352,1024]{1,0:T(8,128)(2,1)}, u32[]{:S(2)}) copy-start(bf16[352,1024]{1,0:T(8,128)(2,1)} %param.13) | copy-start | bytes 2162692
  37.5 27.0 %copy-start.1 = (bf16[6912,128]{0,1:T(8,128)(2,1)}, bf16[6912,128]{0,1:T(8,128)(2,1)S(1)}, u32[]{:S(2)}) copy-start(bf16[6912,128]{0,1:T(8,128)(2,1)S(1)} %pad_maximum_fusion) | copy-start | bytes 5308420
  37.8 20.7 %collective-permute-start.13 = (bf16[88,1024]{1,0:T(8,128)(2,1)S(1)}, bf16[88,1024]{1,0:T(8,128)(2,1)S(1)}, u32[]{:S(2)}, u32[]{:S(2)}) collective-permute-start(bf16[88,1024]{1,0:T(8,128)(2,1)S(1)} %constant_dynamic-slice_fusion.12), channel_id=1, source_target_pairs={{0,2},{2,0},{1,3},{3,1},{4,6},{6,4},{5,7},{7,5},{8,10},{10,8},{9,1... | collective-permute-start | bytes 540680 | tf_op jit(solution)/shard_map/ppermute | solution.py:32
  42.8 110.4 %collective-permute-start.18 = (bf16[352,1024]{1,0:T(8,128)(2,1)}, bf16[352,1024]{1,0:T(8,128)(2,1)}, u32[]{:S(2)}, u32[]{:S(2)}) collective-permute-start(bf16[352,1024]{1,0:T(8,128)(2,1)} %bitcast.11), channel_id=1, source_target_pairs={{0,1},{1,0},{2,3},{3,2},{4,5},{5,4},{6,7},{7,6},{8,9},{9,8},{10,11... | collective-permute-start | bytes 2162696 | tf_op jit(solution)/shard_map/ppermute | solution.py:32
  44.9 17.1 %collective-permute-start.3 = (bf16[1,2,32,2048]{3,2,1,0:T(8,128)(2,1)S(1)}, bf16[1,2,32,2048]{3,2,1,0:T(8,128)(2,1)S(1)}, u32[]{:S(2)}, u32[]{:S(2)}) collective-permute-start(bf16[1,2,32,2048]{3,2,1,0:T(8,128)(2,1)S(1)} %maximum_bitcast_fusion), channel_id=1, source_target_pairs={{0,4},{4,8},{8,12},{12,0},{1,5},{5,9},{9,13},{13,1},{2,6},{6,10},{... | collective-permute-start | bytes 786440 | tf_op jit(solution)/shard_map/ppermute | solution.py:27
  49.9 83.9 %collective-permute-start.6 = (bf16[1728,128]{0,1:T(8,128)(2,1)S(1)}, bf16[1728,128]{0,1:T(8,128)(2,1)}, u32[]{:S(2)}, u32[]{:S(2)}) collective-permute-start(bf16[1728,128]{0,1:T(8,128)(2,1)S(1)} %constant_dynamic-slice_fusion.13), channel_id=1, source_target_pairs={{0,2},{2,0},{1,3},{3,1},{4,6},{6,4},{5,7},{7,5},{8,10},{10,8},{9,1... | collective-permute-start | bytes 1327112 | tf_op jit(solution)/shard_map/ppermute | solution.py:32
  58.5 38.0 %collective-permute-start.4 = (bf16[1,2,32,2048]{3,2,1,0:T(8,128)(2,1)S(1)}, bf16[1,2,32,2048]{3,2,1,0:T(8,128)(2,1)S(1)}, u32[]{:S(2)}, u32[]{:S(2)}) collective-permute-start(bf16[1,2,32,2048]{3,2,1,0:T(8,128)(2,1)S(1)} %maximum_bitcast_fusion), channel_id=1, source_target_pairs={{0,8},{4,12},{8,0},{12,4},{1,9},{5,13},{9,1},{13,5},{2,10},{6,14},... | collective-permute-start | bytes 786440 | tf_op jit(solution)/shard_map/ppermute | solution.py:27
  62.0 40.7 %collective-permute-start.5 = (bf16[1,2,32,2048]{3,2,1,0:T(8,128)(2,1)S(1)}, bf16[1,2,32,2048]{3,2,1,0:T(8,128)(2,1)S(1)}, u32[]{:S(2)}, u32[]{:S(2)}) collective-permute-start(bf16[1,2,32,2048]{3,2,1,0:T(8,128)(2,1)S(1)} %maximum_bitcast_fusion), channel_id=1, source_target_pairs={{0,12},{4,0},{8,4},{12,8},{1,13},{5,1},{9,5},{13,9},{2,14},{6,2},{... | collective-permute-start | bytes 786440 | tf_op jit(solution)/shard_map/ppermute | solution.py:27
  96.5 20.7 %collective-permute-start.21 = (bf16[88,1024]{1,0:T(8,128)(2,1)}, bf16[88,1024]{1,0:T(8,128)(2,1)S(1)}, u32[]{:S(2)}, u32[]{:S(2)}) collective-permute-start(bf16[88,1024]{1,0:T(8,128)(2,1)} %collective-permute-done.19), channel_id=1, source_target_pairs={{0,32},{16,48},{32,64},{48,80},{64,96},{80,112},{96,0},{112,16},{1... | collective-permute-start | bytes 540680 | tf_op jit(solution)/shard_map/ppermute | solution.py:27
  102.7 11.1 %collective-permute-start.20 = (bf16[88,1024]{1,0:T(8,128)(2,1)}, bf16[88,1024]{1,0:T(8,128)(2,1)S(1)}, u32[]{:S(2)}, u32[]{:S(2)}) collective-permute-start(bf16[88,1024]{1,0:T(8,128)(2,1)} %collective-permute-done.19), channel_id=1, source_target_pairs={{0,112},{16,0},{32,16},{48,32},{64,48},{80,64},{96,80},{112,96},{1... | collective-permute-start | bytes 540680 | tf_op jit(solution)/shard_map/ppermute | solution.py:27
  113.8 9.6 %collective-permute-start.22 = (bf16[88,1024]{1,0:T(8,128)(2,1)}, bf16[88,1024]{1,0:T(8,128)(2,1)S(1)}, u32[]{:S(2)}, u32[]{:S(2)}) collective-permute-start(bf16[88,1024]{1,0:T(8,128)(2,1)} %collective-permute-done.19), channel_id=1, source_target_pairs={{0,16},{16,32},{32,48},{48,64},{64,80},{80,96},{96,112},{112,0},{1... | collective-permute-start | bytes 540680 | tf_op jit(solution)/shard_map/ppermute | solution.py:27
  117.2 11.2 %collective-permute-start.14 = (bf16[88,1024]{1,0:T(8,128)(2,1)S(1)}, bf16[88,1024]{1,0:T(8,128)(2,1)S(1)}, u32[]{:S(2)}, u32[]{:S(2)}) collective-permute-start(bf16[88,1024]{1,0:T(8,128)(2,1)S(1)} %collective-permute-done.13), channel_id=1, source_target_pairs={{0,384},{128,0},{256,128},{384,256},{1,385},{129,1},{257,129},{385... | collective-permute-start | bytes 540680 | tf_op jit(solution)/shard_map/ppermute | solution.py:27
  123.4 9.7 %collective-permute-start.15 = (bf16[88,1024]{1,0:T(8,128)(2,1)S(1)}, bf16[88,1024]{1,0:T(8,128)(2,1)S(1)}, u32[]{:S(2)}, u32[]{:S(2)}) collective-permute-start(bf16[88,1024]{1,0:T(8,128)(2,1)S(1)} %collective-permute-done.13), channel_id=1, source_target_pairs={{0,256},{128,384},{256,0},{384,128},{1,257},{129,385},{257,1},{385... | collective-permute-start | bytes 540680 | tf_op jit(solution)/shard_map/ppermute | solution.py:27
  128.4 13.3 %collective-permute-start.16 = (bf16[88,1024]{1,0:T(8,128)(2,1)S(1)}, bf16[88,1024]{1,0:T(8,128)(2,1)S(1)}, u32[]{:S(2)}, u32[]{:S(2)}) collective-permute-start(bf16[88,1024]{1,0:T(8,128)(2,1)S(1)} %collective-permute-done.13), channel_id=1, source_target_pairs={{0,128},{128,256},{256,384},{384,0},{1,129},{129,257},{257,385},{3... | collective-permute-start | bytes 540680 | tf_op jit(solution)/shard_map/ppermute | solution.py:27
  133.8 45.2 %collective-permute-start.9 = (bf16[1728,128]{0,1:T(8,128)(2,1)}, bf16[1728,128]{0,1:T(8,128)(2,1)}, u32[]{:S(2)}, u32[]{:S(2)}) collective-permute-start(bf16[1728,128]{0,1:T(8,128)(2,1)} %collective-permute-done.6), channel_id=1, source_target_pairs={{0,128},{128,256},{256,384},{384,0},{1,129},{129,257},{257,385},{3... | collective-permute-start | bytes 1327112 | tf_op jit(solution)/shard_map/ppermute | solution.py:27
  136.4 36.4 %collective-permute-start.8 = (bf16[1728,128]{0,1:T(8,128)(2,1)}, bf16[1728,128]{0,1:T(8,128)(2,1)}, u32[]{:S(2)}, u32[]{:S(2)}) collective-permute-start(bf16[1728,128]{0,1:T(8,128)(2,1)} %collective-permute-done.6), channel_id=1, source_target_pairs={{0,256},{128,384},{256,0},{384,128},{1,257},{129,385},{257,1},{385... | collective-permute-start | bytes 1327112 | tf_op jit(solution)/shard_map/ppermute | solution.py:27
  141.6 22.3 %collective-permute-start.7 = (bf16[1728,128]{0,1:T(8,128)(2,1)}, bf16[1728,128]{0,1:T(8,128)(2,1)}, u32[]{:S(2)}, u32[]{:S(2)}) collective-permute-start(bf16[1728,128]{0,1:T(8,128)(2,1)} %collective-permute-done.6), channel_id=1, source_target_pairs={{0,384},{128,0},{256,128},{384,256},{1,385},{129,1},{257,129},{385... | collective-permute-start | bytes 1327112 | tf_op jit(solution)/shard_map/ppermute | solution.py:27
  153.1 87.1 %collective-permute-start.10 = (bf16[6912,128]{0,1:T(8,128)(2,1)}, bf16[6912,128]{0,1:T(8,128)(2,1)}, u32[]{:S(2)}, u32[]{:S(2)}) collective-permute-start(bf16[6912,128]{0,1:T(8,128)(2,1)} %copy-done.1), channel_id=1, source_target_pairs={{0,1},{1,0},{2,3},{3,2},{4,5},{5,4},{6,7},{7,6},{8,9},{9,8},{10,11... | collective-permute-start | bytes 5308424 | tf_op jit(solution)/shard_map/ppermute | solution.py:32
  157.1 31.7 %collective-permute-start.17 = (bf16[352,1024]{1,0:T(8,128)(2,1)}, bf16[352,1024]{1,0:T(8,128)(2,1)}, u32[]{:S(2)}, u32[]{:S(2)}) collective-permute-start(bf16[352,1024]{1,0:T(8,128)(2,1)} %constant_dynamic-update-slice_fusion.20), channel_id=1, source_target_pairs={{0,1},{1,0},{2,3},{3,2},{4,5},{5,4},{6,7},{7,6},{8,9},{9,8},{10,11... | collective-permute-start | bytes 2162696 | tf_op jit(solution)/shard_map/ppermute | solution.py:32
  164.0 29.8 %collective-permute-start.23 = (bf16[352,1024]{1,0:T(8,128)(2,1)S(1)}, bf16[352,1024]{1,0:T(8,128)(2,1)}, u32[]{:S(2)}, u32[]{:S(2)}) collective-permute-start(bf16[352,1024]{1,0:T(8,128)(2,1)S(1)} %constant_dynamic-update-slice_fusion.12), channel_id=1, source_target_pairs={{0,1},{1,0},{2,3},{3,2},{4,5},{5,4},{6,7},{7,6},{8,9},{9,8},{10,11... | collective-permute-start | bytes 2162696 | tf_op jit(solution)/shard_map/ppermute | solution.py:32
  172.8 18.1 %copy-start.18 = (f32[1408]{0:T(1024)S(1)}, f32[1408]{0:T(1024)}, u32[]{:S(2)}) copy-start(f32[1408]{0:T(1024)} %param.12) | copy-start | bytes 16900
  186.4 59.4 %collective-permute-start.11 = (bf16[6912,128]{0,1:T(8,128)(2,1)S(1)}, bf16[6912,128]{0,1:T(8,128)(2,1)S(1)}, u32[]{:S(2)}, u32[]{:S(2)}) collective-permute-start(bf16[6912,128]{0,1:T(8,128)(2,1)S(1)} %dynamic_update_slice.119), channel_id=1, source_target_pairs={{0,1},{1,0},{2,3},{3,2},{4,5},{5,4},{6,7},{7,6},{8,9},{9,8},{10,11... | collective-permute-start | bytes 5308424 | tf_op jit(solution)/shard_map/ppermute | solution.py:32
  193.7 5.4 %copy-start.19 = (f32[256,1024]{1,0:T(8,128)}, f32[256,1024]{1,0:T(8,128)S(1)}, u32[]{:S(2)}) copy-start(f32[256,1024]{1,0:T(8,128)S(1)} %fusion.44) | copy-start | bytes 3145732
  199.2 11.4 %collective-permute-start.24 = (bf16[64,1408]{1,0:T(8,128)(2,1)S(1)}, bf16[64,1408]{1,0:T(8,128)(2,1)S(1)}, u32[]{:S(2)}, u32[]{:S(2)}) collective-permute-start(bf16[64,1408]{1,0:T(8,128)(2,1)S(1)} %get-tuple-element.29), channel_id=1, source_target_pairs={{0,4},{4,8},{8,12},{12,0},{1,5},{5,9},{9,13},{13,1},{2,6},{6,10},{... | collective-permute-start | bytes 540680 | tf_op jit(solution)/shard_map/ppermute | solution.py:27
  201.1 11.2 %collective-permute-start.26 = (bf16[64,1408]{1,0:T(8,128)(2,1)S(1)}, bf16[64,1408]{1,0:T(8,128)(2,1)S(1)}, u32[]{:S(2)}, u32[]{:S(2)}) collective-permute-start(bf16[64,1408]{1,0:T(8,128)(2,1)S(1)} %get-tuple-element.30), channel_id=1, source_target_pairs={{0,12},{4,0},{8,4},{12,8},{1,13},{5,1},{9,5},{13,9},{2,14},{6,2},{... | collective-permute-start | bytes 540680 | tf_op jit(solution)/shard_map/ppermute | solution.py:27
  205.0 14.0 %collective-permute-start.25 = (bf16[64,1408]{1,0:T(8,128)(2,1)S(1)}, bf16[64,1408]{1,0:T(8,128)(2,1)S(1)}, u32[]{:S(2)}, u32[]{:S(2)}) collective-permute-start(bf16[64,1408]{1,0:T(8,128)(2,1)S(1)} %get-tuple-element.31), channel_id=1, source_target_pairs={{0,8},{4,12},{8,0},{12,4},{1,9},{5,13},{9,1},{13,5},{2,10},{6,14},... | collective-permute-start | bytes 540680 | tf_op jit(solution)/shard_map/ppermute | solution.py:27
  219.2 9.5 %collective-permute-start.27 = (bf16[64,1408]{1,0:T(8,128)(2,1)S(1)}, bf16[64,1408]{1,0:T(8,128)(2,1)S(1)}, u32[]{:S(2)}, u32[]{:S(2)}) collective-permute-start(bf16[64,1408]{1,0:T(8,128)(2,1)S(1)} %get-tuple-element.11), channel_id=1, source_target_pairs={{0,4},{4,8},{8,12},{12,0},{1,5},{5,9},{9,13},{13,1},{2,6},{6,10},{... | collective-permute-start | bytes 540680 | tf_op jit(solution)/shard_map/ppermute | solution.py:27
  224.1 16.0 %collective-permute-start.28 = (bf16[64,1408]{1,0:T(8,128)(2,1)S(1)}, bf16[64,1408]{1,0:T(8,128)(2,1)S(1)}, u32[]{:S(2)}, u32[]{:S(2)}) collective-permute-start(bf16[64,1408]{1,0:T(8,128)(2,1)S(1)} %get-tuple-element.11), channel_id=1, source_target_pairs={{0,8},{4,12},{8,0},{12,4},{1,9},{5,13},{9,1},{13,5},{2,10},{6,14},... | collective-permute-start | bytes 540680 | tf_op jit(solution)/shard_map/ppermute | solution.py:27
  226.0 14.1 %collective-permute-start.29 = (bf16[64,1408]{1,0:T(8,128)(2,1)S(1)}, bf16[64,1408]{1,0:T(8,128)(2,1)S(1)}, u32[]{:S(2)}, u32[]{:S(2)}) collective-permute-start(bf16[64,1408]{1,0:T(8,128)(2,1)S(1)} %get-tuple-element.11), channel_id=1, source_target_pairs={{0,12},{4,0},{8,4},{12,8},{1,13},{5,1},{9,5},{13,9},{2,14},{6,2},{... | collective-permute-start | bytes 540680 | tf_op jit(solution)/shard_map/ppermute | solution.py:27
  240.2 7.8 %copy-start.3 = (bf16[2048,128]{0,1:T(8,128)(2,1)S(1)}, bf16[2048,128]{0,1:T(8,128)(2,1)}, u32[]{:S(2)}) copy-start(bf16[2048,128]{0,1:T(8,128)(2,1)} %copy-done.2) | copy-start | bytes 1572868
  240.2 7.8 %copy-start.13 = (bf16[4,1,32,2048]{3,2,1,0:T(8,128)(2,1)S(1)}, bf16[4,1,32,2048]{3,2,1,0:T(8,128)(2,1)}, u32[]{:S(2)}) copy-start(bf16[4,1,32,2048]{3,2,1,0:T(8,128)(2,1)} %get-tuple-element.21) | copy-start | bytes 1572868
  262.6 10.3 %collective-permute-start.30 = (bf16[64,1408]{1,0:T(8,128)(2,1)S(1)}, bf16[64,1408]{1,0:T(8,128)(2,1)S(1)}, u32[]{:S(2)}, u32[]{:S(2)}) collective-permute-start(bf16[64,1408]{1,0:T(8,128)(2,1)S(1)} %get-tuple-element.26), channel_id=1, source_target_pairs={{0,4},{4,8},{8,12},{12,0},{1,5},{5,9},{9,13},{13,1},{2,6},{6,10},{... | collective-permute-start | bytes 540680 | tf_op jit(solution)/shard_map/ppermute | solution.py:27
  264.6 13.0 %collective-permute-start.32 = (bf16[64,1408]{1,0:T(8,128)(2,1)S(1)}, bf16[64,1408]{1,0:T(8,128)(2,1)}, u32[]{:S(2)}, u32[]{:S(2)}) collective-permute-start(bf16[64,1408]{1,0:T(8,128)(2,1)S(1)} %get-tuple-element.27), channel_id=1, source_target_pairs={{0,12},{4,0},{8,4},{12,8},{1,13},{5,1},{9,5},{13,9},{2,14},{6,2},{... | collective-permute-start | bytes 540680 | tf_op jit(solution)/shard_map/ppermute | solution.py:27
  268.4 15.7 %collective-permute-start.31 = (bf16[64,1408]{1,0:T(8,128)(2,1)S(1)}, bf16[64,1408]{1,0:T(8,128)(2,1)}, u32[]{:S(2)}, u32[]{:S(2)}) collective-permute-start(bf16[64,1408]{1,0:T(8,128)(2,1)S(1)} %get-tuple-element.28), channel_id=1, source_target_pairs={{0,8},{4,12},{8,0},{12,4},{1,9},{5,13},{9,1},{13,5},{2,10},{6,14},... | collective-permute-start | bytes 540680 | tf_op jit(solution)/shard_map/ppermute | solution.py:27
  286.8 6.9 %copy-start.7 = (bf16[64,1408]{1,0:T(8,128)(2,1)}, bf16[64,1408]{1,0:T(8,128)(2,1)S(1)}, u32[]{:S(2)}) copy-start(bf16[64,1408]{1,0:T(8,128)(2,1)S(1)} %get-tuple-element.9) | copy-start | bytes 540676
  286.8 10.3 %collective-permute-start.33 = (bf16[64,1408]{1,0:T(8,128)(2,1)S(1)}, bf16[64,1408]{1,0:T(8,128)(2,1)S(1)}, u32[]{:S(2)}, u32[]{:S(2)}) collective-permute-start(bf16[64,1408]{1,0:T(8,128)(2,1)S(1)} %get-tuple-element.9), channel_id=1, source_target_pairs={{0,4},{4,8},{8,12},{12,0},{1,5},{5,9},{9,13},{13,1},{2,6},{6,10},{... | collective-permute-start | bytes 540680 | tf_op jit(solution)/shard_map/ppermute | solution.py:27
  289.9 49.0 %collective-permute-start.42 = (bf16[1408,512]{1,0:T(8,128)(2,1)S(1)}, bf16[1408,512]{1,0:T(8,128)(2,1)}, u32[]{:S(2)}, u32[]{:S(2)}) collective-permute-start(bf16[1408,512]{1,0:T(8,128)(2,1)S(1)} %convolution_convert_fusion), channel_id=1, source_target_pairs={{0,1},{1,0},{2,3},{3,2},{4,5},{5,4},{6,7},{7,6},{8,9},{9,8},{10,11... | collective-permute-start | bytes 4325384 | tf_op jit(solution)/shard_map/ppermute | solution.py:32
  291.8 17.5 %collective-permute-start.34 = (bf16[64,1408]{1,0:T(8,128)(2,1)S(1)}, bf16[64,1408]{1,0:T(8,128)(2,1)S(1)}, u32[]{:S(2)}, u32[]{:S(2)}) collective-permute-start(bf16[64,1408]{1,0:T(8,128)(2,1)S(1)} %get-tuple-element.9), channel_id=1, source_target_pairs={{0,8},{4,12},{8,0},{12,4},{1,9},{5,13},{9,1},{13,5},{2,10},{6,14},... | collective-permute-start | bytes 540680 | tf_op jit(solution)/shard_map/ppermute | solution.py:27
  293.8 16.2 %collective-permute-start.35 = (bf16[64,1408]{1,0:T(8,128)(2,1)S(1)}, bf16[64,1408]{1,0:T(8,128)(2,1)S(1)}, u32[]{:S(2)}, u32[]{:S(2)}) collective-permute-start(bf16[64,1408]{1,0:T(8,128)(2,1)S(1)} %get-tuple-element.9), channel_id=1, source_target_pairs={{0,12},{4,0},{8,4},{12,8},{1,13},{5,1},{9,5},{13,9},{2,14},{6,2},{... | collective-permute-start | bytes 540680 | tf_op jit(solution)/shard_map/ppermute | solution.py:27
  318.2 10.7 %collective-permute-start.36 = (bf16[64,1408]{1,0:T(8,128)(2,1)S(1)}, bf16[64,1408]{1,0:T(8,128)(2,1)S(1)}, u32[]{:S(2)}, u32[]{:S(2)}) collective-permute-start(bf16[64,1408]{1,0:T(8,128)(2,1)S(1)} %get-tuple-element.23), channel_id=1, source_target_pairs={{0,4},{4,8},{8,12},{12,0},{1,5},{5,9},{9,13},{13,1},{2,6},{6,10},{... | collective-permute-start | bytes 540680 | tf_op jit(solution)/shard_map/ppermute | solution.py:27
  320.1 11.3 %collective-permute-start.38 = (bf16[64,1408]{1,0:T(8,128)(2,1)S(1)}, bf16[64,1408]{1,0:T(8,128)(2,1)S(1)}, u32[]{:S(2)}, u32[]{:S(2)}) collective-permute-start(bf16[64,1408]{1,0:T(8,128)(2,1)S(1)} %get-tuple-element.24), channel_id=1, source_target_pairs={{0,12},{4,0},{8,4},{12,8},{1,13},{5,1},{9,5},{13,9},{2,14},{6,2},{... | collective-permute-start | bytes 540680 | tf_op jit(solution)/shard_map/ppermute | solution.py:27
  324.0 13.7 %collective-permute-start.37 = (bf16[64,1408]{1,0:T(8,128)(2,1)S(1)}, bf16[64,1408]{1,0:T(8,128)(2,1)S(1)}, u32[]{:S(2)}, u32[]{:S(2)}) collective-permute-start(bf16[64,1408]{1,0:T(8,128)(2,1)S(1)} %get-tuple-element.25), channel_id=1, source_target_pairs={{0,8},{4,12},{8,0},{12,4},{1,9},{5,13},{9,1},{13,5},{2,10},{6,14},... | collective-permute-start | bytes 540680 | tf_op jit(solution)/shard_map/ppermute | solution.py:27
  340.9 25.2 %copy-start.8 = (bf16[64,1408]{1,0:T(8,128)(2,1)S(1)}, bf16[64,1408]{1,0:T(8,128)(2,1)}, u32[]{:S(2)}) copy-start(bf16[64,1408]{1,0:T(8,128)(2,1)} %copy-done.7) | copy-start | bytes 540676
  341.0 21.2 %collective-permute-start.43 = (bf16[352,512]{1,0:T(8,128)(2,1)S(1)}, bf16[352,512]{1,0:T(8,128)(2,1)S(1)}, u32[]{:S(2)}, u32[]{:S(2)}) collective-permute-start(bf16[352,512]{1,0:T(8,128)(2,1)S(1)} %get-tuple-element.18), channel_id=1, source_target_pairs={{0,128},{128,256},{256,384},{384,0},{1,129},{129,257},{257,385},{3... | collective-permute-start | bytes 1081352 | tf_op jit(solution)/shard_map/ppermute | solution.py:27
  342.9 20.4 %collective-permute-start.45 = (bf16[352,512]{1,0:T(8,128)(2,1)S(1)}, bf16[352,512]{1,0:T(8,128)(2,1)S(1)}, u32[]{:S(2)}, u32[]{:S(2)}) collective-permute-start(bf16[352,512]{1,0:T(8,128)(2,1)S(1)} %get-tuple-element.19), channel_id=1, source_target_pairs={{0,384},{128,0},{256,128},{384,256},{1,385},{129,1},{257,129},{385... | collective-permute-start | bytes 1081352 | tf_op jit(solution)/shard_map/ppermute | solution.py:27
  348.1 15.3 %collective-permute-start.44 = (bf16[352,512]{1,0:T(8,128)(2,1)S(1)}, bf16[352,512]{1,0:T(8,128)(2,1)S(1)}, u32[]{:S(2)}, u32[]{:S(2)}) collective-permute-start(bf16[352,512]{1,0:T(8,128)(2,1)S(1)} %get-tuple-element.20), channel_id=1, source_target_pairs={{0,256},{128,384},{256,0},{384,128},{1,257},{129,385},{257,1},{385... | collective-permute-start | bytes 1081352 | tf_op jit(solution)/shard_map/ppermute | solution.py:27
  363.6 13.5 %collective-permute-start.46 = (bf16[352,256]{1,0:T(8,128)(2,1)S(1)}, bf16[352,256]{1,0:T(8,128)(2,1)S(1)}, u32[]{:S(2)}, u32[]{:S(2)}) collective-permute-start(bf16[352,256]{1,0:T(8,128)(2,1)S(1)} %slice.123), channel_id=1, source_target_pairs={{0,2},{2,0},{1,3},{3,1},{4,6},{6,4},{5,7},{7,5},{8,10},{10,8},{9,1... | collective-permute-start | bytes 540680 | tf_op jit(solution)/shard_map/ppermute | solution.py:32
  366.4 26.4 %collective-permute-start.40 = (bf16[64,1408]{1,0:T(8,128)(2,1)S(1)}, bf16[64,1408]{1,0:T(8,128)(2,1)S(1)}, u32[]{:S(2)}, u32[]{:S(2)}) collective-permute-start(bf16[64,1408]{1,0:T(8,128)(2,1)S(1)} %get-tuple-element.6), channel_id=1, source_target_pairs={{0,8},{4,12},{8,0},{12,4},{1,9},{5,13},{9,1},{13,5},{2,10},{6,14},... | collective-permute-start | bytes 540680 | tf_op jit(solution)/shard_map/ppermute | solution.py:27
  368.3 13.7 %collective-permute-start.39 = (bf16[64,1408]{1,0:T(8,128)(2,1)S(1)}, bf16[64,1408]{1,0:T(8,128)(2,1)S(1)}, u32[]{:S(2)}, u32[]{:S(2)}) collective-permute-start(bf16[64,1408]{1,0:T(8,128)(2,1)S(1)} %get-tuple-element.6), channel_id=1, source_target_pairs={{0,4},{4,8},{8,12},{12,0},{1,5},{5,9},{9,13},{13,1},{2,6},{6,10},{... | collective-permute-start | bytes 540680 | tf_op jit(solution)/shard_map/ppermute | solution.py:27
  372.4 25.2 %collective-permute-start.41 = (bf16[64,1408]{1,0:T(8,128)(2,1)S(1)}, bf16[64,1408]{1,0:T(8,128)(2,1)S(1)}, u32[]{:S(2)}, u32[]{:S(2)}) collective-permute-start(bf16[64,1408]{1,0:T(8,128)(2,1)S(1)} %get-tuple-element.6), channel_id=1, source_target_pairs={{0,12},{4,0},{8,4},{12,8},{1,13},{5,1},{9,5},{13,9},{2,14},{6,2},{... | collective-permute-start | bytes 540680 | tf_op jit(solution)/shard_map/ppermute | solution.py:27
  377.2 11.6 %collective-permute-start.47 = (bf16[4,44,256]{2,1,0:T(8,128)(2,1)S(1)}, bf16[4,44,256]{2,1,0:T(8,128)(2,1)S(1)}, u32[]{:S(2)}, u32[]{:S(2)}) collective-permute-start(bf16[4,44,256]{2,1,0:T(8,128)(2,1)S(1)} %dynamic-slice_convert_fusion), channel_id=1, source_target_pairs={{0,64},{16,80},{32,96},{48,112},{64,0},{80,16},{96,32},{112,48},{1... | collective-permute-start | bytes 270344 | tf_op jit(solution)/shard_map/ppermute | solution.py:32
  388.8 6.9 %collective-permute-start.48 = (bf16[2,44,256]{2,1,0:T(8,128)(2,1)S(1)}, bf16[2,44,256]{2,1,0:T(8,128)(2,1)S(1)}, u32[]{:S(2)}, u32[]{:S(2)}) collective-permute-start(bf16[2,44,256]{2,1,0:T(8,128)(2,1)S(1)} %dynamic-slice_convert_fusion.1), channel_id=1, source_target_pairs={{0,32},{16,48},{32,0},{48,16},{64,96},{80,112},{96,64},{112,80},{1... | collective-permute-start | bytes 135176 | tf_op jit(solution)/shard_map/ppermute | solution.py:32
  395.7 5.7 %collective-permute-start.49 = (bf16[1,44,256]{2,1,0:T(8,128)(2,1)S(1)}, bf16[1,44,256]{2,1,0:T(8,128)(2,1)S(1)}, u32[]{:S(2)}, u32[]{:S(2)}) collective-permute-start(bf16[1,44,256]{2,1,0:T(8,128)(2,1)S(1)} %dynamic-slice_convert_fusion.2), channel_id=1, source_target_pairs={{0,16},{16,0},{32,48},{48,32},{64,80},{80,64},{96,112},{112,96},{1... | collective-permute-start | bytes 67592 | tf_op jit(solution)/shard_map/ppermute | solution.py:32
  397.7 4.4 %copy-start.6 = (bf16[1,256,1408]{2,1,0:T(8,128)(2,1)}, bf16[1,256,1408]{2,1,0:T(8,128)(2,1)S(1)}, u32[]{:S(2)}) copy-start(bf16[1,256,1408]{2,1,0:T(8,128)(2,1)S(1)} %bitcast_dynamic-update-slice_fusion) | copy-start | bytes 2162692
  (6 other events, 10.4 us)

commit v2 on v1

v2 whole, which is shorter than its diff:
```python
import functools

import jax
import jax.numpy as jnp
from jax import lax
from jax.experimental import pallas as pl
from jax.experimental.pallas import tpu as pltpu
from jax.sharding import Mesh, PartitionSpec as P

HEAD_DIM = 128
EPSILON = 1e-06
BF = jnp.bfloat16
F32 = jnp.float32
PARTS = 4
PARAMS = pltpu.CompilerParams(vmem_limit_bytes=48 * 1024 * 1024)
VMEM = pl.BlockSpec(memory_space=pltpu.VMEM)
ANY = pl.BlockSpec(memory_space=pl.ANY)
SMEM = pl.BlockSpec(memory_space=pltpu.SMEM)
LAST = (((1,), (1,)), ((), ()))


def layer_norm(values, gain):
    floats = values.astype(F32)
    centre = jnp.mean(floats, axis=-1, keepdims=True)
    spread = jnp.mean(jnp.square(floats - centre), axis=-1, keepdims=True)
    inverse = lax.rsqrt(spread + EPSILON)
    normal = (floats - centre) * inverse
    return (normal * gain, normal, inverse)


def gelu_pair(values):
    c = 0.7978845608028654
    square = values * values
    tanh = jnp.tanh(c * values * (1.0 + 0.044715 * square))
    half = 0.5 * (1.0 + tanh)
    slope = half + 0.5 * values * (1.0 - tanh * tanh) * c * (1.0 + 3 * 0.044715 * square)
    return values * half, slope


def dot(a, b):
    return jnp.dot(a, b, preferred_element_type=F32)


def dot_last(a, b):
    return lax.dot_general(a, b, LAST, preferred_element_type=F32)


def block_copies(place, blocks, whole, sems):
    rows = blocks[0].shape[0]
    group = place[0]
    copies = []
    for bits, block in enumerate(blocks):
        start = pl.multiple_of((group ^ bits) * rows, 16)
        copies.append(pltpu.make_async_copy(block, whole.at[pl.ds(start, rows)], sems.at[bits]))
    return copies


def up_kernel(place, image, gain, u0, u1, u2, u3, act, slope, in_rows, up, rows4, sems, row_sems):
    copies = block_copies(place, (u0, u1, u2, u3), up, sems)
    rows = in_rows.shape[0]
    moves = []
    for k in range(PARTS):
        start = pl.multiple_of(lax.rem(place[1] + PARTS - k, PARTS) * rows, 16)
        moves.append(
            pltpu.make_async_copy(
                image.at[pl.ds(start, rows)], rows4.at[pl.ds(k * rows, rows)], row_sems.at[k]
            )
        )
    for copy in moves + copies:
        copy.start()
    for copy in moves:
        copy.wait()
    in_rows[...] = rows4[pl.ds(0, rows)]
    normed = layer_norm(rows4[...], gain[...])[0].astype(BF)
    for copy in copies:
        copy.wait()
    for n in range(4):
        cols = pl.ds(n * 256, 256)
        value, grad = gelu_pair(dot(normed, up[:, cols]))
        act[:, cols] = value.astype(BF)
        slope[:, cols] = grad


def down_kernel(place, act, d0, d1, d2, d3, o0, o1, o2, o3, down, sems):
    copies = block_copies(place, (d0, d1, d2, d3), down, sems)
    for copy in copies:
        copy.start()
    for copy in copies:
        copy.wait()
    split_rows(dot_last(act[...], down[...]).astype(BF), (o0, o1, o2, o3))


def split_rows(value, outs):
    rows = outs[0].shape[0]
    for k, out in enumerate(outs):
        out[...] = value[k * rows : (k + 1) * rows]


def query_kernel(caption, p0, p1, p2, p3, query, d_attn, w, sems):
    dec = caption.shape[-1]
    skip = p0.shape[1] - dec
    copies = [
        pltpu.make_async_copy(p.at[:, pl.ds(skip, dec)], w.at[k], sems.at[k])
        for k, p in enumerate((p0, p1, p2, p3))
    ]
    for copy in copies:
        copy.start()
    text = caption[:, 0].reshape(-1, dec)
    cot = caption[:, 1].reshape(-1, dec)
    for k, copy in enumerate(copies):
        copy.wait()
        query[k] = (dot_last(text, w[k, :HEAD_DIM]) * HEAD_DIM ** (-0.5)).astype(BF)
        d_attn[k] = dot_last(cot, w[k, HEAD_DIM:]).astype(BF)


def attention_kernel(
    e0, e1, e2, e3, query, d_attn, p0, p1, p2, p3, o0, o1, o2, o3, encoded, d_pair, w, sems
):
    width = e0.shape[1]
    copies = [
        pltpu.make_async_copy(p.at[:, pl.ds(0, width)], w.at[k], sems.at[k])
        for k, p in enumerate((p0, p1, p2, p3))
    ]
    for copy in copies:
        copy.start()
    rows = e0.shape[0]
    for k, e in enumerate((e0, e1, e2, e3)):
        encoded[pl.ds(k * rows, rows)] = e[...]
    tokens = encoded[...]
    term = None
    for k, copy in enumerate(copies):
        copy.wait()
        pair = dot_last(tokens, w[k]).astype(BF)
        keys, values = pair[:, :HEAD_DIM], pair[:, HEAD_DIM:]
        q, da = query[k], d_attn[k]
        scores = dot_last(keys, q)
        expo = jnp.exp(scores - jnp.max(scores, axis=0, keepdims=True))
        probs = expo / jnp.sum(expo, axis=0, keepdims=True)
        d_probs = dot_last(values, da)
        mean = jnp.sum(probs * d_probs, axis=0, keepdims=True)
        d_scores = (probs * (d_probs - mean)).astype(BF)
        d_keys = dot(d_scores, q).astype(BF)
        d_values = dot(probs.astype(BF), da).astype(BF)
        grads = jnp.concatenate([d_keys, d_values], axis=1)
        d_pair[:, pl.ds(k * 2 * HEAD_DIM, 2 * HEAD_DIM)] = grads
    for k in range(PARTS):
        part = dot(d_pair[:, pl.ds(k * 2 * HEAD_DIM, 2 * HEAD_DIM)], w[k])
        term = part if term is None else term + part
    split_rows(term.astype(BF), (o0, o1, o2, o3))


def back_kernel(
    place, g0, g1, g2, g3, slope, d0, d1, d2, d3, u0, u1, u2, u3,
    o0, o1, o2, o3, down, up, grads, d_pre, down_sems, up_sems,
):
    first = block_copies(place, (d0, d1, d2, d3), down, down_sems)
    second = block_copies(place, (u0, u1, u2, u3), up, up_sems)
    for copy in first + second:
        copy.start()
    rows = g0.shape[0]
    for k, g in enumerate((g0, g1, g2, g3)):
        grads[pl.ds(k * rows, rows)] = g[...]
    for copy in first:
        copy.wait()
    for n in range(4):
        cols = pl.ds(n * 256, 256)
        d_pre[:, cols] = (dot(grads[...], down[:, cols]) * slope[:, cols]).astype(BF)
    for copy in second:
        copy.wait()
    split_rows(dot_last(d_pre[...], up[...]).astype(BF), (o0, o1, o2, o3))


def shift(value, axis, by):
    size = lax.axis_size(axis)
    return lax.ppermute(value, axis, [(i, (i + by) % size) for i in range(size)])


def swap(value, axis, bit=1):
    size = lax.axis_size(axis)
    return lax.ppermute(value, axis, [(i, i ^ bit) for i in range(size)])


def rows_at(value, start, size):
    return lax.dynamic_slice_in_dim(value, start, size, axis=0)


def after(value, *others):
    return lax.optimization_barrier((value,) + others)[0]


def far_block(own, axis):
    quarter = own.shape[0] // PARTS
    piece = swap(rows_at(own, lax.axis_index(axis) * quarter, quarter), "yh")
    return lax.all_gather(piece, axis, axis=0, tiled=True)


def group_blocks(own, axis):
    far = far_block(own, axis)
    return own, swap(own, "core"), far, swap(far, "core")


def sum_blocks(blocks):
    total = blocks[0].astype(F32)
    for by in range(1, PARTS):
        total = total + shift(blocks[PARTS - by], "tensor", by).astype(F32)
    return total


def gather_blocks(block):
    return [block] + [shift(block, "tensor", by) for by in range(1, PARTS)]


def scatter_sum(partial, axis):
    size = lax.axis_size(axis)
    rows = partial.shape[0] // size
    here = lax.axis_index(axis)
    total = rows_at(partial, here * rows, rows).astype(F32)
    for by in range(1, size):
        block = rows_at(partial, lax.rem(here + by, size) * rows, rows)
        total = total + shift(block, axis, by).astype(F32)
    return total


def halved(partial, axis, bit):
    half = partial.shape[0] // 2
    side = (lax.axis_index(axis) // bit) % 2
    sent = rows_at(partial, (1 - side) * half, half).astype(BF)
    return rows_at(partial, side * half, half) + swap(sent, axis, bit).astype(F32)


def local(
    image_in, enc_gain, enc_up, enc_down, text_in, query_gain, w_query, w_key, w_value, w_out, cotangent
):
    _, patches, width = image_in.shape
    group = lax.axis_index("yh") * 2 + lax.axis_index("core")
    tensor = lax.axis_index("tensor")
    place = jnp.stack([group, tensor]).astype(jnp.int32)
    flat_in = image_in.reshape(patches, width)
    rows = patches // PARTS
    hidden = enc_up.shape[1]
    dec = w_query.shape[0]
    shape = jax.ShapeDtypeStruct
    row_outs = [shape((rows, width), BF)] * PARTS
    gain = enc_gain.reshape(1, width)
    dma = pltpu.SemaphoreType.DMA

    up = group_blocks(enc_up, "x")
    down = group_blocks(enc_down.T, "zl")
    pair_own = jnp.concatenate([w_key, w_value], axis=1).T
    text_own = jnp.concatenate([w_query.T, w_out], axis=0)
    heads = group_blocks(jnp.concatenate([pair_own, text_own], axis=1), "x")

    text_normed = layer_norm(text_in, query_gain)[0].astype(BF)
    both = jnp.stack([text_normed, cotangent], axis=1)
    group_rows = []
    for other in range(4):
        block = lax.dynamic_index_in_dim(both, group ^ other, axis=0, keepdims=False)
        if other:
            block = lax.ppermute(block, ("yh", "core"), [(i, i ^ other) for i in range(4)])
        group_rows.append(block)
    caption = jnp.concatenate(group_rows, axis=1)
    caption = lax.all_gather(caption, "tensor", axis=0)

    act, slope, in_rows = pl.pallas_call(
        up_kernel,
        name="encoder_up",
        out_shape=[shape((patches, hidden), BF), shape((patches, hidden), F32), row_outs[0]],
        in_specs=[SMEM, ANY, VMEM] + [ANY] * 4,
        out_specs=[VMEM] * 3,
        scratch_shapes=[
            pltpu.VMEM((width, hidden), BF),
            pltpu.VMEM((patches, width), BF),
            dma((4,)),
            dma((PARTS,)),
        ],
        compiler_params=PARAMS,
    )(place, flat_in, gain, *up)
    branch = pl.pallas_call(
        down_kernel,
        name="encoder_down",
        out_shape=row_outs,
        in_specs=[SMEM, VMEM] + [ANY] * 4,
        out_specs=[VMEM] * PARTS,
        scratch_shapes=[pltpu.VMEM((width, hidden), BF), dma((4,))],
        compiler_params=PARAMS,
    )(place, act, *down)
    encoded_rows = (in_rows.astype(F32) + sum_blocks(branch)).astype(BF)
    encoded_blocks = gather_blocks(encoded_rows)

    head_shape = shape((4, PARTS * caption.shape[2], HEAD_DIM), BF)
    query, d_attn = pl.pallas_call(
        query_kernel,
        name="query",
        out_shape=[head_shape, head_shape],
        in_specs=[VMEM] + [ANY] * 4,
        out_specs=[VMEM] * 2,
        scratch_shapes=[pltpu.VMEM((4, 2 * HEAD_DIM, dec), BF), dma((4,))],
        compiler_params=PARAMS,
    )(caption, *heads)
    *term, encoded, d_pair = pl.pallas_call(
        attention_kernel,
        name="attention",
        out_shape=row_outs + [shape((patches, width), BF), shape((patches, 8 * HEAD_DIM), BF)],
        in_specs=[VMEM] * 6 + [ANY] * 4,
        out_specs=[VMEM] * 6,
        scratch_shapes=[pltpu.VMEM((4, 2 * HEAD_DIM, width), BF), dma((4,))],
        compiler_params=PARAMS,
    )(*encoded_blocks, query, d_attn, *heads)
    grad_rows = sum_blocks(term).astype(BF)
    grad_blocks = gather_blocks(grad_rows)

    pair_cols = 2 * HEAD_DIM
    cols = [d_pair[:, k * pair_cols : (k + 1) * pair_cols] for k in range(4)]
    contract = (((0,), (0,)), ((), ()))
    give = lax.dot_general(
        encoded, jnp.concatenate([cols[1], cols[3]], axis=1), contract, preferred_element_type=F32
    ).astype(BF)
    keep = lax.dot_general(
        encoded, jnp.concatenate([cols[0], cols[2]], axis=1), contract, preferred_element_type=F32
    )
    sums = (keep + swap(give, "core").astype(F32)).astype(BF)
    sums = scatter_sum(after(sums, grad_rows), "x")
    sums = sums[:, :pair_cols] + swap(sums[:, pair_cols:].astype(BF), "yh").astype(F32)
    sums = sums.reshape(8, -1, pair_cols)
    sums = halved(sums, "zh", 1)
    for bit in (2, 1):
        sums = halved(sums, "zl", bit)
    sums = sums[0]
    key_grad, value_grad = sums[:, :HEAD_DIM], sums[:, HEAD_DIM:]

    d_norm = pl.pallas_call(
        back_kernel,
        name="encoder_back",
        out_shape=row_outs,
        in_specs=[SMEM] + [VMEM] * 5 + [ANY] * 8,
        out_specs=[VMEM] * PARTS,
        scratch_shapes=[
            pltpu.VMEM((width, hidden), BF),
            pltpu.VMEM((width, hidden), BF),
            pltpu.VMEM((patches, width), BF),
            pltpu.VMEM((patches, hidden), BF),
            dma((4,)),
            dma((4,)),
        ],
        compiler_params=PARAMS,
    )(place, *grad_blocks, slope, *down, *up)
    d_normed = sum_blocks(d_norm)
    _, normal, inverse = layer_norm(in_rows, enc_gain)
    scaled_grad = d_normed * enc_gain
    d_input = inverse * (
        scaled_grad
        - jnp.mean(scaled_grad, axis=-1, keepdims=True)
        - normal * jnp.mean(scaled_grad * normal, axis=-1, keepdims=True)
    )
    image_rows = (grad_rows.astype(F32) + d_input).astype(BF)
    image_grad = lax.all_gather(image_rows, "tensor", axis=0, tiled=True).reshape(1, patches, width)
    return (image_grad, key_grad, value_grad)


def solution(mesh):
    fine = Mesh(
        mesh.devices.reshape(4, 2, 4, 4, 2, 2), ("x", "zh", "zl", "tensor", "yh", "core")
    )
    dp, group, heads = ("x", "zh", "zl"), ("yh", "core"), ("tensor", "yh", "core")
    in_specs = (
        P(dp + group, None, None),
        P(),
        P(group, "tensor"),
        P("tensor", group),
        P(dp, heads, None),
        P(),
        P(None, heads),
        P(None, heads),
        P(None, heads),
        P(heads, None),
        P(dp, heads, None),
    )
    out_specs = (P(dp + group, None, None), P(dp, heads), P(dp, heads))
    return jax.shard_map(local, mesh=fine, in_specs=in_specs, out_specs=out_specs, check_vma=False)
```

time: 409 us -> 322 us (0.79); the launches traced: 402 us -> 321 us
  local copies, waits for them, and re-layouts: 75.6 us -> 13.6 us
  blocking collectives: 0 us -> 55.5 us
  starting transfers between devices: 166 us -> 119 us
  waiting for transfers between devices: 124 us -> 83.6 us
  Pallas kernels: 0 us -> 22 us
  matrix products: 22.9 us -> 3.64 us
  between operations: 2.19 us -> 14.9 us
    all_gather x0 -> x3, blocking collectives: none -> 55.5 us  [the longest x2 38.4 us: far_block(): return lax.all_gather(piece, axis, axis=0, tiled=True)]
    ppermute x33 -> x18, waiting for transfers between devices: 109 us -> 53.5 us  [shift(): lax.ppermute(value, axis, [(i, (i + by) % size) for i in range(size)])]
    ppermute x33 -> x18, starting transfers between devices: 109 us -> 59.4 us  [shift(): lax.ppermute(value, axis, [(i, (i + by) % size) for i in range(size)])]
    dynamic_update_slice x31 -> x0, local copies, waits for them, and re-layouts: 45.8 us -> none  [put(): return lax.dynamic_update_slice_in_dim(buffer, block, start, axis=0)]
    pallas_call x0 -> x5, Pallas kernels: none -> 22 us  [the longest x1 6.22 us: local(): pl.pallas_call(attention_kernel, name='attention', out_shape=row_outs + [...]
    dot_general x12 -> x2, matrix products: 22.4 us -> 3.64 us  [the longest x1 1.93 us: local(): lax.dot_general(encoded, jnp.concatenate([cols[0], cols[2]], axis=1), con...]
    ppermute x14, waiting for transfers between devices: 15.5 us -> 30 us  [swap(): return lax.ppermute(value, axis, [(i, i ^ bit) for i in range(size)])]
    another operation x7 -> x0, local copies, waits for them, and re-layouts: 5.94 us -> none
  transfers between devices with their start and end apart: 50 -> 37, of which waited for: 20 -> 11; matrix products, arithmetic and copies ran while one was open for 21% -> 4% of each run, Pallas kernels for 0% -> 5%
where the time goes in v2:
time: 322 us; the launch traced here: 321 us
  starting transfers between devices  119 us (37%)
  waiting for transfers between devices  83.6 us (26%)
  blocking collectives  55.5 us (17%)
  Pallas kernels  22 us (7%)
  between operations  14.9 us (5%)
  local copies, waits for them, and re-layouts  13.6 us (4%)
  other arithmetic  8.56 us (3%)
  matrix products  3.64 us (1%)
    ppermute x18, starting transfers between devices, shift(): lax.ppermute(value, axis, [(i, (i + by) % size) for i in range(size)])  59.4 us
    ppermute x18, waiting for transfers between devices, shift(): lax.ppermute(value, axis, [(i, (i + by) % size) for i in range(size)])  53.5 us
    ppermute x14, starting transfers between devices, swap(): return lax.ppermute(value, axis, [(i, i ^ bit) for i in range(size)])  47.8 us
    all_gather x2, blocking collectives, far_block(): return lax.all_gather(piece, axis, axis=0, tiled=True)  38.4 us
    ppermute x14, waiting for transfers between devices, swap(): return lax.ppermute(value, axis, [(i, i ^ bit) for i in range(size)])  30 us
    all_gather x1, blocking collectives, local(): lax.all_gather(image_rows, 'tensor', axis=0, tiled=True)  17.1 us
    ppermute x3, starting transfers between devices, local(): lax.ppermute(block, ('yh', 'core'), [(i, i ^ other) for i in range(4)])  11.6 us
    unnamed x34, local copies, waits for them, and re-layouts  9.43 us
  transfers between devices with their start and end apart: 37, of which 11 were waited for; matrix products, arithmetic and copies ran while one was open for 4% of the time, Pallas kernels for 5%

profile of v2, /device:TPU:56, one launch (start us, length us, event | category | flops | bytes accessed | tf_op | source)
XLA Modules:
  0.0 320.7 jit_solution(6124556653081898529)
XLA Ops:
  7.2 1.2 copy.20
  8.5 1.2 copy.21
  10.2 4.7 %collective-permute-start.16 = (bf16[64,3456]{1,0:T(8,128)(2,1)S(1)}, bf16[64,3456]{1,0:T(8,128)(2,1)S(1)}, u32[]{:S(2)}, u32[]{:S(2)}) collective-permute-start(bf16[64,3456]{1,0:T(8,128)(2,1)S(1)} %constant_dynamic-slice_fusion.3), channel_id=1, source_target_pairs={{0,2},{2,0},{1,3},{3,1},{4,6},{6,4},{5,7},{7,5},{8,10},{10,8},{9,1... | collective-permute-start | bytes 1327112 | tf_op jit(solution)/shard_map/ppermute | solution.py:180
  14.9 22.3 %collective-permute-done.16 = bf16[64,3456]{1,0:T(8,128)(2,1)S(1)} collective-permute-done((bf16[64,3456]{1,0:T(8,128)(2,1)S(1)}, bf16[64,3456]{1,0:T(8,128)(2,1)S(1)}, u32[]{:S(2)}, u32[]{:S(2)}) %collective-permute-start.16) | collective-permute-done | bytes 442400 | tf_op jit(solution)/shard_map/ppermute | solution.py:180
  38.0 1.9 collective-permute-start.15
  43.1 1.5 fusion.27
  44.7 2.5 collective-permute-start.12
  47.2 2.6 collective-permute-start.13
  49.9 6.4 %collective-permute-start.14 = (bf16[2,8,2048]{2,1,0:T(8,128)(2,1)}, bf16[2,8,2048]{2,1,0:T(8,128)(2,1)}, u32[]{:S(2)}, u32[]{:S(2)}) collective-permute-start(bf16[2,8,2048]{2,1,0:T(8,128)(2,1)} %get-tuple-element.56), channel_id=1, source_target_pairs={{0,3},{1,2},{2,1},{3,0},{4,7},{5,6},{6,5},{7,4},{8,11},{9,10},{10,... | collective-permute-start | bytes 196616 | tf_op jit(solution)/shard_map/ppermute | solution.py:259
  56.3 2.7 collective-permute-start
  59.0 1.6 constant_dynamic-slice_fusion.4
  60.6 1.6 dynamic-slice_bitcast_fusion
  62.2 2.7 collective-permute-start.1
  64.9 7.1 %collective-permute-start.4 = (bf16[88,1024]{1,0:T(8,128)(2,1)}, bf16[88,1024]{1,0:T(8,128)(2,1)}, u32[]{:S(2)}, u32[]{:S(2)}) collective-permute-start(bf16[88,1024]{1,0:T(8,128)(2,1)} %dynamic-slice_bitcast_fusion), channel_id=1, source_target_pairs={{0,2},{2,0},{1,3},{3,1},{4,6},{6,4},{5,7},{7,5},{8,10},{10,8},{9,1... | collective-permute-start | bytes 540680 | tf_op jit(solution)/shard_map/ppermute | solution.py:180
  72.0 1.9 collective-permute-start.3
  73.9 1.7 pad_maximum_fusion
  75.6 3.2 %collective-permute-done.1 = bf16[88,1024]{1,0:T(8,128)(2,1)} collective-permute-done((bf16[88,1024]{1,0:T(8,128)(2,1)}, bf16[88,1024]{1,0:T(8,128)(2,1)}, u32[]{:S(2)}, u32[]{:S(2)}) %collective-permute-start.1) | collective-permute-done | bytes 180256 | tf_op jit(solution)/shard_map/ppermute | solution.py:180
  78.9 1.9 collective-permute-start.17
  80.8 16.3 %all_gather.18.u2 = bf16[352,1024]{1,0:T(8,128)(2,1)} all-gather(bf16[88,1024]{1,0:T(8,128)(2,1)} %collective-permute-done.1), channel_id=1, replica_groups=mesh['x'=4,'zh'=2,'zl'=4,'tensor'=4,'yh'=2,'core'=2] {'x'}, dimensions={0}, use_global_device_ids=true | all-gather | bytes 901120 | tf_op jit(solution)/shard_map/all_gather | solution.py:194
  97.1 1.9 collective-permute-start.2
  99.0 22.1 %all_gather.19.d2 = bf16[352,1024]{1,0:T(8,128)(2,1)} all-gather(bf16[88,1024]{1,0:T(8,128)(2,1)} %collective-permute-done.4), channel_id=1, replica_groups=mesh['x'=4,'zh'=2,'zl'=4,'tensor'=4,'yh'=2,'core'=2] {'zl'}, dimensions={0}, use_global_device_ids=true | all-gather | bytes 901120 | tf_op jit(solution)/shard_map/all_gather | solution.py:194
  121.1 1.9 collective-permute-start.5
  123.1 1.1 copy-done.3
  125.3 4.9 %encoder_up.1 = (bf16[256,1024]{1,0:T(8,128)(2,1)S(1)}, f32[256,1024]{1,0:T(8,128)S(1)}, bf16[64,1408]{1,0:T(8,128)(2,1)S(1)}) custom-call(s32[2]{0:T(128)S(1)} %pad_add_fusion.place, bf16[256,1408]{1,0:T(8,128)(2,1)S(1)} %bitcast.30, f32[1,1408]{1,0:T(1,128)S(1)} %reshape.53.gain, bf16[352,1024]{1,0:T(8,128)(2,1)S(1)} %copy-done.3, ...), custom_call_target="tpu_custom_call" | custom-call | tf_op jit(solution)/shard_map/encoder_up/pallas_call | solution.py:264
  131.3 3.4 %encoder_down.1 = (bf16[64,1408]{1,0:T(8,128)(2,1)S(1)}, bf16[64,1408]{1,0:T(8,128)(2,1)S(1)}, bf16[64,1408]{1,0:T(8,128)(2,1)S(1)}, bf16[64,1408]{1,0:T(8,128)(2,1)S(1)}) custom-call(s32[2]{0:T(128)S(1)} %pad_add_fusion.place, bf16[256,1024]{1,0:T(8,128)(2,1)S(1)} %get-tuple-element.24.act, bf16[352,1024]{1,0:T(8,128)(2,1)S(1)} %bitcast.27, ...), custom_call_target="tpu_custom_call" | custom-call | tf_op jit(solution)/shard_map/encoder_down/pallas_call | solution.py:278
  134.7 5.6 %collective-permute-start.6 = (bf16[64,1408]{1,0:T(8,128)(2,1)S(1)}, bf16[64,1408]{1,0:T(8,128)(2,1)S(1)}, u32[]{:S(2)}, u32[]{:S(2)}) collective-permute-start(bf16[64,1408]{1,0:T(8,128)(2,1)S(1)} %get-tuple-element.26), channel_id=1, source_target_pairs={{0,4},{4,8},{8,12},{12,0},{1,5},{5,9},{9,13},{13,1},{2,6},{6,10},{... | collective-permute-start | bytes 540680 | tf_op jit(solution)/shard_map/ppermute | solution.py:175
  140.3 2.2 collective-permute-start.7
  142.5 3.6 %collective-permute-start.8 = (bf16[64,1408]{1,0:T(8,128)(2,1)S(1)}, bf16[64,1408]{1,0:T(8,128)(2,1)S(1)}, u32[]{:S(2)}, u32[]{:S(2)}) collective-permute-start(bf16[64,1408]{1,0:T(8,128)(2,1)S(1)} %get-tuple-element.28), channel_id=1, source_target_pairs={{0,12},{4,0},{8,4},{12,8},{1,13},{5,1},{9,5},{13,9},{2,14},{6,2},{... | collective-permute-start | bytes 540680 | tf_op jit(solution)/shard_map/ppermute | solution.py:175
  146.2 11.4 %collective-permute-done.7 = bf16[64,1408]{1,0:T(8,128)(2,1)S(1)} collective-permute-done((bf16[64,1408]{1,0:T(8,128)(2,1)S(1)}, bf16[64,1408]{1,0:T(8,128)(2,1)S(1)}, u32[]{:S(2)}, u32[]{:S(2)}) %collective-permute-start.7) | collective-permute-done | bytes 180256 | tf_op jit(solution)/shard_map/ppermute | solution.py:175
  158.4 4.2 %collective-permute-start.10 = (bf16[64,1408]{1,0:T(8,128)(2,1)}, bf16[64,1408]{1,0:T(8,128)(2,1)}, u32[]{:S(2)}, u32[]{:S(2)}) collective-permute-start(bf16[64,1408]{1,0:T(8,128)(2,1)} %get-tuple-element.57.e0), channel_id=1, source_target_pairs={{0,8},{4,12},{8,0},{12,4},{1,9},{5,13},{9,1},{13,5},{2,10},{6,14},... | collective-permute-start | bytes 540680 | tf_op jit(solution)/shard_map/ppermute | solution.py:175
  162.6 1.9 collective-permute-start.11
  164.6 5.7 %collective-permute-start.9 = (bf16[64,1408]{1,0:T(8,128)(2,1)}, bf16[64,1408]{1,0:T(8,128)(2,1)}, u32[]{:S(2)}, u32[]{:S(2)}) collective-permute-start(bf16[64,1408]{1,0:T(8,128)(2,1)} %get-tuple-element.57.e0), channel_id=1, source_target_pairs={{0,4},{4,8},{8,12},{12,0},{1,5},{5,9},{9,13},{13,1},{2,6},{6,10},{... | collective-permute-start | bytes 540680 | tf_op jit(solution)/shard_map/ppermute | solution.py:175
  170.4 1.9 copy-done.8
  172.2 2.3 query.1
  174.5 1.2 collective-permute-done.10.e2
  175.7 3.6 %collective-permute-done.9.e1 = bf16[64,1408]{1,0:T(8,128)(2,1)} collective-permute-done((bf16[64,1408]{1,0:T(8,128)(2,1)}, bf16[64,1408]{1,0:T(8,128)(2,1)}, u32[]{:S(2)}, u32[]{:S(2)}) %collective-permute-start.9) | collective-permute-done | bytes 180256 | tf_op jit(solution)/shard_map/ppermute | solution.py:175
  179.3 6.2 %attention.1 = (bf16[64,1408]{1,0:T(8,128)(2,1)S(1)}, bf16[64,1408]{1,0:T(8,128)(2,1)S(1)}, bf16[64,1408]{1,0:T(8,128)(2,1)S(1)}, bf16[64,1408]{1,0:T(8,128)(2,1...) custom-call(bf16[64,1408]{1,0:T(8,128)(2,1)} %get-tuple-element.57.e0, ...), custom_call_target="tpu_custom_call" | custom-call | tf_op jit(solution)/shard_map/attention/pallas_call | solution.py:300
  185.6 1.7 convolution_convert_fusion
  187.3 1.9 collective-permute-start.27
  189.2 1.9 collective-permute-start.18
  191.1 4.0 %collective-permute-start.19 = (bf16[64,1408]{1,0:T(8,128)(2,1)S(1)}, bf16[64,1408]{1,0:T(8,128)(2,1)S(1)}, u32[]{:S(2)}, u32[]{:S(2)}) collective-permute-start(bf16[64,1408]{1,0:T(8,128)(2,1)S(1)} %get-tuple-element.33), channel_id=1, source_target_pairs={{0,8},{4,12},{8,0},{12,4},{1,9},{5,13},{9,1},{13,5},{2,10},{6,14},... | collective-permute-start | bytes 540680 | tf_op jit(solution)/shard_map/ppermute | solution.py:175
  195.1 1.9 collective-permute-start.20
  197.1 1.2 collective-permute-done.18
  198.3 11.3 %collective-permute-done.19 = bf16[64,1408]{1,0:T(8,128)(2,1)S(1)} collective-permute-done((bf16[64,1408]{1,0:T(8,128)(2,1)S(1)}, bf16[64,1408]{1,0:T(8,128)(2,1)S(1)}, u32[]{:S(2)}, u32[]{:S(2)}) %collective-permute-start.19) | collective-permute-done | bytes 180256 | tf_op jit(solution)/shard_map/ppermute | solution.py:175
  209.8 2.1 collective-permute-start.21
  211.9 1.9 fusion
  213.9 2.1 collective-permute-start.28
  216.0 4.5 %collective-permute-start.29 = (bf16[352,512]{1,0:T(8,128)(2,1)S(1)}, bf16[352,512]{1,0:T(8,128)(2,1)S(1)}, u32[]{:S(2)}, u32[]{:S(2)}) collective-permute-start(bf16[352,512]{1,0:T(8,128)(2,1)S(1)} %get-tuple-element.48), channel_id=1, source_target_pairs={{0,256},{128,384},{256,0},{384,128},{1,257},{129,385},{257,1},{385... | collective-permute-start | bytes 1081352 | tf_op jit(solution)/shard_map/ppermute | solution.py:175
  220.5 3.4 %collective-permute-start.30 = (bf16[352,512]{1,0:T(8,128)(2,1)S(1)}, bf16[352,512]{1,0:T(8,128)(2,1)S(1)}, u32[]{:S(2)}, u32[]{:S(2)}) collective-permute-start(bf16[352,512]{1,0:T(8,128)(2,1)S(1)} %get-tuple-element.47), channel_id=1, source_target_pairs={{0,384},{128,0},{256,128},{384,256},{1,385},{129,1},{257,129},{385... | collective-permute-start | bytes 1081352 | tf_op jit(solution)/shard_map/ppermute | solution.py:175
  224.2 3.1 collective-permute-start.22
  227.3 3.9 %collective-permute-start.23 = (bf16[64,1408]{1,0:T(8,128)(2,1)S(1)}, bf16[64,1408]{1,0:T(8,128)(2,1)S(1)}, u32[]{:S(2)}, u32[]{:S(2)}) collective-permute-start(bf16[64,1408]{1,0:T(8,128)(2,1)S(1)} %add_convert_fusion.g0), channel_id=1, source_target_pairs={{0,12},{4,0},{8,4},{12,8},{1,13},{5,1},{9,5},{13,9},{2,14},{6,2},{... | collective-permute-start | bytes 540680 | tf_op jit(solution)/shard_map/ppermute | solution.py:175
  231.2 8.8 %collective-permute-done.22.g2 = bf16[64,1408]{1,0:T(8,128)(2,1)S(1)} collective-permute-done((bf16[64,1408]{1,0:T(8,128)(2,1)S(1)}, bf16[64,1408]{1,0:T(8,128)(2,1)S(1)}, u32[]{:S(2)}, u32[]{:S(2)}) %collective-permute-start.22) | collective-permute-done | bytes 180256 | tf_op jit(solution)/shard_map/ppermute | solution.py:175
  240.0 5.2 %encoder_back.1 = (bf16[64,1408]{1,0:T(8,128)(2,1)S(1)}, bf16[64,1408]{1,0:T(8,128)(2,1)S(1)}, bf16[64,1408]{1,0:T(8,128)(2,1)S(1)}, bf16[64,1408]{1,0:T(8,128)(2,1)S(1)}) custom-call(s32[2]{0:T(128)S(1)} %pad_add_fusion.place, bf16[64,1408]{1,0:T(8,128)(2,1)S(1)} %add_convert_fusion.g0, bf16[64,1408]{1,0:T(8,128)(2,1)S(1)} %collective-permute-done.21.g1, ...), custom_call_target="tpu_custom_call" | custom-call | tf_op jit(solution)/shard_map/encoder_back/pallas_call | solution.py:331
  245.2 2.8 collective-permute-start.24
  248.0 2.6 collective-permute-start.25
  250.6 3.9 %collective-permute-start.26 = (bf16[64,1408]{1,0:T(8,128)(2,1)S(1)}, bf16[64,1408]{1,0:T(8,128)(2,1)S(1)}, u32[]{:S(2)}, u32[]{:S(2)}) collective-permute-start(bf16[64,1408]{1,0:T(8,128)(2,1)S(1)} %get-tuple-element.39), channel_id=1, source_target_pairs={{0,12},{4,0},{8,4},{12,8},{1,13},{5,1},{9,5},{13,9},{2,14},{6,2},{... | collective-permute-start | bytes 540680 | tf_op jit(solution)/shard_map/ppermute | solution.py:175
  254.8 1.9 collective-permute-start.31
  256.7 16.0 %collective-permute-done.25 = bf16[64,1408]{1,0:T(8,128)(2,1)S(1)} collective-permute-done((bf16[64,1408]{1,0:T(8,128)(2,1)S(1)}, bf16[64,1408]{1,0:T(8,128)(2,1)S(1)}, u32[]{:S(2)}, u32[]{:S(2)}) %collective-permute-start.25) | collective-permute-done | bytes 180256 | tf_op jit(solution)/shard_map/ppermute | solution.py:175
  273.1 8.2 %collective-permute-start.32 = (bf16[4,44,256]{2,1,0:T(8,128)(2,1)S(1)}, bf16[4,44,256]{2,1,0:T(8,128)(2,1)S(1)}, u32[]{:S(2)}, u32[]{:S(2)}) collective-permute-start(bf16[4,44,256]{2,1,0:T(8,128)(2,1)S(1)} %dynamic-slice_convert_fusion), channel_id=1, source_target_pairs={{0,64},{64,0},{1,65},{65,1},{2,66},{66,2},{3,67},{67,3},{4,68},{68... | collective-permute-start | bytes 270344 | tf_op jit(solution)/shard_map/ppermute | solution.py:180
  281.4 2.7 collective-permute-done.32
  284.1 4.8 %collective-permute-start.33 = (bf16[2,44,256]{2,1,0:T(8,128)(2,1)S(1)}, bf16[2,44,256]{2,1,0:T(8,128)(2,1)S(1)}, u32[]{:S(2)}, u32[]{:S(2)}) collective-permute-start(bf16[2,44,256]{2,1,0:T(8,128)(2,1)S(1)} %dynamic-slice_convert_fusion.1), channel_id=1, source_target_pairs={{0,32},{16,48},{32,0},{48,16},{1,33},{17,49},{33,1},{49,17},{2,34}... | collective-permute-start | bytes 135176 | tf_op jit(solution)/shard_map/ppermute | solution.py:180
  289.2 1.8 collective-permute-done.33
  291.0 4.1 %collective-permute-start.34 = (bf16[1,44,256]{2,1,0:T(8,128)(2,1)S(1)}, bf16[1,44,256]{2,1,0:T(8,128)(2,1)S(1)}, u32[]{:S(2)}, u32[]{:S(2)}) collective-permute-start(bf16[1,44,256]{2,1,0:T(8,128)(2,1)S(1)} %dynamic-slice_convert_fusion.2), channel_id=1, source_target_pairs={{0,16},{16,0},{32,48},{48,32},{1,17},{17,1},{33,49},{49,33},{2,18}... | collective-permute-start | bytes 67592 | tf_op jit(solution)/shard_map/ppermute | solution.py:180
  295.2 17.1 %all_gather.23 = bf16[256,1408]{1,0:T(8,128)(2,1)S(1)} all-gather(bf16[64,1408]{1,0:T(8,128)(2,1)S(1)} %fusion.9), channel_id=1, replica_groups=mesh['x'=4,'zh'=2,'zl'=4,'tensor'=4,'yh'=2,'core'=2] {'tensor'}, dimensions={0}, use_global_device_ids=true | all-gather | bytes 901120 | tf_op jit(solution)/shard_map/all_gather | solution.py:356
  (91 shorter events, 10.5 us)
Async XLA Ops:
  7.2 2.6 copy-start.11
  7.2 71.7 %all-gather.4.cloned.1.call-start = ((), (), s32[]{:S(2)}) async-start(), calls=%async_computation | async-start | bytes 2211840 | tf_op jit(solution)/shard_map/all_gather | solution.py:194
  8.5 1.6 copy-start.10
  10.0 32.1 %copy-start.14 = (f32[2048]{0:T(1024)S(1)}, f32[2048]{0:T(1024)}, u32[]{:S(2)}) copy-start(f32[2048]{0:T(1024)} %param.16) | copy-start | bytes 24580
  10.2 27.0 %collective-permute-start.16 = (bf16[64,3456]{1,0:T(8,128)(2,1)S(1)}, bf16[64,3456]{1,0:T(8,128)(2,1)S(1)}, u32[]{:S(2)}, u32[]{:S(2)}) collective-permute-start(bf16[64,3456]{1,0:T(8,128)(2,1)S(1)} %constant_dynamic-slice_fusion.3), channel_id=1, source_target_pairs={{0,2},{2,0},{1,3},{3,1},{4,6},{6,4},{5,7},{7,5},{8,10},{10,8},{9,1... | collective-permute-start | bytes 1327112 | tf_op jit(solution)/shard_map/ppermute | solution.py:180
  37.2 0.8 copy-start.12
  38.0 132.3 %all-gather.6.cloned.1.call-start = ((), (), s32[]{:S(2)}) async-start(), calls=%async_computation.1 | async-start | bytes 1310720 | tf_op jit(solution)/shard_map/all_gather | solution.py:262
  38.0 132.3 %collective-permute-start.15 = (bf16[256,3456]{1,0:T(8,128)(2,1)S(1)}, bf16[256,3456]{1,0:T(8,128)(2,1)S(1)}, u32[]{:S(2)}, u32[]{:S(2)}) collective-permute-start(bf16[256,3456]{1,0:T(8,128)(2,1)S(1)} %maximum_maximum_fusion.p0), channel_id=1, source_target_pairs={{0,1},{1,0},{2,3},{3,2},{4,5},{5,4},{6,7},{7,6},{8,9},{9,8},{10,11... | collective-permute-start | bytes 5308424 | tf_op jit(solution)/shard_map/ppermute | solution.py:180
  44.7 78.3 %copy-start.13 = (f32[1408]{0:T(1024)S(1)}, f32[1408]{0:T(1024)}, u32[]{:S(2)}) copy-start(f32[1408]{0:T(1024)} %param.12) | copy-start | bytes 16900
  44.7 17.6 %collective-permute-start.12 = (bf16[2,8,2048]{2,1,0:T(8,128)(2,1)}, bf16[2,8,2048]{2,1,0:T(8,128)(2,1)}, u32[]{:S(2)}, u32[]{:S(2)}) collective-permute-start(bf16[2,8,2048]{2,1,0:T(8,128)(2,1)} %get-tuple-element.54), channel_id=1, source_target_pairs={{0,1},{1,0},{2,3},{3,2},{4,5},{5,4},{6,7},{7,6},{8,9},{9,8},{10,11... | collective-permute-start | bytes 196616 | tf_op jit(solution)/shard_map/ppermute | solution.py:259
  47.2 17.7 %collective-permute-start.13 = (bf16[2,8,2048]{2,1,0:T(8,128)(2,1)}, bf16[2,8,2048]{2,1,0:T(8,128)(2,1)}, u32[]{:S(2)}, u32[]{:S(2)}) collective-permute-start(bf16[2,8,2048]{2,1,0:T(8,128)(2,1)} %get-tuple-element.55), channel_id=1, source_target_pairs={{0,2},{1,3},{2,0},{3,1},{4,6},{5,7},{6,4},{7,5},{8,10},{9,11},{10,... | collective-permute-start | bytes 196616 | tf_op jit(solution)/shard_map/ppermute | solution.py:259
  49.9 22.1 %collective-permute-start.14 = (bf16[2,8,2048]{2,1,0:T(8,128)(2,1)}, bf16[2,8,2048]{2,1,0:T(8,128)(2,1)}, u32[]{:S(2)}, u32[]{:S(2)}) collective-permute-start(bf16[2,8,2048]{2,1,0:T(8,128)(2,1)} %get-tuple-element.56), channel_id=1, source_target_pairs={{0,3},{1,2},{2,1},{3,0},{4,7},{5,6},{6,5},{7,4},{8,11},{9,10},{10,... | collective-permute-start | bytes 196616 | tf_op jit(solution)/shard_map/ppermute | solution.py:259
  56.3 64.7 %collective-permute-start = (bf16[352,1024]{1,0:T(8,128)(2,1)}, bf16[352,1024]{1,0:T(8,128)(2,1)}, u32[]{:S(2)}, u32[]{:S(2)}) collective-permute-start(bf16[352,1024]{1,0:T(8,128)(2,1)} %u0.3), channel_id=1, source_target_pairs={{0,1},{1,0},{2,3},{3,2},{4,5},{5,4},{6,7},{7,6},{8,9},{9,8},{10,11... | collective-permute-start | bytes 2162696 | tf_op jit(solution)/shard_map/ppermute | solution.py:180
  62.2 16.6 %collective-permute-start.1 = (bf16[88,1024]{1,0:T(8,128)(2,1)}, bf16[88,1024]{1,0:T(8,128)(2,1)}, u32[]{:S(2)}, u32[]{:S(2)}) collective-permute-start(bf16[88,1024]{1,0:T(8,128)(2,1)} %constant_dynamic-slice_fusion.4), channel_id=1, source_target_pairs={{0,2},{2,0},{1,3},{3,1},{4,6},{6,4},{5,7},{7,5},{8,10},{10,8},{9,1... | collective-permute-start | bytes 540680 | tf_op jit(solution)/shard_map/ppermute | solution.py:180
  64.9 32.1 %collective-permute-start.4 = (bf16[88,1024]{1,0:T(8,128)(2,1)}, bf16[88,1024]{1,0:T(8,128)(2,1)}, u32[]{:S(2)}, u32[]{:S(2)}) collective-permute-start(bf16[88,1024]{1,0:T(8,128)(2,1)} %dynamic-slice_bitcast_fusion), channel_id=1, source_target_pairs={{0,2},{2,0},{1,3},{3,1},{4,6},{6,4},{5,7},{7,5},{8,10},{10,8},{9,1... | collective-permute-start | bytes 540680 | tf_op jit(solution)/shard_map/ppermute | solution.py:180
  72.0 59.2 %collective-permute-start.3 = (bf16[352,1024]{1,0:T(8,128)(2,1)}, bf16[352,1024]{1,0:T(8,128)(2,1)}, u32[]{:S(2)}, u32[]{:S(2)}) collective-permute-start(bf16[352,1024]{1,0:T(8,128)(2,1)} %bitcast.26), channel_id=1, source_target_pairs={{0,1},{1,0},{2,3},{3,2},{4,5},{5,4},{6,7},{7,6},{8,9},{9,8},{10,11... | collective-permute-start | bytes 2162696 | tf_op jit(solution)/shard_map/ppermute | solution.py:180
  78.9 91.5 %collective-permute-start.17 = (bf16[256,3456]{1,0:T(8,128)(2,1)}, bf16[256,3456]{1,0:T(8,128)(2,1)}, u32[]{:S(2)}, u32[]{:S(2)}) collective-permute-start(bf16[256,3456]{1,0:T(8,128)(2,1)} %all-gather.4.cloned.1.call-done.p2), channel_id=1, source_target_pairs={{0,1},{1,0},{2,3},{3,2},{4,5},{5,4},{6,7},{7,6},{8,9},{9,8},{10,11... | collective-permute-start | bytes 5308424 | tf_op jit(solution)/shard_map/ppermute | solution.py:180
  97.1 26.0 %collective-permute-start.2 = (bf16[352,1024]{1,0:T(8,128)(2,1)}, bf16[352,1024]{1,0:T(8,128)(2,1)}, u32[]{:S(2)}, u32[]{:S(2)}) collective-permute-start(bf16[352,1024]{1,0:T(8,128)(2,1)} %all_gather.18.u2), channel_id=1, source_target_pairs={{0,1},{1,0},{2,3},{3,2},{4,5},{5,4},{6,7},{7,6},{8,9},{9,8},{10,11... | collective-permute-start | bytes 2162696 | tf_op jit(solution)/shard_map/ppermute | solution.py:180
  121.1 10.2 %collective-permute-start.5 = (bf16[352,1024]{1,0:T(8,128)(2,1)}, bf16[352,1024]{1,0:T(8,128)(2,1)}, u32[]{:S(2)}, u32[]{:S(2)}) collective-permute-start(bf16[352,1024]{1,0:T(8,128)(2,1)} %all_gather.19.d2), channel_id=1, source_target_pairs={{0,1},{1,0},{2,3},{3,2},{4,5},{5,4},{6,7},{7,6},{8,9},{9,8},{10,11... | collective-permute-start | bytes 2162696 | tf_op jit(solution)/shard_map/ppermute | solution.py:180
  123.1 1.1 copy-start.3
  124.2 1.1 copy-start.9
  125.3 5.9 %copy-start.1 = (bf16[1024,352]{0,1:T(8,128)(2,1)S(1)}, bf16[1024,352]{0,1:T(8,128)(2,1)}, u32[]{:S(2)}) copy-start(bf16[1024,352]{0,1:T(8,128)(2,1)} %param.14) | copy-start | bytes 2162692
  130.2 1.0 copy-start.7
  131.2 27.2 %copy-start.5 = (bf16[64,1408]{1,0:T(8,128)(2,1)}, bf16[64,1408]{1,0:T(8,128)(2,1)S(1)}, u32[]{:S(2)}) copy-start(bf16[64,1408]{1,0:T(8,128)(2,1)S(1)} %get-tuple-element.23) | copy-start | bytes 540676
  134.7 11.5 %collective-permute-start.6 = (bf16[64,1408]{1,0:T(8,128)(2,1)S(1)}, bf16[64,1408]{1,0:T(8,128)(2,1)S(1)}, u32[]{:S(2)}, u32[]{:S(2)}) collective-permute-start(bf16[64,1408]{1,0:T(8,128)(2,1)S(1)} %get-tuple-element.26), channel_id=1, source_target_pairs={{0,4},{4,8},{8,12},{12,0},{1,5},{5,9},{9,13},{13,1},{2,6},{6,10},{... | collective-permute-start | bytes 540680 | tf_op jit(solution)/shard_map/ppermute | solution.py:175
  140.3 17.2 %collective-permute-start.7 = (bf16[64,1408]{1,0:T(8,128)(2,1)S(1)}, bf16[64,1408]{1,0:T(8,128)(2,1)S(1)}, u32[]{:S(2)}, u32[]{:S(2)}) collective-permute-start(bf16[64,1408]{1,0:T(8,128)(2,1)S(1)} %get-tuple-element.27), channel_id=1, source_target_pairs={{0,8},{4,12},{8,0},{12,4},{1,9},{5,13},{9,1},{13,5},{2,10},{6,14},... | collective-permute-start | bytes 540680 | tf_op jit(solution)/shard_map/ppermute | solution.py:175
  142.5 15.0 %collective-permute-start.8 = (bf16[64,1408]{1,0:T(8,128)(2,1)S(1)}, bf16[64,1408]{1,0:T(8,128)(2,1)S(1)}, u32[]{:S(2)}, u32[]{:S(2)}) collective-permute-start(bf16[64,1408]{1,0:T(8,128)(2,1)S(1)} %get-tuple-element.28), channel_id=1, source_target_pairs={{0,12},{4,0},{8,4},{12,8},{1,13},{5,1},{9,5},{13,9},{2,14},{6,2},{... | collective-permute-start | bytes 540680 | tf_op jit(solution)/shard_map/ppermute | solution.py:175
  158.4 17.3 %collective-permute-start.10 = (bf16[64,1408]{1,0:T(8,128)(2,1)}, bf16[64,1408]{1,0:T(8,128)(2,1)}, u32[]{:S(2)}, u32[]{:S(2)}) collective-permute-start(bf16[64,1408]{1,0:T(8,128)(2,1)} %get-tuple-element.57.e0), channel_id=1, source_target_pairs={{0,8},{4,12},{8,0},{12,4},{1,9},{5,13},{9,1},{13,5},{2,10},{6,14},... | collective-permute-start | bytes 540680 | tf_op jit(solution)/shard_map/ppermute | solution.py:175
  162.6 13.1 %collective-permute-start.11 = (bf16[64,1408]{1,0:T(8,128)(2,1)}, bf16[64,1408]{1,0:T(8,128)(2,1)}, u32[]{:S(2)}, u32[]{:S(2)}) collective-permute-start(bf16[64,1408]{1,0:T(8,128)(2,1)} %get-tuple-element.57.e0), channel_id=1, source_target_pairs={{0,12},{4,0},{8,4},{12,8},{1,13},{5,1},{9,5},{13,9},{2,14},{6,2},{... | collective-permute-start | bytes 540680 | tf_op jit(solution)/shard_map/ppermute | solution.py:175
  164.6 14.7 %collective-permute-start.9 = (bf16[64,1408]{1,0:T(8,128)(2,1)}, bf16[64,1408]{1,0:T(8,128)(2,1)}, u32[]{:S(2)}, u32[]{:S(2)}) collective-permute-start(bf16[64,1408]{1,0:T(8,128)(2,1)} %get-tuple-element.57.e0), channel_id=1, source_target_pairs={{0,4},{4,8},{8,12},{12,0},{1,5},{5,9},{9,13},{13,1},{2,6},{6,10},{... | collective-permute-start | bytes 540680 | tf_op jit(solution)/shard_map/ppermute | solution.py:175
  170.3 4.2 %copy-start = (bf16[256,3456]{1,0:T(8,128)(2,1)}, bf16[256,3456]{1,0:T(8,128)(2,1)S(1)}, u32[]{:S(2)}) copy-start(bf16[256,3456]{1,0:T(8,128)(2,1)S(1)} %collective-permute-done.15.p1) | copy-start | bytes 5308420
  170.3 1.9 copy-start.8
  187.3 24.6 %collective-permute-start.27 = (bf16[1408,512]{1,0:T(8,128)(2,1)}, bf16[1408,512]{1,0:T(8,128)(2,1)}, u32[]{:S(2)}, u32[]{:S(2)}) collective-permute-start(bf16[1408,512]{1,0:T(8,128)(2,1)} %convolution_convert_fusion), channel_id=1, source_target_pairs={{0,1},{1,0},{2,3},{3,2},{4,5},{5,4},{6,7},{7,6},{8,9},{9,8},{10,11... | collective-permute-start | bytes 4325384 | tf_op jit(solution)/shard_map/ppermute | solution.py:180
  189.2 9.1 %collective-permute-start.18 = (bf16[64,1408]{1,0:T(8,128)(2,1)S(1)}, bf16[64,1408]{1,0:T(8,128)(2,1)S(1)}, u32[]{:S(2)}, u32[]{:S(2)}) collective-permute-start(bf16[64,1408]{1,0:T(8,128)(2,1)S(1)} %get-tuple-element.32), channel_id=1, source_target_pairs={{0,4},{4,8},{8,12},{12,0},{1,5},{5,9},{9,13},{13,1},{2,6},{6,10},{... | collective-permute-start | bytes 540680 | tf_op jit(solution)/shard_map/ppermute | solution.py:175
  191.1 18.5 %collective-permute-start.19 = (bf16[64,1408]{1,0:T(8,128)(2,1)S(1)}, bf16[64,1408]{1,0:T(8,128)(2,1)S(1)}, u32[]{:S(2)}, u32[]{:S(2)}) collective-permute-start(bf16[64,1408]{1,0:T(8,128)(2,1)S(1)} %get-tuple-element.33), channel_id=1, source_target_pairs={{0,8},{4,12},{8,0},{12,4},{1,9},{5,13},{9,1},{13,5},{2,10},{6,14},... | collective-permute-start | bytes 540680 | tf_op jit(solution)/shard_map/ppermute | solution.py:175
  195.1 14.6 %collective-permute-start.20 = (bf16[64,1408]{1,0:T(8,128)(2,1)S(1)}, bf16[64,1408]{1,0:T(8,128)(2,1)S(1)}, u32[]{:S(2)}, u32[]{:S(2)}) collective-permute-start(bf16[64,1408]{1,0:T(8,128)(2,1)S(1)} %get-tuple-element.34), channel_id=1, source_target_pairs={{0,12},{4,0},{8,4},{12,8},{1,13},{5,1},{9,5},{13,9},{2,14},{6,2},{... | collective-permute-start | bytes 540680 | tf_op jit(solution)/shard_map/ppermute | solution.py:175
  209.8 17.5 %collective-permute-start.21 = (bf16[64,1408]{1,0:T(8,128)(2,1)S(1)}, bf16[64,1408]{1,0:T(8,128)(2,1)S(1)}, u32[]{:S(2)}, u32[]{:S(2)}) collective-permute-start(bf16[64,1408]{1,0:T(8,128)(2,1)S(1)} %add_convert_fusion.g0), channel_id=1, source_target_pairs={{0,4},{4,8},{8,12},{12,0},{1,5},{5,9},{9,13},{13,1},{2,6},{6,10},{... | collective-permute-start | bytes 540680 | tf_op jit(solution)/shard_map/ppermute | solution.py:175
  213.8 10.1 %copy-start.6 = (bf16[64,1408]{1,0:T(8,128)(2,1)S(1)}, bf16[64,1408]{1,0:T(8,128)(2,1)}, u32[]{:S(2)}) copy-start(bf16[64,1408]{1,0:T(8,128)(2,1)} %copy-done.5) | copy-start | bytes 540676
  213.8 26.2 %copy-start.2 = (bf16[1024,352]{0,1:T(8,128)(2,1)S(1)}, bf16[1024,352]{0,1:T(8,128)(2,1)}, u32[]{:S(2)}) copy-start(bf16[1024,352]{0,1:T(8,128)(2,1)} %param.14) | copy-start | bytes 2162692
  213.8 26.2 %copy-start.4 = (bf16[352,1024]{1,0:T(8,128)(2,1)S(1)}, bf16[352,1024]{1,0:T(8,128)(2,1)}, u32[]{:S(2)}) copy-start(bf16[352,1024]{1,0:T(8,128)(2,1)} %u0.3) | copy-start | bytes 2162692
  213.9 36.6 %collective-permute-start.28 = (bf16[352,512]{1,0:T(8,128)(2,1)S(1)}, bf16[352,512]{1,0:T(8,128)(2,1)S(1)}, u32[]{:S(2)}, u32[]{:S(2)}) collective-permute-start(bf16[352,512]{1,0:T(8,128)(2,1)S(1)} %get-tuple-element.46), channel_id=1, source_target_pairs={{0,128},{128,256},{256,384},{384,0},{1,129},{129,257},{257,385},{3... | collective-permute-start | bytes 1081352 | tf_op jit(solution)/shard_map/ppermute | solution.py:175
  216.0 38.5 %collective-permute-start.29 = (bf16[352,512]{1,0:T(8,128)(2,1)S(1)}, bf16[352,512]{1,0:T(8,128)(2,1)S(1)}, u32[]{:S(2)}, u32[]{:S(2)}) collective-permute-start(bf16[352,512]{1,0:T(8,128)(2,1)S(1)} %get-tuple-element.48), channel_id=1, source_target_pairs={{0,256},{128,384},{256,0},{384,128},{1,257},{129,385},{257,1},{385... | collective-permute-start | bytes 1081352 | tf_op jit(solution)/shard_map/ppermute | solution.py:175
  220.5 34.1 %collective-permute-start.30 = (bf16[352,512]{1,0:T(8,128)(2,1)S(1)}, bf16[352,512]{1,0:T(8,128)(2,1)S(1)}, u32[]{:S(2)}, u32[]{:S(2)}) collective-permute-start(bf16[352,512]{1,0:T(8,128)(2,1)S(1)} %get-tuple-element.47), channel_id=1, source_target_pairs={{0,384},{128,0},{256,128},{384,256},{1,385},{129,1},{257,129},{385... | collective-permute-start | bytes 1081352 | tf_op jit(solution)/shard_map/ppermute | solution.py:175
  224.2 15.8 %collective-permute-start.22 = (bf16[64,1408]{1,0:T(8,128)(2,1)S(1)}, bf16[64,1408]{1,0:T(8,128)(2,1)S(1)}, u32[]{:S(2)}, u32[]{:S(2)}) collective-permute-start(bf16[64,1408]{1,0:T(8,128)(2,1)S(1)} %add_convert_fusion.g0), channel_id=1, source_target_pairs={{0,8},{4,12},{8,0},{12,4},{1,9},{5,13},{9,1},{13,5},{2,10},{6,14},... | collective-permute-start | bytes 540680 | tf_op jit(solution)/shard_map/ppermute | solution.py:175
  227.3 12.7 %collective-permute-start.23 = (bf16[64,1408]{1,0:T(8,128)(2,1)S(1)}, bf16[64,1408]{1,0:T(8,128)(2,1)S(1)}, u32[]{:S(2)}, u32[]{:S(2)}) collective-permute-start(bf16[64,1408]{1,0:T(8,128)(2,1)S(1)} %add_convert_fusion.g0), channel_id=1, source_target_pairs={{0,12},{4,0},{8,4},{12,8},{1,13},{5,1},{9,5},{13,9},{2,14},{6,2},{... | collective-permute-start | bytes 540680 | tf_op jit(solution)/shard_map/ppermute | solution.py:175
  245.2 11.5 %collective-permute-start.24 = (bf16[64,1408]{1,0:T(8,128)(2,1)S(1)}, bf16[64,1408]{1,0:T(8,128)(2,1)S(1)}, u32[]{:S(2)}, u32[]{:S(2)}) collective-permute-start(bf16[64,1408]{1,0:T(8,128)(2,1)S(1)} %get-tuple-element.37), channel_id=1, source_target_pairs={{0,4},{4,8},{8,12},{12,0},{1,5},{5,9},{9,13},{13,1},{2,6},{6,10},{... | collective-permute-start | bytes 540680 | tf_op jit(solution)/shard_map/ppermute | solution.py:175
  248.0 24.8 %collective-permute-start.25 = (bf16[64,1408]{1,0:T(8,128)(2,1)S(1)}, bf16[64,1408]{1,0:T(8,128)(2,1)S(1)}, u32[]{:S(2)}, u32[]{:S(2)}) collective-permute-start(bf16[64,1408]{1,0:T(8,128)(2,1)S(1)} %get-tuple-element.38), channel_id=1, source_target_pairs={{0,8},{4,12},{8,0},{12,4},{1,9},{5,13},{9,1},{13,5},{2,10},{6,14},... | collective-permute-start | bytes 540680 | tf_op jit(solution)/shard_map/ppermute | solution.py:175
  250.6 22.1 %collective-permute-start.26 = (bf16[64,1408]{1,0:T(8,128)(2,1)S(1)}, bf16[64,1408]{1,0:T(8,128)(2,1)S(1)}, u32[]{:S(2)}, u32[]{:S(2)}) collective-permute-start(bf16[64,1408]{1,0:T(8,128)(2,1)S(1)} %get-tuple-element.39), channel_id=1, source_target_pairs={{0,12},{4,0},{8,4},{12,8},{1,13},{5,1},{9,5},{13,9},{2,14},{6,2},{... | collective-permute-start | bytes 540680 | tf_op jit(solution)/shard_map/ppermute | solution.py:175
  254.8 18.2 %collective-permute-start.31 = (bf16[352,256]{1,0:T(8,128)(2,1)S(1)}, bf16[352,256]{1,0:T(8,128)(2,1)S(1)}, u32[]{:S(2)}, u32[]{:S(2)}) collective-permute-start(bf16[352,256]{1,0:T(8,128)(2,1)S(1)} %slice.39), channel_id=1, source_target_pairs={{0,2},{2,0},{1,3},{3,1},{4,6},{6,4},{5,7},{7,5},{8,10},{10,8},{9,1... | collective-permute-start | bytes 540680 | tf_op jit(solution)/shard_map/ppermute | solution.py:180
  273.1 10.9 %collective-permute-start.32 = (bf16[4,44,256]{2,1,0:T(8,128)(2,1)S(1)}, bf16[4,44,256]{2,1,0:T(8,128)(2,1)S(1)}, u32[]{:S(2)}, u32[]{:S(2)}) collective-permute-start(bf16[4,44,256]{2,1,0:T(8,128)(2,1)S(1)} %dynamic-slice_convert_fusion), channel_id=1, source_target_pairs={{0,64},{64,0},{1,65},{65,1},{2,66},{66,2},{3,67},{67,3},{4,68},{68... | collective-permute-start | bytes 270344 | tf_op jit(solution)/shard_map/ppermute | solution.py:180
  284.1 6.9 %collective-permute-start.33 = (bf16[2,44,256]{2,1,0:T(8,128)(2,1)S(1)}, bf16[2,44,256]{2,1,0:T(8,128)(2,1)S(1)}, u32[]{:S(2)}, u32[]{:S(2)}) collective-permute-start(bf16[2,44,256]{2,1,0:T(8,128)(2,1)S(1)} %dynamic-slice_convert_fusion.1), channel_id=1, source_target_pairs={{0,32},{16,48},{32,0},{48,16},{1,33},{17,49},{33,1},{49,17},{2,34}... | collective-permute-start | bytes 135176 | tf_op jit(solution)/shard_map/ppermute | solution.py:180
  291.0 21.3 %collective-permute-start.34 = (bf16[1,44,256]{2,1,0:T(8,128)(2,1)S(1)}, bf16[1,44,256]{2,1,0:T(8,128)(2,1)S(1)}, u32[]{:S(2)}, u32[]{:S(2)}) collective-permute-start(bf16[1,44,256]{2,1,0:T(8,128)(2,1)S(1)} %dynamic-slice_convert_fusion.2), channel_id=1, source_target_pairs={{0,16},{16,0},{32,48},{48,32},{1,17},{17,1},{33,49},{49,33},{2,18}... | collective-permute-start | bytes 67592 | tf_op jit(solution)/shard_map/ppermute | solution.py:180
Sparse Core Ops, SparseCore 0:
  38.1 37.7 all-gather.3
  78.0 38.6 all-gather.5

commit v3 on v2

--- a/solution.py
+++ b/solution.py
@@ -12,6 +12,7 @@
 BF = jnp.bfloat16
 F32 = jnp.float32
 PARTS = 4
+COPIES = 2 + 2 * PARTS
 PARAMS = pltpu.CompilerParams(vmem_limit_bytes=48 * 1024 * 1024)
 VMEM = pl.BlockSpec(memory_space=pltpu.VMEM)
 ANY = pl.BlockSpec(memory_space=pl.ANY)
@@ -45,18 +46,34 @@
     return lax.dot_general(a, b, LAST, preferred_element_type=F32)
 
 
-def block_copies(place, blocks, whole, sems):
-    rows = blocks[0].shape[0]
+def block_copies(place, first, blocks, whole, sems):
+    rows, cols = blocks[0].shape[0] // 2, blocks[0].shape[1]
     group = place[0]
     copies = []
     for bits, block in enumerate(blocks):
-        start = pl.multiple_of((group ^ bits) * rows, 16)
-        copies.append(pltpu.make_async_copy(block, whole.at[pl.ds(start, rows)], sems.at[bits]))
+        source = block.at[pl.ds(first * rows, rows)]
+        place_rows = pl.ds(pl.multiple_of((group ^ bits) * rows, 16), rows)
+        if bits < 2:
+            copies.append(pltpu.make_async_copy(source, whole.at[place_rows], sems.at[bits]))
+            continue
+        quarter = cols // PARTS
+        for k in range(PARTS):
+            start = pl.multiple_of(lax.rem(place[2] + k, PARTS) * quarter, 256)
+            copies.append(
+                pltpu.make_async_copy(
+                    block.at[pl.ds(first * rows, rows), pl.ds(k * quarter, quarter)],
+                    whole.at[place_rows, pl.ds(start, quarter)],
+                    sems.at[PARTS * bits + k - 6],
+                )
+            )
     return copies
 
 
-def up_kernel(place, image, gain, u0, u1, u2, u3, act, slope, in_rows, up, rows4, sems, row_sems):
-    copies = block_copies(place, (u0, u1, u2, u3), up, sems)
+def up_kernel(
+    place, image, gain, w0, w1, w2, w3, act, slope, in_rows, up, rows4, sems, row_sems
+):
+    weights = (w0, w1, w2, w3)
+    copies = block_copies(place, 0, weights, up, sems)
     rows = in_rows.shape[0]
     moves = []
     for k in range(PARTS):
@@ -81,8 +98,9 @@
         slope[:, cols] = grad
 
 
-def down_kernel(place, act, d0, d1, d2, d3, o0, o1, o2, o3, down, sems):
-    copies = block_copies(place, (d0, d1, d2, d3), down, sems)
+def down_kernel(place, act, w0, w1, w2, w3, o0, o1, o2, o3, down, sems):
+    weights = (w0, w1, w2, w3)
+    copies = block_copies(place, 1, weights, down, sems)
     for copy in copies:
         copy.start()
     for copy in copies:
@@ -96,8 +114,9 @@
         out[...] = value[k * rows : (k + 1) * rows]
 
 
-def query_kernel(caption, p0, p1, p2, p3, query, d_attn, w, sems):
-    dec = caption.shape[-1]
+def query_kernel(c0, c1, c2, c3, p0, p1, p2, p3, query, d_attn, w, sems):
+    captions = (c0, c1, c2, c3)
+    dec = c0.shape[-1]
     skip = p0.shape[1] - dec
     copies = [
         pltpu.make_async_copy(p.at[:, pl.ds(skip, dec)], w.at[k], sems.at[k])
@@ -105,8 +124,8 @@
     ]
     for copy in copies:
         copy.start()
-    text = caption[:, 0].reshape(-1, dec)
-    cot = caption[:, 1].reshape(-1, dec)
+    text = jnp.concatenate([c[0] for c in captions], axis=0)
+    cot = jnp.concatenate([c[1] for c in captions], axis=0)
     for k, copy in enumerate(copies):
         copy.wait()
         query[k] = (dot_last(text, w[k, :HEAD_DIM]) * HEAD_DIM ** (-0.5)).astype(BF)
@@ -150,11 +169,12 @@
 
 
 def back_kernel(
-    place, g0, g1, g2, g3, slope, d0, d1, d2, d3, u0, u1, u2, u3,
+    place, g0, g1, g2, g3, slope, w0, w1, w2, w3,
     o0, o1, o2, o3, down, up, grads, d_pre, down_sems, up_sems,
 ):
-    first = block_copies(place, (d0, d1, d2, d3), down, down_sems)
-    second = block_copies(place, (u0, u1, u2, u3), up, up_sems)
+    weights = (w0, w1, w2, w3)
+    first = block_copies(place, 1, weights, down, down_sems)
+    second = block_copies(place, 0, weights, up, up_sems)
     for copy in first + second:
         copy.start()
     rows = g0.shape[0]
@@ -188,44 +208,24 @@
     return lax.optimization_barrier((value,) + others)[0]
 
 
-def far_block(own, axis):
-    quarter = own.shape[0] // PARTS
-    piece = swap(rows_at(own, lax.axis_index(axis) * quarter, quarter), "yh")
-    return lax.all_gather(piece, axis, axis=0, tiled=True)
-
-
-def group_blocks(own, axis):
-    far = far_block(own, axis)
-    return own, swap(own, "core"), far, swap(far, "core")
-
-
-def sum_blocks(blocks):
+def quarter_of(value, which, dim):
+    quarter = value.shape[dim] // PARTS
+    return lax.dynamic_slice_in_dim(value, which * quarter, quarter, axis=dim)
+
+
+def send_blocks(blocks):
+    return [blocks[0]] + [shift(blocks[PARTS - by], "tensor", by) for by in range(1, PARTS)]
+
+
+def add_blocks(blocks):
     total = blocks[0].astype(F32)
-    for by in range(1, PARTS):
-        total = total + shift(blocks[PARTS - by], "tensor", by).astype(F32)
+    for block in blocks[1:]:
+        total = total + block.astype(F32)
     return total
 
 
 def gather_blocks(block):
     return [block] + [shift(block, "tensor", by) for by in range(1, PARTS)]
-
-
-def scatter_sum(partial, axis):
-    size = lax.axis_size(axis)
-    rows = partial.shape[0] // size
-    here = lax.axis_index(axis)
-    total = rows_at(partial, here * rows, rows).astype(F32)
-    for by in range(1, size):
-        block = rows_at(partial, lax.rem(here + by, size) * rows, rows)
-        total = total + shift(block, axis, by).astype(F32)
-    return total
-
-
-def halved(partial, axis, bit):
-    half = partial.shape[0] // 2
-    side = (lax.axis_index(axis) // bit) % 2
-    sent = rows_at(partial, (1 - side) * half, half).astype(BF)
-    return rows_at(partial, side * half, half) + swap(sent, axis, bit).astype(F32)
 
 
 def local(
@@ -234,7 +234,6 @@
     _, patches, width = image_in.shape
     group = lax.axis_index("yh") * 2 + lax.axis_index("core")
     tensor = lax.axis_index("tensor")
-    place = jnp.stack([group, tensor]).astype(jnp.int32)
     flat_in = image_in.reshape(patches, width)
     rows = patches // PARTS
     hidden = enc_up.shape[1]
@@ -244,22 +243,30 @@
     gain = enc_gain.reshape(1, width)
     dma = pltpu.SemaphoreType.DMA
 
-    up = group_blocks(enc_up, "x")
-    down = group_blocks(enc_down.T, "zl")
+    which = lax.rem(lax.axis_index("x") + lax.axis_index("zl"), PARTS)
+    piece = jnp.concatenate(
+        [quarter_of(enc_up, which, 1), quarter_of(enc_down, which, 0).T], axis=0
+    )
+    place = jnp.stack([group, tensor, which]).astype(jnp.int32)
+    piece = swap(piece, "yh")
+    pieces = [piece, shift(piece, "x", -1), shift(piece, "x", 2), shift(piece, ("zh", "zl"), 1)]
+    far = jnp.concatenate(pieces, axis=1)
+    own = jnp.concatenate([enc_up, enc_down.T], axis=0)
+    weights = (own, swap(own, "core"), far, swap(far, "core"))
     pair_own = jnp.concatenate([w_key, w_value], axis=1).T
     text_own = jnp.concatenate([w_query.T, w_out], axis=0)
-    heads = group_blocks(jnp.concatenate([pair_own, text_own], axis=1), "x")
+    heads_own = jnp.concatenate([pair_own, text_own], axis=1)
+
+    heads_piece = swap(quarter_of(after(heads_own, piece), lax.axis_index("x"), 0), "yh")
+    heads_near = swap(after(heads_own, far), "core")
 
     text_normed = layer_norm(text_in, query_gain)[0].astype(BF)
-    both = jnp.stack([text_normed, cotangent], axis=1)
-    group_rows = []
-    for other in range(4):
-        block = lax.dynamic_index_in_dim(both, group ^ other, axis=0, keepdims=False)
-        if other:
-            block = lax.ppermute(block, ("yh", "core"), [(i, i ^ other) for i in range(4)])
-        group_rows.append(block)
-    caption = jnp.concatenate(group_rows, axis=1)
-    caption = lax.all_gather(caption, "tensor", axis=0)
+    both = after(jnp.stack([text_normed, cotangent], axis=1), far)
+    both = both.reshape((2, 2) + both.shape[1:])
+    core, yh = lax.axis_index("core"), lax.axis_index("yh")
+    pick = functools.partial(lax.dynamic_index_in_dim, keepdims=False)
+    near = jnp.concatenate([pick(both, core, 1), swap(pick(both, 1 - core, 1), "core")], axis=2)
+    caption = jnp.concatenate([pick(near, yh, 0), swap(pick(near, 1 - yh, 0), "yh")], axis=1)
 
     act, slope, in_rows = pl.pallas_call(
         up_kernel,
@@ -270,33 +277,39 @@
         scratch_shapes=[
             pltpu.VMEM((width, hidden), BF),
             pltpu.VMEM((patches, width), BF),
-            dma((4,)),
+            dma((COPIES,)),
             dma((PARTS,)),
         ],
         compiler_params=PARAMS,
-    )(place, flat_in, gain, *up)
+    )(place, flat_in, gain, *weights)
     branch = pl.pallas_call(
         down_kernel,
         name="encoder_down",
         out_shape=row_outs,
         in_specs=[SMEM, VMEM] + [ANY] * 4,
         out_specs=[VMEM] * PARTS,
-        scratch_shapes=[pltpu.VMEM((width, hidden), BF), dma((4,))],
-        compiler_params=PARAMS,
-    )(place, act, *down)
-    encoded_rows = (in_rows.astype(F32) + sum_blocks(branch)).astype(BF)
+        scratch_shapes=[pltpu.VMEM((width, hidden), BF), dma((COPIES,))],
+        compiler_params=PARAMS,
+    )(place, act, *weights)
+    captions = gather_blocks(caption)
+    *branch, c0, c1, c2, c3 = lax.optimization_barrier((*branch, *captions))
+    captions = (c0, c1, c2, c3)
+    encoded_rows = (in_rows.astype(F32) + add_blocks(send_blocks(branch))).astype(BF)
     encoded_blocks = gather_blocks(encoded_rows)
 
-    head_shape = shape((4, PARTS * caption.shape[2], HEAD_DIM), BF)
+    heads_far = lax.all_gather(after(heads_piece, far), "x", axis=0, tiled=True)
+    heads = (heads_own, heads_near, heads_far, swap(after(heads_far, encoded_rows), "core"))
+
+    head_shape = shape((4, PARTS * caption.shape[1], HEAD_DIM), BF)
     query, d_attn = pl.pallas_call(
         query_kernel,
         name="query",
         out_shape=[head_shape, head_shape],
-        in_specs=[VMEM] + [ANY] * 4,
+        in_specs=[VMEM] * PARTS + [ANY] * 4,
         out_specs=[VMEM] * 2,
         scratch_shapes=[pltpu.VMEM((4, 2 * HEAD_DIM, dec), BF), dma((4,))],
         compiler_params=PARAMS,
-    )(caption, *heads)
+    )(*captions, *heads)
     *term, encoded, d_pair = pl.pallas_call(
         attention_kernel,
         name="attention",
@@ -306,7 +319,8 @@
         scratch_shapes=[pltpu.VMEM((4, 2 * HEAD_DIM, width), BF), dma((4,))],
         compiler_params=PARAMS,
     )(*encoded_blocks, query, d_attn, *heads)
-    grad_rows = sum_blocks(term).astype(BF)
+    term_blocks = send_blocks(term)
+    grad_rows = add_blocks(term_blocks).astype(BF)
     grad_blocks = gather_blocks(grad_rows)
 
     pair_cols = 2 * HEAD_DIM
@@ -319,32 +333,29 @@
         encoded, jnp.concatenate([cols[0], cols[2]], axis=1), contract, preferred_element_type=F32
     )
     sums = (keep + swap(give, "core").astype(F32)).astype(BF)
-    sums = scatter_sum(after(sums, grad_rows), "x")
-    sums = sums[:, :pair_cols] + swap(sums[:, pair_cols:].astype(BF), "yh").astype(F32)
-    sums = sums.reshape(8, -1, pair_cols)
-    sums = halved(sums, "zh", 1)
-    for bit in (2, 1):
-        sums = halved(sums, "zl", bit)
-    sums = sums[0]
-    key_grad, value_grad = sums[:, :HEAD_DIM], sums[:, HEAD_DIM:]
+    sums = lax.psum_scatter(sums, "x", scatter_dimension=0, tiled=True)
+    sums = sums[:, :pair_cols].astype(F32) + swap(sums[:, pair_cols:], "yh").astype(F32)
 
     d_norm = pl.pallas_call(
         back_kernel,
         name="encoder_back",
         out_shape=row_outs,
-        in_specs=[SMEM] + [VMEM] * 5 + [ANY] * 8,
+        in_specs=[SMEM] + [VMEM] * 5 + [ANY] * 4,
         out_specs=[VMEM] * PARTS,
         scratch_shapes=[
             pltpu.VMEM((width, hidden), BF),
             pltpu.VMEM((width, hidden), BF),
             pltpu.VMEM((patches, width), BF),
             pltpu.VMEM((patches, hidden), BF),
-            dma((4,)),
-            dma((4,)),
+            dma((COPIES,)),
+            dma((COPIES,)),
         ],
         compiler_params=PARAMS,
-    )(place, *grad_blocks, slope, *down, *up)
-    d_normed = sum_blocks(d_norm)
+    )(place, *grad_blocks, slope, *weights)
+    *d_norm, sums = lax.optimization_barrier((*d_norm, sums))
+    sums = sums.astype(BF).reshape(8, -1, pair_cols)
+    sums = lax.all_to_all(sums, ("zh", "zl"), 0, 0, tiled=True)
+    d_normed = add_blocks(send_blocks(d_norm))
     _, normal, inverse = layer_norm(in_rows, enc_gain)
     scaled_grad = d_normed * enc_gain
     d_input = inverse * (
@@ -353,6 +364,9 @@
         - normal * jnp.mean(scaled_grad * normal, axis=-1, keepdims=True)
     )
     image_rows = (grad_rows.astype(F32) + d_input).astype(BF)
+    image_rows, sums = lax.optimization_barrier((image_rows, sums))
+    sums = jnp.sum(sums.astype(F32), axis=0)
+    key_grad, value_grad = sums[:, :HEAD_DIM], sums[:, HEAD_DIM:]
     image_grad = lax.all_gather(image_rows, "tensor", axis=0, tiled=True).reshape(1, patches, width)
     return (image_grad, key_grad, value_grad)
 

time: 322 us -> 282 us (0.88)
  blocking collectives: 55.5 us -> 17.5 us
  starting transfers between devices: 119 us -> 110 us
  local copies, waits for them, and re-layouts: 13.6 us -> 18.9 us
  waiting for transfers between devices: 83.6 us -> 88.7 us
    all_gather x2 -> x0, blocking collectives: 38.4 us -> none  [far_block(): return lax.all_gather(piece, axis, axis=0, tiled=True)]
    ppermute x14 -> x10, starting transfers between devices: 47.8 us -> 29.2 us  [swap(): return lax.ppermute(value, axis, [(i, i ^ bit) for i in range(size)])]
    all_to_all x0 -> x1, starting transfers between devices: none -> 12.3 us  [local(): sums = lax.all_to_all(sums, ('zh', 'zl'), 0, 0, tiled=True)]
    ppermute x3 -> x0, starting transfers between devices: 11.6 us -> none  [local(): lax.ppermute(block, ('yh', 'core'), [(i, i ^ other) for i in range(4)])]
    all_to_all x0 -> x1, waiting for transfers between devices: none -> 9.29 us  [local(): sums = lax.all_to_all(sums, ('zh', 'zl'), 0, 0, tiled=True)]
    ppermute x18 -> x21, starting transfers between devices: 59.4 us -> 68 us  [shift(): lax.ppermute(value, axis, [(i, (i + by) % size) for i in range(size)])]
    ppermute x18 -> x21, waiting for transfers between devices: 53.5 us -> 49 us  [shift(): lax.ppermute(value, axis, [(i, (i + by) % size) for i in range(size)])]
    unnamed x34 -> x55, local copies, waits for them, and re-layouts: 9.43 us -> 13.8 us
  transfers between devices with their start and end apart: 37 -> 34, of which waited for: 11 -> 14; matrix products, arithmetic and copies ran while one was open for 4% -> 5% of each run, Pallas kernels for 5% -> 6%
where the time goes in v3:
time: 282 us; the launch traced here: 280 us
  starting transfers between devices  110 us (39%)
  waiting for transfers between devices  88.7 us (31%)
  Pallas kernels  22.6 us (8%)
  local copies, waits for them, and re-layouts  18.9 us (7%)
  blocking collectives  17.5 us (6%)
  between operations  14.8 us (5%)
  other arithmetic  6.07 us (2%)
    ppermute x21, starting transfers between devices, shift(): lax.ppermute(value, axis, [(i, (i + by) % size) for i in range(size)])  68 us
    ppermute x21, waiting for transfers between devices, shift(): lax.ppermute(value, axis, [(i, (i + by) % size) for i in range(size)])  49 us
    ppermute x10, starting transfers between devices, swap(): return lax.ppermute(value, axis, [(i, i ^ bit) for i in range(size)])  29.2 us
    ppermute x10, waiting for transfers between devices, swap(): return lax.ppermute(value, axis, [(i, i ^ bit) for i in range(size)])  27.5 us
    all_gather x1, blocking collectives, local(): lax.all_gather(image_rows, 'tensor', axis=0, tiled=True)  17.5 us
    unnamed x55, local copies, waits for them, and re-layouts  13.8 us
    all_to_all x1, starting transfers between devices, local(): sums = lax.all_to_all(sums, ('zh', 'zl'), 0, 0, tiled=True)  12.3 us
    all_to_all x1, waiting for transfers between devices, local(): sums = lax.all_to_all(sums, ('zh', 'zl'), 0, 0, tiled=True)  9.29 us
  transfers between devices with their start and end apart: 34, of which 14 were waited for; matrix products, arithmetic and copies ran while one was open for 5% of the time, Pallas kernels for 6%

profile of v3, /device:TPU:56, one launch (start us, length us, event | category | flops | bytes accessed | tf_op | source)
XLA Modules:
  0.0 280.4 jit_solution(6115150396023770591)
XLA Ops:
  7.2 1.0 constant_dynamic-slice_fusion.3
  8.3 0.9 dynamic-slice_bitcast_fusion
  10.0 4.7 %collective-permute-start.1 = (bf16[704,256]{1,0:T(8,128)(2,1)}, bf16[704,256]{1,0:T(8,128)(2,1)}, u32[]{:S(2)}, u32[]{:S(2)}) collective-permute-start(bf16[704,256]{1,0:T(8,128)(2,1)} %pad_maximum_fusion.1), channel_id=1, source_target_pairs={{0,2},{2,0},{1,3},{3,1},{4,6},{6,4},{5,7},{7,5},{8,10},{10,8},{9,1... | collective-permute-start | bytes 1081352 | tf_op jit(solution)/shard_map/ppermute | solution.py:200
  14.9 2.1 collective-permute-start
  16.9 1.2 copy.21
  18.1 1.2 copy.22
  19.3 1.0 copy.23
  20.4 1.0 copy-done.15
  21.4 1.2 maximum_maximum_fusion.p0
  22.7 10.5 %collective-permute-done.1 = bf16[704,256]{1,0:T(8,128)(2,1)} collective-permute-done((bf16[704,256]{1,0:T(8,128)(2,1)}, bf16[704,256]{1,0:T(8,128)(2,1)}, u32[]{:S(2)}, u32[]{:S(2)}) %collective-permute-start.1) | collective-permute-done | bytes 360480 | tf_op jit(solution)/shard_map/ppermute | solution.py:200
  33.2 4.7 %collective-permute-start.2 = (bf16[704,256]{1,0:T(8,128)(2,1)}, bf16[704,256]{1,0:T(8,128)(2,1)S(1)}, u32[]{:S(2)}, u32[]{:S(2)}) collective-permute-start(bf16[704,256]{1,0:T(8,128)(2,1)} %collective-permute-done.1), channel_id=1, source_target_pairs={{0,384},{128,0},{256,128},{384,256},{1,385},{129,1},{257,129},{385... | collective-permute-start | bytes 1081352 | tf_op jit(solution)/shard_map/ppermute | solution.py:195
  37.9 2.7 collective-permute-start.3
  40.6 2.7 collective-permute-start.18
  43.3 4.3 %collective-permute-start.4 = (bf16[704,256]{1,0:T(8,128)(2,1)}, bf16[704,256]{1,0:T(8,128)(2,1)S(1)}, u32[]{:S(2)}, u32[]{:S(2)}) collective-permute-start(bf16[704,256]{1,0:T(8,128)(2,1)} %collective-permute-done.1), channel_id=1, source_target_pairs={{0,16},{16,32},{32,48},{48,64},{64,80},{80,96},{96,112},{112,0},{1... | collective-permute-start | bytes 1081352 | tf_op jit(solution)/shard_map/ppermute | solution.py:195
  47.6 1.8 constant_dynamic-update-slice_fusion.3
  49.4 4.1 %collective-permute-done.2 = bf16[704,256]{1,0:T(8,128)(2,1)S(1)} collective-permute-done((bf16[704,256]{1,0:T(8,128)(2,1)}, bf16[704,256]{1,0:T(8,128)(2,1)S(1)}, u32[]{:S(2)}, u32[]{:S(2)}) %collective-permute-start.2) | collective-permute-done | bytes 360480 | tf_op jit(solution)/shard_map/ppermute | solution.py:195
  55.1 6.4 %collective-permute-done.4 = bf16[704,256]{1,0:T(8,128)(2,1)S(1)} collective-permute-done((bf16[704,256]{1,0:T(8,128)(2,1)}, bf16[704,256]{1,0:T(8,128)(2,1)S(1)}, u32[]{:S(2)}, u32[]{:S(2)}) %collective-permute-start.4) | collective-permute-done | bytes 360480 | tf_op jit(solution)/shard_map/ppermute | solution.py:195
  62.3 3.1 %collective-permute-done.18 = bf16[64,3456]{1,0:T(8,128)(2,1)} collective-permute-done((bf16[64,3456]{1,0:T(8,128)(2,1)S(1)}, bf16[64,3456]{1,0:T(8,128)(2,1)}, u32[]{:S(2)}, u32[]{:S(2)}) %collective-permute-start.18) | collective-permute-done | bytes 442400 | tf_op jit(solution)/shard_map/ppermute | solution.py:200
  65.8 1.9 collective-permute-start.5
  67.8 2.4 collective-permute-start.6
  70.2 1.1 collective-permute-done.6
  72.2 4.4 %collective-permute-start.7 = (bf16[2,16,2048]{2,1,0:T(8,128)(2,1)S(1)}, bf16[2,16,2048]{2,1,0:T(8,128)(2,1)S(1)}, u32[]{:S(2)}, u32[]{:S(2)}) collective-permute-start(bf16[2,16,2048]{2,1,0:T(8,128)(2,1)S(1)} %get-tuple-element.89), channel_id=1, source_target_pairs={{0,2},{2,0},{1,3},{3,1},{4,6},{6,4},{5,7},{7,5},{8,10},{10,8},{9,1... | collective-permute-start | bytes 393224 | tf_op jit(solution)/shard_map/ppermute | solution.py:200
  76.7 9.7 %collective-permute-done.7 = bf16[2,16,2048]{2,1,0:T(8,128)(2,1)S(1)} collective-permute-done((bf16[2,16,2048]{2,1,0:T(8,128)(2,1)S(1)}, bf16[2,16,2048]{2,1,0:T(8,128)(2,1)S(1)}, u32[]{:S(2)}, u32[]{:S(2)}) %collective-permute-start.7) | collective-permute-done | bytes 131104 | tf_op jit(solution)/shard_map/ppermute | solution.py:200
  87.0 3.0 %collective-permute-start.10 = (bf16[2,32,2048]{2,1,0:T(8,128)(2,1)}, bf16[2,32,2048]{2,1,0:T(8,128)(2,1)}, u32[]{:S(2)}, u32[]{:S(2)}) collective-permute-start(bf16[2,32,2048]{2,1,0:T(8,128)(2,1)} %pad_maximum_fusion.3.c0), channel_id=1, source_target_pairs={{0,12},{4,0},{8,4},{12,8},{1,13},{5,1},{9,5},{13,9},{2,14},{6,2},{... | collective-permute-start | bytes 786440 | tf_op jit(solution)/shard_map/ppermute | solution.py:195
  90.1 4.6 %collective-permute-start.8 = (bf16[2,32,2048]{2,1,0:T(8,128)(2,1)}, bf16[2,32,2048]{2,1,0:T(8,128)(2,1)}, u32[]{:S(2)}, u32[]{:S(2)}) collective-permute-start(bf16[2,32,2048]{2,1,0:T(8,128)(2,1)} %pad_maximum_fusion.3.c0), channel_id=1, source_target_pairs={{0,4},{4,8},{8,12},{12,0},{1,5},{5,9},{9,13},{13,1},{2,6},{6,10},{... | collective-permute-start | bytes 786440 | tf_op jit(solution)/shard_map/ppermute | solution.py:195
  94.7 1.9 collective-permute-start.9
  96.7 1.1 copy-done.2
  97.8 5.0 %encoder_up.1 = (bf16[256,1024]{1,0:T(8,128)(2,1)S(1)}, f32[256,1024]{1,0:T(8,128)S(1)}, bf16[64,1408]{1,0:T(8,128)(2,1)S(1)}) custom-call(s32[3]{0:T(128)S(1)} %pad_add_fusion.place, bf16[256,1408]{1,0:T(8,128)(2,1)S(1)} %bitcast.27, f32[1,1408]{1,0:T(1,128)S(1)} %reshape.56.gain, bf16[704,1024]{1,0:T(8,128)(2,1)S(1)} %pad_maximum_fusion.w0, ...), custom_call_target="tpu_custom_call" | custom-call | tf_op jit(solution)/shard_map/encoder_up/pallas_call | solution.py:271
  102.8 1.0 copy-done
  103.8 3.5 %encoder_down.1 = (bf16[64,1408]{1,0:T(8,128)(2,1)S(1)}, bf16[64,1408]{1,0:T(8,128)(2,1)S(1)}, bf16[64,1408]{1,0:T(8,128)(2,1)S(1)}, bf16[64,1408]{1,0:T(8,128)(2,1)S(1)}) custom-call(s32[3]{0:T(128)S(1)} %pad_add_fusion.place, bf16[256,1024]{1,0:T(8,128)(2,1)S(1)} %get-tuple-element.43.act, bf16[704,1024]{1,0:T(8,128)(2,1)S(1)} %pad_maximum_fusion.w0, ...), custom_call_target="tpu_custom_call" | custom-call | tf_op jit(solution)/shard_map/encoder_down/pallas_call | solution.py:285
  107.3 7.5 %collective-permute-done.9.c2 = bf16[2,32,2048]{2,1,0:T(8,128)(2,1)} collective-permute-done((bf16[2,32,2048]{2,1,0:T(8,128)(2,1)}, bf16[2,32,2048]{2,1,0:T(8,128)(2,1)}, u32[]{:S(2)}, u32[]{:S(2)}) %collective-permute-start.9) | collective-permute-done | bytes 262176 | tf_op jit(solution)/shard_map/ppermute | solution.py:195
  114.8 2.7 collective-permute-start.11
  117.5 1.9 collective-permute-start.12
  119.5 3.1 %collective-permute-start.13 = (bf16[64,1408]{1,0:T(8,128)(2,1)S(1)}, bf16[64,1408]{1,0:T(8,128)(2,1)S(1)}, u32[]{:S(2)}, u32[]{:S(2)}) collective-permute-start(bf16[64,1408]{1,0:T(8,128)(2,1)S(1)} %get-tuple-element.52), channel_id=1, source_target_pairs={{0,12},{4,0},{8,4},{12,8},{1,13},{5,1},{9,5},{13,9},{2,14},{6,2},{... | collective-permute-start | bytes 540680 | tf_op jit(solution)/shard_map/ppermute | solution.py:195
  122.6 1.9 collective-permute-start.17
  124.5 8.8 %collective-permute-done.12 = bf16[64,1408]{1,0:T(8,128)(2,1)S(1)} collective-permute-done((bf16[64,1408]{1,0:T(8,128)(2,1)S(1)}, bf16[64,1408]{1,0:T(8,128)(2,1)S(1)}, u32[]{:S(2)}, u32[]{:S(2)}) %collective-permute-start.12) | collective-permute-done | bytes 180256 | tf_op jit(solution)/shard_map/ppermute | solution.py:195
  134.2 2.1 collective-permute-start.19
  136.3 2.9 %collective-permute-start.14 = (bf16[64,1408]{1,0:T(8,128)(2,1)}, bf16[64,1408]{1,0:T(8,128)(2,1)S(1)}, u32[]{:S(2)}, u32[]{:S(2)}) collective-permute-start(bf16[64,1408]{1,0:T(8,128)(2,1)} %get-tuple-element.92.e0), channel_id=1, source_target_pairs={{0,4},{4,8},{8,12},{12,0},{1,5},{5,9},{9,13},{13,1},{2,6},{6,10},{... | collective-permute-start | bytes 540680 | tf_op jit(solution)/shard_map/ppermute | solution.py:195
  139.2 3.1 %collective-permute-start.15 = (bf16[64,1408]{1,0:T(8,128)(2,1)}, bf16[64,1408]{1,0:T(8,128)(2,1)S(1)}, u32[]{:S(2)}, u32[]{:S(2)}) collective-permute-start(bf16[64,1408]{1,0:T(8,128)(2,1)} %get-tuple-element.92.e0), channel_id=1, source_target_pairs={{0,8},{4,12},{8,0},{12,4},{1,9},{5,13},{9,1},{13,5},{2,10},{6,14},... | collective-permute-start | bytes 540680 | tf_op jit(solution)/shard_map/ppermute | solution.py:195
  142.3 3.9 %collective-permute-start.16 = (bf16[64,1408]{1,0:T(8,128)(2,1)}, bf16[64,1408]{1,0:T(8,128)(2,1)S(1)}, u32[]{:S(2)}, u32[]{:S(2)}) collective-permute-start(bf16[64,1408]{1,0:T(8,128)(2,1)} %get-tuple-element.92.e0), channel_id=1, source_target_pairs={{0,12},{4,0},{8,4},{12,8},{1,13},{5,1},{9,5},{13,9},{2,14},{6,2},{... | collective-permute-start | bytes 540680 | tf_op jit(solution)/shard_map/ppermute | solution.py:195
  146.3 1.2 copy-done.14
  147.5 3.8 %query.1 = (bf16[4,128,128]{2,1,0:T(8,128)(2,1)S(1)}, bf16[4,128,128]{2,1,0:T(8,128)(2,1)S(1)}) custom-call(bf16[2,32,2048]{2,1,0:T(8,128)(2,1)} %pad_maximum_fusion.3.c0, bf16[2,32,2048]{2,1,0:T(8,128)(2,1)} %collective-permute-done.8.c1, bf16[2,32,2048]{2,1,0:T(8,128)(2,1)} %collective-permute-done.9.c2, bf16[2,32,2048]{2,1,0:T(8,128)(2,1)} %collective-permute-done.10.c3, ...), custom_call_target="tpu_custom_call" | custom-call | tf_op jit(solution)/shard_map/query/pallas_call | solution.py:304
  151.4 6.0 %collective-permute-done.15.e2 = bf16[64,1408]{1,0:T(8,128)(2,1)S(1)} collective-permute-done((bf16[64,1408]{1,0:T(8,128)(2,1)}, bf16[64,1408]{1,0:T(8,128)(2,1)S(1)}, u32[]{:S(2)}, u32[]{:S(2)}) %collective-permute-start.15) | collective-permute-done | bytes 180256 | tf_op jit(solution)/shard_map/ppermute | solution.py:195
  157.4 5.0 %attention.1 = (bf16[64,1408]{1,0:T(8,128)(2,1)S(1)}, bf16[64,1408]{1,0:T(8,128)(2,1)S(1)}, bf16[64,1408]{1,0:T(8,128)(2,1)S(1)}, bf16[64,1408]{1,0:T(8,128)(2,1...) custom-call(bf16[64,1408]{1,0:T(8,128)(2,1)S(1)} %copy-done.3, ...), custom_call_target="tpu_custom_call" | custom-call | tf_op jit(solution)/shard_map/attention/pallas_call | solution.py:313
  163.3 1.9 collective-permute-start.26
  165.2 3.2 %collective-permute-done.26 = bf16[1408,512]{1,0:T(8,128)(2,1)S(1)} collective-permute-done((bf16[1408,512]{1,0:T(8,128)(2,1)S(1)}, bf16[1408,512]{1,0:T(8,128)(2,1)S(1)}, u32[]{:S(2)}, u32[]{:S(2)}) %collective-permute-start.26) | collective-permute-done | bytes 1441824 | tf_op jit(solution)/shard_map/ppermute | solution.py:200
  168.4 1.7 fusion
  171.0 1.9 collective-permute-start.20
  172.9 3.4 %collective-permute-start.21 = (bf16[64,1408]{1,0:T(8,128)(2,1)S(1)}, bf16[64,1408]{1,0:T(8,128)(2,1)S(1)}, u32[]{:S(2)}, u32[]{:S(2)}) collective-permute-start(bf16[64,1408]{1,0:T(8,128)(2,1)S(1)} %copy-done.11), channel_id=1, source_target_pairs={{0,8},{4,12},{8,0},{12,4},{1,9},{5,13},{9,1},{13,5},{2,10},{6,14},... | collective-permute-start | bytes 540680 | tf_op jit(solution)/shard_map/ppermute | solution.py:195
  176.4 3.9 %collective-permute-start.22 = (bf16[64,1408]{1,0:T(8,128)(2,1)S(1)}, bf16[64,1408]{1,0:T(8,128)(2,1)S(1)}, u32[]{:S(2)}, u32[]{:S(2)}) collective-permute-start(bf16[64,1408]{1,0:T(8,128)(2,1)S(1)} %copy-done.9), channel_id=1, source_target_pairs={{0,12},{4,0},{8,4},{12,8},{1,13},{5,1},{9,5},{13,9},{2,14},{6,2},{... | collective-permute-start | bytes 540680 | tf_op jit(solution)/shard_map/ppermute | solution.py:195
  180.3 10.5 %collective-permute-done.21 = bf16[64,1408]{1,0:T(8,128)(2,1)S(1)} collective-permute-done((bf16[64,1408]{1,0:T(8,128)(2,1)S(1)}, bf16[64,1408]{1,0:T(8,128)(2,1)S(1)}, u32[]{:S(2)}, u32[]{:S(2)}) %collective-permute-start.21) | collective-permute-done | bytes 180256 | tf_op jit(solution)/shard_map/ppermute | solution.py:195
  191.0 2.0 collective-permute-start.23
  192.9 3.3 %collective-permute-start.24 = (bf16[64,1408]{1,0:T(8,128)(2,1)S(1)}, bf16[64,1408]{1,0:T(8,128)(2,1)S(1)}, u32[]{:S(2)}, u32[]{:S(2)}) collective-permute-start(bf16[64,1408]{1,0:T(8,128)(2,1)S(1)} %add_convert_fusion.g0), channel_id=1, source_target_pairs={{0,8},{4,12},{8,0},{12,4},{1,9},{5,13},{9,1},{13,5},{2,10},{6,14},... | collective-permute-start | bytes 540680 | tf_op jit(solution)/shard_map/ppermute | solution.py:195
  196.2 3.9 %collective-permute-start.25 = (bf16[64,1408]{1,0:T(8,128)(2,1)S(1)}, bf16[64,1408]{1,0:T(8,128)(2,1)S(1)}, u32[]{:S(2)}, u32[]{:S(2)}) collective-permute-start(bf16[64,1408]{1,0:T(8,128)(2,1)S(1)} %add_convert_fusion.g0), channel_id=1, source_target_pairs={{0,12},{4,0},{8,4},{12,8},{1,13},{5,1},{9,5},{13,9},{2,14},{6,2},{... | collective-permute-start | bytes 540680 | tf_op jit(solution)/shard_map/ppermute | solution.py:195
  200.2 2.8 reduce-scatter.2.cloned.1.call-done
  203.9 5.1 %collective-permute-start.27 = (bf16[352,256]{1,0:T(8,128)(2,1)S(1)}, bf16[352,256]{1,0:T(8,128)(2,1)S(1)}, u32[]{:S(2)}, u32[]{:S(2)}) collective-permute-start(bf16[352,256]{1,0:T(8,128)(2,1)S(1)} %slice.33), channel_id=1, source_target_pairs={{0,2},{2,0},{1,3},{3,1},{4,6},{6,4},{5,7},{7,5},{8,10},{10,8},{9,1... | collective-permute-start | bytes 540680 | tf_op jit(solution)/shard_map/ppermute | solution.py:200
  209.2 5.7 %collective-permute-done.24.g2 = bf16[64,1408]{1,0:T(8,128)(2,1)S(1)} collective-permute-done((bf16[64,1408]{1,0:T(8,128)(2,1)S(1)}, bf16[64,1408]{1,0:T(8,128)(2,1)S(1)}, u32[]{:S(2)}, u32[]{:S(2)}) %collective-permute-start.24) | collective-permute-done | bytes 180256 | tf_op jit(solution)/shard_map/ppermute | solution.py:195
  214.9 5.3 %encoder_back.1 = (bf16[64,1408]{1,0:T(8,128)(2,1)S(1)}, bf16[64,1408]{1,0:T(8,128)(2,1)}, bf16[64,1408]{1,0:T(8,128)(2,1)}, bf16[64,1408]{1,0:T(8,128)(2,1)}) custom-call(s32[3]{0:T(128)S(1)} %pad_add_fusion.place, bf16[64,1408]{1,0:T(8,128)(2,1)S(1)} %add_convert_fusion.g0, bf16[64,1408]{1,0:T(8,128)(2,1)S(1)} %collective-permute-done.23.g1, ...), custom_call_target="tpu_custom_call" | custom-call | tf_op jit(solution)/shard_map/encoder_back/pallas_call | solution.py:339
  221.0 2.1 collective-permute-start.28
  223.1 4.7 %collective-permute-start.29 = (bf16[64,1408]{1,0:T(8,128)(2,1)}, bf16[64,1408]{1,0:T(8,128)(2,1)S(1)}, u32[]{:S(2)}, u32[]{:S(2)}) collective-permute-start(bf16[64,1408]{1,0:T(8,128)(2,1)} %get-tuple-element.76), channel_id=1, source_target_pairs={{0,8},{4,12},{8,0},{12,4},{1,9},{5,13},{9,1},{13,5},{2,10},{6,14},... | collective-permute-start | bytes 540680 | tf_op jit(solution)/shard_map/ppermute | solution.py:195
  227.8 3.9 %collective-permute-start.30 = (bf16[64,1408]{1,0:T(8,128)(2,1)}, bf16[64,1408]{1,0:T(8,128)(2,1)S(1)}, u32[]{:S(2)}, u32[]{:S(2)}) collective-permute-start(bf16[64,1408]{1,0:T(8,128)(2,1)} %get-tuple-element.77), channel_id=1, source_target_pairs={{0,12},{4,0},{8,4},{12,8},{1,13},{5,1},{9,5},{13,9},{2,14},{6,2},{... | collective-permute-start | bytes 540680 | tf_op jit(solution)/shard_map/ppermute | solution.py:195
  232.4 12.3 %all-to-all-start = ((bf16[8,44,256]{2,1,0:T(8,128)(2,1)}), bf16[8,44,256]{2,1,0:T(8,128)(2,1)S(1)}, u32[]{:S(2)}, u32[]{:S(2)}) async-start(bf16[8,44,256]{2,1,0:T(8,128)(2,1)} %reshape.58), calls=%async_computation.1 | async-start | bytes 393216 | tf_op jit(solution)/shard_map/all_to_all | solution.py:357
  245.2 9.3 %all-to-all-done = bf16[8,44,256]{2,1,0:T(8,128)(2,1)S(1)} async-done(((bf16[8,44,256]{2,1,0:T(8,128)(2,1)}), bf16[8,44,256]{2,1,0:T(8,128)(2,1)S(1)}, u32[]{:S(2)}, u32[]{:S(2)}) %all-to-all-start) | async-done | bytes 180256 | tf_op jit(solution)/shard_map/all_to_all | solution.py:357
  254.5 17.5 %all_gather.7 = bf16[256,1408]{1,0:T(8,128)(2,1)S(1)} all-gather(bf16[64,1408]{1,0:T(8,128)(2,1)S(1)} %fusion.9), channel_id=1, replica_groups=mesh['x'=4,'zh'=2,'zl'=4,'tensor'=4,'yh'=2,'core'=2] {'tensor'}, dimensions={0}, use_global_device_ids=true | all-gather | bytes 901120 | tf_op jit(solution)/shard_map/all_gather | solution.py:370
  (104 shorter events, 13.1 us)
Async XLA Ops:
  7.2 7.6 %copy-start.18 = (bf16[352,1024]{1,0:T(8,128)(2,1)S(1)}, bf16[352,1024]{1,0:T(8,128)(2,1)}, u32[]{:S(2)}) copy-start(bf16[352,1024]{1,0:T(8,128)(2,1)} %param.13) | copy-start | bytes 2162692
  7.2 7.6 %copy-start.17 = (bf16[1024,352]{0,1:T(8,128)(2,1)S(1)}, bf16[1024,352]{0,1:T(8,128)(2,1)}, u32[]{:S(2)}) copy-start(bf16[1024,352]{0,1:T(8,128)(2,1)} %param.14) | copy-start | bytes 2162692
  7.2 127.0 %all-gather.2.cloned.1.call-start = ((), (), s32[]{:S(2)}) async-start(), calls=%async_computation.2 | async-start | bytes 2211840 | tf_op jit(solution)/shard_map/all_gather | solution.py:300
  10.0 23.2 %collective-permute-start.1 = (bf16[704,256]{1,0:T(8,128)(2,1)}, bf16[704,256]{1,0:T(8,128)(2,1)}, u32[]{:S(2)}, u32[]{:S(2)}) collective-permute-start(bf16[704,256]{1,0:T(8,128)(2,1)} %pad_maximum_fusion.1), channel_id=1, source_target_pairs={{0,2},{2,0},{1,3},{3,1},{4,6},{6,4},{5,7},{7,5},{8,10},{10,8},{9,1... | collective-permute-start | bytes 1081352 | tf_op jit(solution)/shard_map/ppermute | solution.py:200
  14.7 4.6 %copy-start.19 = (bf16[2048,128]{1,0:T(8,128)(2,1)S(1)}, bf16[2048,128]{1,0:T(8,128)(2,1)}, u32[]{:S(2)}) copy-start(bf16[2048,128]{1,0:T(8,128)(2,1)} %param.17) | copy-start | bytes 1572868
  14.9 81.9 %collective-permute-start = (bf16[704,1024]{1,0:T(8,128)(2,1)S(1)}, bf16[704,1024]{1,0:T(8,128)(2,1)}, u32[]{:S(2)}, u32[]{:S(2)}) collective-permute-start(bf16[704,1024]{1,0:T(8,128)(2,1)S(1)} %pad_maximum_fusion.w0), channel_id=1, source_target_pairs={{0,1},{1,0},{2,3},{3,2},{4,5},{5,4},{6,7},{7,6},{8,9},{9,8},{10,11... | collective-permute-start | bytes 4325384 | tf_op jit(solution)/shard_map/ppermute | solution.py:200
  20.3 1.0 copy-start.15
  21.4 1.2 copy-start.16
  33.2 20.3 %collective-permute-start.2 = (bf16[704,256]{1,0:T(8,128)(2,1)}, bf16[704,256]{1,0:T(8,128)(2,1)S(1)}, u32[]{:S(2)}, u32[]{:S(2)}) collective-permute-start(bf16[704,256]{1,0:T(8,128)(2,1)} %collective-permute-done.1), channel_id=1, source_target_pairs={{0,384},{128,0},{256,128},{384,256},{1,385},{129,1},{257,129},{385... | collective-permute-start | bytes 1081352 | tf_op jit(solution)/shard_map/ppermute | solution.py:195
  37.9 16.5 %collective-permute-start.3 = (bf16[704,256]{1,0:T(8,128)(2,1)}, bf16[704,256]{1,0:T(8,128)(2,1)S(1)}, u32[]{:S(2)}, u32[]{:S(2)}) collective-permute-start(bf16[704,256]{1,0:T(8,128)(2,1)} %collective-permute-done.1), channel_id=1, source_target_pairs={{0,256},{128,384},{256,0},{384,128},{1,257},{129,385},{257,1},{385... | collective-permute-start | bytes 1081352 | tf_op jit(solution)/shard_map/ppermute | solution.py:195
  40.6 24.8 %collective-permute-start.18 = (bf16[64,3456]{1,0:T(8,128)(2,1)S(1)}, bf16[64,3456]{1,0:T(8,128)(2,1)}, u32[]{:S(2)}, u32[]{:S(2)}) collective-permute-start(bf16[64,3456]{1,0:T(8,128)(2,1)S(1)} %constant_dynamic-slice_fusion), channel_id=1, source_target_pairs={{0,2},{2,0},{1,3},{3,1},{4,6},{6,4},{5,7},{7,5},{8,10},{10,8},{9,1... | collective-permute-start | bytes 1327112 | tf_op jit(solution)/shard_map/ppermute | solution.py:200
  43.3 18.2 %collective-permute-start.4 = (bf16[704,256]{1,0:T(8,128)(2,1)}, bf16[704,256]{1,0:T(8,128)(2,1)S(1)}, u32[]{:S(2)}, u32[]{:S(2)}) collective-permute-start(bf16[704,256]{1,0:T(8,128)(2,1)} %collective-permute-done.1), channel_id=1, source_target_pairs={{0,16},{16,32},{32,48},{48,64},{64,80},{80,96},{96,112},{112,0},{1... | collective-permute-start | bytes 1081352 | tf_op jit(solution)/shard_map/ppermute | solution.py:195
  49.4 16.3 %copy-start.23 = (f32[2048]{0:T(1024)S(1)}, f32[2048]{0:T(1024)}, u32[]{:S(2)}) copy-start(f32[2048]{0:T(1024)} %param.16) | copy-start | bytes 24580
  49.4 18.3 %copy-start.21 = (bf16[4,8,2048]{2,1,0:T(8,128)(2,1)S(1)}, bf16[4,8,2048]{2,1,0:T(8,128)(2,1)}, u32[]{:S(2)}) copy-start(bf16[4,8,2048]{2,1,0:T(8,128)(2,1)} %param.21) | copy-start | bytes 393220
  65.4 137.6 %reduce-scatter.2.cloned.1.call-start = ((), (), s32[]{:S(2)}) async-start(), calls=%async_computation.3 | async-start | bytes 1802240 | tf_op jit(solution)/shard_map/reduce_scatter | solution.py:336
  65.6 31.0 %copy-start.22 = (f32[1408]{0:T(1024)S(1)}, f32[1408]{0:T(1024)}, u32[]{:S(2)}) copy-start(f32[1408]{0:T(1024)} %param.12) | copy-start | bytes 16900
  65.8 31.0 %collective-permute-start.5 = (bf16[704,1024]{1,0:T(8,128)(2,1)}, bf16[704,1024]{1,0:T(8,128)(2,1)}, u32[]{:S(2)}, u32[]{:S(2)}) collective-permute-start(bf16[704,1024]{1,0:T(8,128)(2,1)} %constant_dynamic-update-slice_fusion.w2), channel_id=1, source_target_pairs={{0,1},{1,0},{2,3},{3,2},{4,5},{5,4},{6,7},{7,6},{8,9},{9,8},{10,11... | collective-permute-start | bytes 4325384 | tf_op jit(solution)/shard_map/ppermute | solution.py:200
  67.8 3.5 %collective-permute-start.6 = (bf16[2,2,8,2048]{3,2,1,0:T(8,128)(2,1)S(1)}, bf16[2,2,8,2048]{3,2,1,0:T(8,128)(2,1)}, u32[]{:S(2)}, u32[]{:S(2)}) collective-permute-start(bf16[2,2,8,2048]{3,2,1,0:T(8,128)(2,1)S(1)} %bitcast.33), channel_id=1, source_target_pairs={{0,1},{1,0},{2,3},{3,2},{4,5},{5,4},{6,7},{7,6},{8,9},{9,8},{10,11... | collective-permute-start | bytes 393224 | tf_op jit(solution)/shard_map/ppermute | solution.py:200
  72.2 14.1 %collective-permute-start.7 = (bf16[2,16,2048]{2,1,0:T(8,128)(2,1)S(1)}, bf16[2,16,2048]{2,1,0:T(8,128)(2,1)S(1)}, u32[]{:S(2)}, u32[]{:S(2)}) collective-permute-start(bf16[2,16,2048]{2,1,0:T(8,128)(2,1)S(1)} %get-tuple-element.89), channel_id=1, source_target_pairs={{0,2},{2,0},{1,3},{3,1},{4,6},{6,4},{5,7},{7,5},{8,10},{10,8},{9,1... | collective-permute-start | bytes 393224 | tf_op jit(solution)/shard_map/ppermute | solution.py:200
  87.0 20.2 %collective-permute-start.10 = (bf16[2,32,2048]{2,1,0:T(8,128)(2,1)}, bf16[2,32,2048]{2,1,0:T(8,128)(2,1)}, u32[]{:S(2)}, u32[]{:S(2)}) collective-permute-start(bf16[2,32,2048]{2,1,0:T(8,128)(2,1)} %pad_maximum_fusion.3.c0), channel_id=1, source_target_pairs={{0,12},{4,0},{8,4},{12,8},{1,13},{5,1},{9,5},{13,9},{2,14},{6,2},{... | collective-permute-start | bytes 786440 | tf_op jit(solution)/shard_map/ppermute | solution.py:195
  90.1 17.2 %collective-permute-start.8 = (bf16[2,32,2048]{2,1,0:T(8,128)(2,1)}, bf16[2,32,2048]{2,1,0:T(8,128)(2,1)}, u32[]{:S(2)}, u32[]{:S(2)}) collective-permute-start(bf16[2,32,2048]{2,1,0:T(8,128)(2,1)} %pad_maximum_fusion.3.c0), channel_id=1, source_target_pairs={{0,4},{4,8},{8,12},{12,0},{1,5},{5,9},{9,13},{13,1},{2,6},{6,10},{... | collective-permute-start | bytes 786440 | tf_op jit(solution)/shard_map/ppermute | solution.py:195
  94.7 20.1 %collective-permute-start.9 = (bf16[2,32,2048]{2,1,0:T(8,128)(2,1)}, bf16[2,32,2048]{2,1,0:T(8,128)(2,1)}, u32[]{:S(2)}, u32[]{:S(2)}) collective-permute-start(bf16[2,32,2048]{2,1,0:T(8,128)(2,1)} %pad_maximum_fusion.3.c0), channel_id=1, source_target_pairs={{0,8},{4,12},{8,0},{12,4},{1,9},{5,13},{9,1},{13,5},{2,10},{6,14},... | collective-permute-start | bytes 786440 | tf_op jit(solution)/shard_map/ppermute | solution.py:195
  96.7 1.1 copy-start.2
  102.8 1.0 copy-start
  114.8 9.7 %collective-permute-start.11 = (bf16[64,1408]{1,0:T(8,128)(2,1)S(1)}, bf16[64,1408]{1,0:T(8,128)(2,1)S(1)}, u32[]{:S(2)}, u32[]{:S(2)}) collective-permute-start(bf16[64,1408]{1,0:T(8,128)(2,1)S(1)} %get-tuple-element.50), channel_id=1, source_target_pairs={{0,4},{4,8},{8,12},{12,0},{1,5},{5,9},{9,13},{13,1},{2,6},{6,10},{... | collective-permute-start | bytes 540680 | tf_op jit(solution)/shard_map/ppermute | solution.py:195
  117.5 15.8 %collective-permute-start.12 = (bf16[64,1408]{1,0:T(8,128)(2,1)S(1)}, bf16[64,1408]{1,0:T(8,128)(2,1)S(1)}, u32[]{:S(2)}, u32[]{:S(2)}) collective-permute-start(bf16[64,1408]{1,0:T(8,128)(2,1)S(1)} %get-tuple-element.51), channel_id=1, source_target_pairs={{0,8},{4,12},{8,0},{12,4},{1,9},{5,13},{9,1},{13,5},{2,10},{6,14},... | collective-permute-start | bytes 540680 | tf_op jit(solution)/shard_map/ppermute | solution.py:195
  119.5 13.8 %collective-permute-start.13 = (bf16[64,1408]{1,0:T(8,128)(2,1)S(1)}, bf16[64,1408]{1,0:T(8,128)(2,1)S(1)}, u32[]{:S(2)}, u32[]{:S(2)}) collective-permute-start(bf16[64,1408]{1,0:T(8,128)(2,1)S(1)} %get-tuple-element.52), channel_id=1, source_target_pairs={{0,12},{4,0},{8,4},{12,8},{1,13},{5,1},{9,5},{13,9},{2,14},{6,2},{... | collective-permute-start | bytes 540680 | tf_op jit(solution)/shard_map/ppermute | solution.py:195
  122.6 23.7 %collective-permute-start.17 = (bf16[256,3456]{1,0:T(8,128)(2,1)S(1)}, bf16[256,3456]{1,0:T(8,128)(2,1)}, u32[]{:S(2)}, u32[]{:S(2)}) collective-permute-start(bf16[256,3456]{1,0:T(8,128)(2,1)S(1)} %maximum_maximum_fusion.p0), channel_id=1, source_target_pairs={{0,1},{1,0},{2,3},{3,2},{4,5},{5,4},{6,7},{7,6},{8,9},{9,8},{10,11... | collective-permute-start | bytes 5308424 | tf_op jit(solution)/shard_map/ppermute | solution.py:200
  134.2 23.2 %copy-start.3 = (bf16[64,1408]{1,0:T(8,128)(2,1)S(1)}, bf16[64,1408]{1,0:T(8,128)(2,1)}, u32[]{:S(2)}) copy-start(bf16[64,1408]{1,0:T(8,128)(2,1)} %get-tuple-element.92.e0) | copy-start | bytes 540676
  134.2 12.0 %collective-permute-start.19 = (bf16[256,3456]{1,0:T(8,128)(2,1)}, bf16[256,3456]{1,0:T(8,128)(2,1)S(1)}, u32[]{:S(2)}, u32[]{:S(2)}) collective-permute-start(bf16[256,3456]{1,0:T(8,128)(2,1)} %all-gather.2.cloned.1.call-done.p2), channel_id=1, source_target_pairs={{0,1},{1,0},{2,3},{3,2},{4,5},{5,4},{6,7},{7,6},{8,9},{9,8},{10,11... | collective-permute-start | bytes 5308424 | tf_op jit(solution)/shard_map/ppermute | solution.py:200
  136.3 15.1 %collective-permute-start.14 = (bf16[64,1408]{1,0:T(8,128)(2,1)}, bf16[64,1408]{1,0:T(8,128)(2,1)S(1)}, u32[]{:S(2)}, u32[]{:S(2)}) collective-permute-start(bf16[64,1408]{1,0:T(8,128)(2,1)} %get-tuple-element.92.e0), channel_id=1, source_target_pairs={{0,4},{4,8},{8,12},{12,0},{1,5},{5,9},{9,13},{13,1},{2,6},{6,10},{... | collective-permute-start | bytes 540680 | tf_op jit(solution)/shard_map/ppermute | solution.py:195
  139.2 18.1 %collective-permute-start.15 = (bf16[64,1408]{1,0:T(8,128)(2,1)}, bf16[64,1408]{1,0:T(8,128)(2,1)S(1)}, u32[]{:S(2)}, u32[]{:S(2)}) collective-permute-start(bf16[64,1408]{1,0:T(8,128)(2,1)} %get-tuple-element.92.e0), channel_id=1, source_target_pairs={{0,8},{4,12},{8,0},{12,4},{1,9},{5,13},{9,1},{13,5},{2,10},{6,14},... | collective-permute-start | bytes 540680 | tf_op jit(solution)/shard_map/ppermute | solution.py:195
  142.3 15.1 %collective-permute-start.16 = (bf16[64,1408]{1,0:T(8,128)(2,1)}, bf16[64,1408]{1,0:T(8,128)(2,1)S(1)}, u32[]{:S(2)}, u32[]{:S(2)}) collective-permute-start(bf16[64,1408]{1,0:T(8,128)(2,1)} %get-tuple-element.92.e0), channel_id=1, source_target_pairs={{0,12},{4,0},{8,4},{12,8},{1,13},{5,1},{9,5},{13,9},{2,14},{6,2},{... | collective-permute-start | bytes 540680 | tf_op jit(solution)/shard_map/ppermute | solution.py:195
  146.3 1.2 copy-start.14
  162.4 0.7 copy-start.6
  162.4 0.7 copy-start.8
  162.4 0.8 copy-start.10
  162.4 0.8 copy-start.12
  163.3 5.1 %collective-permute-start.26 = (bf16[1408,512]{1,0:T(8,128)(2,1)S(1)}, bf16[1408,512]{1,0:T(8,128)(2,1)S(1)}, u32[]{:S(2)}, u32[]{:S(2)}) collective-permute-start(bf16[1408,512]{1,0:T(8,128)(2,1)S(1)} %convolution_convert_fusion), channel_id=1, source_target_pairs={{0,1},{1,0},{2,3},{3,2},{4,5},{5,4},{6,7},{7,6},{8,9},{9,8},{10,11... | collective-permute-start | bytes 4325384 | tf_op jit(solution)/shard_map/ppermute | solution.py:200
  170.1 0.9 copy-start.13
  170.1 2.8 %copy-start.11 = (bf16[64,1408]{1,0:T(8,128)(2,1)S(1)}, bf16[64,1408]{1,0:T(8,128)(2,1)}, u32[]{:S(2)}) copy-start(bf16[64,1408]{1,0:T(8,128)(2,1)} %copy-done.10) | copy-start | bytes 540676
  170.1 6.3 %copy-start.9 = (bf16[64,1408]{1,0:T(8,128)(2,1)S(1)}, bf16[64,1408]{1,0:T(8,128)(2,1)}, u32[]{:S(2)}) copy-start(bf16[64,1408]{1,0:T(8,128)(2,1)} %copy-done.8) | copy-start | bytes 540676
  170.1 20.8 %copy-start.7 = (bf16[64,1408]{1,0:T(8,128)(2,1)S(1)}, bf16[64,1408]{1,0:T(8,128)(2,1)}, u32[]{:S(2)}) copy-start(bf16[64,1408]{1,0:T(8,128)(2,1)} %copy-done.6) | copy-start | bytes 540676
  170.1 44.8 %copy-start.1 = (f32[256,1024]{1,0:T(8,128)S(1)}, f32[256,1024]{1,0:T(8,128)}, u32[]{:S(2)}) copy-start(f32[256,1024]{1,0:T(8,128)} %copy-done) | copy-start | bytes 3145732
  171.0 9.3 %collective-permute-start.20 = (bf16[64,1408]{1,0:T(8,128)(2,1)S(1)}, bf16[64,1408]{1,0:T(8,128)(2,1)S(1)}, u32[]{:S(2)}, u32[]{:S(2)}) collective-permute-start(bf16[64,1408]{1,0:T(8,128)(2,1)S(1)} %copy-done.13), channel_id=1, source_target_pairs={{0,4},{4,8},{8,12},{12,0},{1,5},{5,9},{9,13},{13,1},{2,6},{6,10},{... | collective-permute-start | bytes 540680 | tf_op jit(solution)/shard_map/ppermute | solution.py:195
  172.9 17.9 %collective-permute-start.21 = (bf16[64,1408]{1,0:T(8,128)(2,1)S(1)}, bf16[64,1408]{1,0:T(8,128)(2,1)S(1)}, u32[]{:S(2)}, u32[]{:S(2)}) collective-permute-start(bf16[64,1408]{1,0:T(8,128)(2,1)S(1)} %copy-done.11), channel_id=1, source_target_pairs={{0,8},{4,12},{8,0},{12,4},{1,9},{5,13},{9,1},{13,5},{2,10},{6,14},... | collective-permute-start | bytes 540680 | tf_op jit(solution)/shard_map/ppermute | solution.py:195
  176.4 14.5 %collective-permute-start.22 = (bf16[64,1408]{1,0:T(8,128)(2,1)S(1)}, bf16[64,1408]{1,0:T(8,128)(2,1)S(1)}, u32[]{:S(2)}, u32[]{:S(2)}) collective-permute-start(bf16[64,1408]{1,0:T(8,128)(2,1)S(1)} %copy-done.9), channel_id=1, source_target_pairs={{0,12},{4,0},{8,4},{12,8},{1,13},{5,1},{9,5},{13,9},{2,14},{6,2},{... | collective-permute-start | bytes 540680 | tf_op jit(solution)/shard_map/ppermute | solution.py:195
  191.0 18.3 %collective-permute-start.23 = (bf16[64,1408]{1,0:T(8,128)(2,1)S(1)}, bf16[64,1408]{1,0:T(8,128)(2,1)S(1)}, u32[]{:S(2)}, u32[]{:S(2)}) collective-permute-start(bf16[64,1408]{1,0:T(8,128)(2,1)S(1)} %add_convert_fusion.g0), channel_id=1, source_target_pairs={{0,4},{4,8},{8,12},{12,0},{1,5},{5,9},{9,13},{13,1},{2,6},{6,10},{... | collective-permute-start | bytes 540680 | tf_op jit(solution)/shard_map/ppermute | solution.py:195
  192.9 22.0 %collective-permute-start.24 = (bf16[64,1408]{1,0:T(8,128)(2,1)S(1)}, bf16[64,1408]{1,0:T(8,128)(2,1)S(1)}, u32[]{:S(2)}, u32[]{:S(2)}) collective-permute-start(bf16[64,1408]{1,0:T(8,128)(2,1)S(1)} %add_convert_fusion.g0), channel_id=1, source_target_pairs={{0,8},{4,12},{8,0},{12,4},{1,9},{5,13},{9,1},{13,5},{2,10},{6,14},... | collective-permute-start | bytes 540680 | tf_op jit(solution)/shard_map/ppermute | solution.py:195
  196.2 18.7 %collective-permute-start.25 = (bf16[64,1408]{1,0:T(8,128)(2,1)S(1)}, bf16[64,1408]{1,0:T(8,128)(2,1)S(1)}, u32[]{:S(2)}, u32[]{:S(2)}) collective-permute-start(bf16[64,1408]{1,0:T(8,128)(2,1)S(1)} %add_convert_fusion.g0), channel_id=1, source_target_pairs={{0,12},{4,0},{8,4},{12,8},{1,13},{5,1},{9,5},{13,9},{2,14},{6,2},{... | collective-permute-start | bytes 540680 | tf_op jit(solution)/shard_map/ppermute | solution.py:195
  203.9 17.0 %collective-permute-start.27 = (bf16[352,256]{1,0:T(8,128)(2,1)S(1)}, bf16[352,256]{1,0:T(8,128)(2,1)S(1)}, u32[]{:S(2)}, u32[]{:S(2)}) collective-permute-start(bf16[352,256]{1,0:T(8,128)(2,1)S(1)} %slice.33), channel_id=1, source_target_pairs={{0,2},{2,0},{1,3},{3,1},{4,6},{6,4},{5,7},{7,5},{8,10},{10,8},{9,1... | collective-permute-start | bytes 540680 | tf_op jit(solution)/shard_map/ppermute | solution.py:200
  214.9 6.0 %copy-start.20 = (bf16[352,512]{1,0:T(8,128)(2,1)S(1)}, bf16[352,512]{1,0:T(8,128)(2,1)}, u32[]{:S(2)}) copy-start(bf16[352,512]{1,0:T(8,128)(2,1)} %reduce-scatter.2.cloned.1.call-done) | copy-start | bytes 1081348
  220.3 0.7 copy-start.4
  221.0 23.8 %copy-start.5 = (bf16[64,1408]{1,0:T(8,128)(2,1)S(1)}, bf16[64,1408]{1,0:T(8,128)(2,1)}, u32[]{:S(2)}) copy-start(bf16[64,1408]{1,0:T(8,128)(2,1)} %copy-done.4) | copy-start | bytes 540676
  221.0 23.7 %collective-permute-start.28 = (bf16[64,1408]{1,0:T(8,128)(2,1)}, bf16[64,1408]{1,0:T(8,128)(2,1)S(1)}, u32[]{:S(2)}, u32[]{:S(2)}) collective-permute-start(bf16[64,1408]{1,0:T(8,128)(2,1)} %get-tuple-element.75), channel_id=1, source_target_pairs={{0,4},{4,8},{8,12},{12,0},{1,5},{5,9},{9,13},{13,1},{2,6},{6,10},{... | collective-permute-start | bytes 540680 | tf_op jit(solution)/shard_map/ppermute | solution.py:195
  223.1 21.6 %collective-permute-start.29 = (bf16[64,1408]{1,0:T(8,128)(2,1)}, bf16[64,1408]{1,0:T(8,128)(2,1)S(1)}, u32[]{:S(2)}, u32[]{:S(2)}) collective-permute-start(bf16[64,1408]{1,0:T(8,128)(2,1)} %get-tuple-element.76), channel_id=1, source_target_pairs={{0,8},{4,12},{8,0},{12,4},{1,9},{5,13},{9,1},{13,5},{2,10},{6,14},... | collective-permute-start | bytes 540680 | tf_op jit(solution)/shard_map/ppermute | solution.py:195
  227.8 16.9 %collective-permute-start.30 = (bf16[64,1408]{1,0:T(8,128)(2,1)}, bf16[64,1408]{1,0:T(8,128)(2,1)S(1)}, u32[]{:S(2)}, u32[]{:S(2)}) collective-permute-start(bf16[64,1408]{1,0:T(8,128)(2,1)} %get-tuple-element.77), channel_id=1, source_target_pairs={{0,12},{4,0},{8,4},{12,8},{1,13},{5,1},{9,5},{13,9},{2,14},{6,2},{... | collective-permute-start | bytes 540680 | tf_op jit(solution)/shard_map/ppermute | solution.py:195
  232.4 22.1 %all-to-all-start = ((bf16[8,44,256]{2,1,0:T(8,128)(2,1)}), bf16[8,44,256]{2,1,0:T(8,128)(2,1)S(1)}, u32[]{:S(2)}, u32[]{:S(2)}) async-start(bf16[8,44,256]{2,1,0:T(8,128)(2,1)} %reshape.58), calls=%async_computation.1 | async-start | bytes 393216 | tf_op jit(solution)/shard_map/all_to_all | solution.py:357
Sparse Core Ops, SparseCore 0:
  65.5 35.8 all-gather.1
  170.2 32.6 reduce-scatter.1

commit v4 on v3

--- a/solution.py
+++ b/solution.py
@@ -114,9 +114,8 @@
         out[...] = value[k * rows : (k + 1) * rows]
 
 
-def query_kernel(c0, c1, c2, c3, p0, p1, p2, p3, query, d_attn, w, sems):
-    captions = (c0, c1, c2, c3)
-    dec = c0.shape[-1]
+def query_kernel(caption, p0, p1, p2, p3, query, d_attn, w, sems):
+    dec = caption.shape[-1]
     skip = p0.shape[1] - dec
     copies = [
         pltpu.make_async_copy(p.at[:, pl.ds(skip, dec)], w.at[k], sems.at[k])
@@ -124,8 +123,7 @@
     ]
     for copy in copies:
         copy.start()
-    text = jnp.concatenate([c[0] for c in captions], axis=0)
-    cot = jnp.concatenate([c[1] for c in captions], axis=0)
+    text, cot = caption[0], caption[1]
     for k, copy in enumerate(copies):
         copy.wait()
         query[k] = (dot_last(text, w[k, :HEAD_DIM]) * HEAD_DIM ** (-0.5)).astype(BF)
@@ -261,12 +259,9 @@
     heads_near = swap(after(heads_own, far), "core")
 
     text_normed = layer_norm(text_in, query_gain)[0].astype(BF)
-    both = after(jnp.stack([text_normed, cotangent], axis=1), far)
-    both = both.reshape((2, 2) + both.shape[1:])
-    core, yh = lax.axis_index("core"), lax.axis_index("yh")
-    pick = functools.partial(lax.dynamic_index_in_dim, keepdims=False)
-    near = jnp.concatenate([pick(both, core, 1), swap(pick(both, 1 - core, 1), "core")], axis=2)
-    caption = jnp.concatenate([pick(near, yh, 0), swap(pick(near, 1 - yh, 0), "yh")], axis=1)
+    both = after(jnp.stack([text_normed, cotangent], axis=1), piece)
+    sent = jnp.broadcast_to(both, (PARTS,) + both.shape).reshape((-1,) + both.shape[1:])
+    caption = lax.all_to_all(sent, ("tensor", "yh", "core"), 0, 0, tiled=True)
 
     act, slope, in_rows = pl.pallas_call(
         up_kernel,
@@ -291,25 +286,24 @@
         scratch_shapes=[pltpu.VMEM((width, hidden), BF), dma((COPIES,))],
         compiler_params=PARAMS,
     )(place, act, *weights)
-    captions = gather_blocks(caption)
-    *branch, c0, c1, c2, c3 = lax.optimization_barrier((*branch, *captions))
-    captions = (c0, c1, c2, c3)
+    *branch, caption = lax.optimization_barrier((*branch, caption))
+    caption = jnp.swapaxes(caption, 0, 1).reshape(2, -1, dec)
     encoded_rows = (in_rows.astype(F32) + add_blocks(send_blocks(branch))).astype(BF)
     encoded_blocks = gather_blocks(encoded_rows)
 
     heads_far = lax.all_gather(after(heads_piece, far), "x", axis=0, tiled=True)
     heads = (heads_own, heads_near, heads_far, swap(after(heads_far, encoded_rows), "core"))
 
-    head_shape = shape((4, PARTS * caption.shape[1], HEAD_DIM), BF)
+    head_shape = shape((4, caption.shape[1], HEAD_DIM), BF)
     query, d_attn = pl.pallas_call(
         query_kernel,
         name="query",
         out_shape=[head_shape, head_shape],
-        in_specs=[VMEM] * PARTS + [ANY] * 4,
+        in_specs=[VMEM] + [ANY] * 4,
         out_specs=[VMEM] * 2,
         scratch_shapes=[pltpu.VMEM((4, 2 * HEAD_DIM, dec), BF), dma((4,))],
         compiler_params=PARAMS,
-    )(*captions, *heads)
+    )(caption, *heads)
     *term, encoded, d_pair = pl.pallas_call(
         attention_kernel,
         name="attention",

time: 282 us -> 272 us (0.965)
  the two profiles are of different devices: /device:TPU:56 before, /device:TPU:4 now
where the time goes in v4:
time: 272 us; the launch traced here: 270 us
  starting transfers between devices  127 us (47%)
  waiting for transfers between devices  59.2 us (22%)
  local copies, waits for them, and re-layouts  22 us (8%)
  Pallas kernels  21.5 us (8%)
  blocking collectives  17 us (6%)
  between operations  14.8 us (5%)
  other arithmetic  6.66 us (2%)
    ppermute x18, starting transfers between devices, shift(): lax.ppermute(value, axis, [(i, (i + by) % size) for i in range(size)])  75.1 us
    ppermute x8, starting transfers between devices, swap(): return lax.ppermute(value, axis, [(i, i ^ bit) for i in range(size)])  36.5 us
    ppermute x18, waiting for transfers between devices, shift(): lax.ppermute(value, axis, [(i, (i + by) % size) for i in range(size)])  27.9 us
    all_gather x1, blocking collectives, local(): lax.all_gather(image_rows, 'tensor', axis=0, tiled=True)  17 us
    ppermute x8, waiting for transfers between devices, swap(): return lax.ppermute(value, axis, [(i, i ^ bit) for i in range(size)])  16.6 us
    unnamed x63, local copies, waits for them, and re-layouts  14.5 us
    all_to_all x1, starting transfers between devices, local(): sums = lax.all_to_all(sums, ('zh', 'zl'), 0, 0, tiled=True)  10.3 us
    all_to_all x1, waiting for transfers between devices, local(): sums = lax.all_to_all(sums, ('zh', 'zl'), 0, 0, tiled=True)  9.58 us
  transfers between devices with their start and end apart: 30, of which 13 were waited for; matrix products, arithmetic and copies ran while one was open for 5% of the time, Pallas kernels for 6%

profile of v4, /device:TPU:4, one launch (start us, length us, event | category | flops | bytes accessed | tf_op | source)
XLA Modules:
  0.0 270.2 jit_solution(10118042087972791925)
XLA Ops:
  7.3 1.0 constant_dynamic-slice_fusion.1
  8.3 0.9 dynamic-slice_bitcast_fusion
  10.0 7.7 %collective-permute-start.1 = (bf16[704,256]{1,0:T(8,128)(2,1)}, bf16[704,256]{1,0:T(8,128)(2,1)}, u32[]{:S(2)}, u32[]{:S(2)}) collective-permute-start(bf16[704,256]{1,0:T(8,128)(2,1)} %pad_maximum_fusion.1), channel_id=1, source_target_pairs={{0,2},{2,0},{1,3},{3,1},{4,6},{6,4},{5,7},{7,5},{8,10},{10,8},{9,1... | collective-permute-start | bytes 1081352 | tf_op jit(solution)/shard_map/ppermute | solution.py:198
  18.6 1.2 maximum_maximum_fusion.p0
  20.0 10.1 %collective-permute-done.1 = bf16[704,256]{1,0:T(8,128)(2,1)} collective-permute-done((bf16[704,256]{1,0:T(8,128)(2,1)}, bf16[704,256]{1,0:T(8,128)(2,1)}, u32[]{:S(2)}, u32[]{:S(2)}) %collective-permute-start.1) | collective-permute-done | bytes 360480 | tf_op jit(solution)/shard_map/ppermute | solution.py:198
  30.1 2.4 collective-permute-start.2
  32.5 4.6 %collective-permute-start.3 = (bf16[704,256]{1,0:T(8,128)(2,1)}, bf16[704,256]{1,0:T(8,128)(2,1)S(1)}, u32[]{:S(2)}, u32[]{:S(2)}) collective-permute-start(bf16[704,256]{1,0:T(8,128)(2,1)} %collective-permute-done.1), channel_id=1, source_target_pairs={{0,256},{128,384},{256,0},{384,128},{1,257},{129,385},{257,1},{385... | collective-permute-start | bytes 1081352 | tf_op jit(solution)/shard_map/ppermute | solution.py:193
  37.2 11.6 %collective-permute-start.13 = (bf16[64,3456]{1,0:T(8,128)(2,1)S(1)}, bf16[64,3456]{1,0:T(8,128)(2,1)S(1)}, u32[]{:S(2)}, u32[]{:S(2)}) collective-permute-start(bf16[64,3456]{1,0:T(8,128)(2,1)S(1)} %constant_dynamic-slice_fusion), channel_id=1, source_target_pairs={{0,2},{2,0},{1,3},{3,1},{4,6},{6,4},{5,7},{7,5},{8,10},{10,8},{9,1... | collective-permute-start | bytes 1327112 | tf_op jit(solution)/shard_map/ppermute | solution.py:198
  48.9 4.3 %collective-permute-start.4 = (bf16[704,256]{1,0:T(8,128)(2,1)}, bf16[704,256]{1,0:T(8,128)(2,1)S(1)}, u32[]{:S(2)}, u32[]{:S(2)}) collective-permute-start(bf16[704,256]{1,0:T(8,128)(2,1)} %collective-permute-done.1), channel_id=1, source_target_pairs={{0,16},{16,32},{32,48},{48,64},{64,80},{80,96},{96,112},{112,0},{1... | collective-permute-start | bytes 1081352 | tf_op jit(solution)/shard_map/ppermute | solution.py:193
  53.2 1.8 constant_dynamic-update-slice_fusion.3
  55.0 0.8 constant_dynamic-update-slice_fusion.2
  55.8 0.8 constant_dynamic-update-slice_fusion.1
  56.6 8.8 %collective-permute-done.4 = bf16[704,256]{1,0:T(8,128)(2,1)S(1)} collective-permute-done((bf16[704,256]{1,0:T(8,128)(2,1)}, bf16[704,256]{1,0:T(8,128)(2,1)S(1)}, u32[]{:S(2)}, u32[]{:S(2)}) %collective-permute-start.4) | collective-permute-done | bytes 360480 | tf_op jit(solution)/shard_map/ppermute | solution.py:193
  65.4 0.8 constant_dynamic-update-slice_fusion.w2
  67.2 1.1 broadcast_in_dim.2
  68.3 4.7 %all-to-all-start = ((bf16[16,2,8,2048]{3,2,1,0:T(8,128)(2,1)}), bf16[16,2,8,2048]{3,2,1,0:T(8,128)(2,1)}, u32[]{:S(2)}, u32[]{:S(2)}) async-start(bf16[16,2,8,2048]{3,2,1,0:T(8,128)(2,1)} %bitcast.8), calls=%async_computation | async-start | bytes 2097152 | tf_op jit(solution)/shard_map/all_to_all | solution.py:264
  73.1 1.4 pad_maximum_fusion.w0
  74.5 2.3 collective-permute-start
  76.8 2.1 collective-permute-start.5
  79.8 2.5 collective-permute-done.5.w3
  82.3 1.1 copy-done.2
  83.4 5.0 %encoder_up.1 = (bf16[256,1024]{1,0:T(8,128)(2,1)S(1)}, f32[256,1024]{1,0:T(8,128)S(1)}, bf16[64,1408]{1,0:T(8,128)(2,1)S(1)}) custom-call(s32[3]{0:T(128)S(1)} %pad_add_fusion.place, bf16[256,1408]{1,0:T(8,128)(2,1)S(1)} %bitcast.22, f32[1,1408]{1,0:T(1,128)S(1)} %reshape.59.gain, bf16[704,1024]{1,0:T(8,128)(2,1)S(1)} %pad_maximum_fusion.w0, ...), custom_call_target="tpu_custom_call" | custom-call | tf_op jit(solution)/shard_map/encoder_up/pallas_call | solution.py:266
  88.4 1.0 copy-done
  89.4 3.5 %encoder_down.1 = (bf16[64,1408]{1,0:T(8,128)(2,1)S(1)}, bf16[64,1408]{1,0:T(8,128)(2,1)S(1)}, bf16[64,1408]{1,0:T(8,128)(2,1)S(1)}, bf16[64,1408]{1,0:T(8,128)(2,1)S(1)}) custom-call(s32[3]{0:T(128)S(1)} %pad_add_fusion.place, bf16[256,1024]{1,0:T(8,128)(2,1)S(1)} %get-tuple-element.40.act, bf16[704,1024]{1,0:T(8,128)(2,1)S(1)} %pad_maximum_fusion.w0, ...), custom_call_target="tpu_custom_call" | custom-call | tf_op jit(solution)/shard_map/encoder_down/pallas_call | solution.py:280
  95.6 5.1 %all-to-all-done = bf16[16,2,8,2048]{3,2,1,0:T(8,128)(2,1)} async-done(((bf16[16,2,8,2048]{3,2,1,0:T(8,128)(2,1)}), bf16[16,2,8,2048]{3,2,1,0:T(8,128)(2,1)}, u32[]{:S(2)}, u32[]{:S(2)}) %all-to-all-start) | async-done | bytes 1048608 | tf_op jit(solution)/shard_map/all_to_all | solution.py:264
  100.7 1.9 collective-permute-start.6
  102.6 4.4 %collective-permute-start.7 = (bf16[64,1408]{1,0:T(8,128)(2,1)}, bf16[64,1408]{1,0:T(8,128)(2,1)S(1)}, u32[]{:S(2)}, u32[]{:S(2)}) collective-permute-start(bf16[64,1408]{1,0:T(8,128)(2,1)} %copy-done.16), channel_id=1, source_target_pairs={{0,8},{4,12},{8,0},{12,4},{1,9},{5,13},{9,1},{13,5},{2,10},{6,14},... | collective-permute-start | bytes 540680 | tf_op jit(solution)/shard_map/ppermute | solution.py:193
  107.0 4.8 %collective-permute-start.8 = (bf16[64,1408]{1,0:T(8,128)(2,1)}, bf16[64,1408]{1,0:T(8,128)(2,1)S(1)}, u32[]{:S(2)}, u32[]{:S(2)}) collective-permute-start(bf16[64,1408]{1,0:T(8,128)(2,1)} %copy-done.15), channel_id=1, source_target_pairs={{0,12},{4,0},{8,4},{12,8},{1,13},{5,1},{9,5},{13,9},{2,14},{6,2},{... | collective-permute-start | bytes 540680 | tf_op jit(solution)/shard_map/ppermute | solution.py:193
  111.8 1.9 collective-permute-start.12
  113.7 5.4 %collective-permute-done.7 = bf16[64,1408]{1,0:T(8,128)(2,1)S(1)} collective-permute-done((bf16[64,1408]{1,0:T(8,128)(2,1)}, bf16[64,1408]{1,0:T(8,128)(2,1)S(1)}, u32[]{:S(2)}, u32[]{:S(2)}) %collective-permute-start.7) | collective-permute-done | bytes 180256 | tf_op jit(solution)/shard_map/ppermute | solution.py:193
  119.5 1.8 fusion.11
  121.3 1.9 collective-permute-start.14
  123.2 5.2 %collective-permute-start.10 = (bf16[64,1408]{1,0:T(8,128)(2,1)}, bf16[64,1408]{1,0:T(8,128)(2,1)S(1)}, u32[]{:S(2)}, u32[]{:S(2)}) collective-permute-start(bf16[64,1408]{1,0:T(8,128)(2,1)} %get-tuple-element.82.e0), channel_id=1, source_target_pairs={{0,8},{4,12},{8,0},{12,4},{1,9},{5,13},{9,1},{13,5},{2,10},{6,14},... | collective-permute-start | bytes 540680 | tf_op jit(solution)/shard_map/ppermute | solution.py:193
  128.4 5.2 %collective-permute-start.11 = (bf16[64,1408]{1,0:T(8,128)(2,1)}, bf16[64,1408]{1,0:T(8,128)(2,1)S(1)}, u32[]{:S(2)}, u32[]{:S(2)}) collective-permute-start(bf16[64,1408]{1,0:T(8,128)(2,1)} %get-tuple-element.82.e0), channel_id=1, source_target_pairs={{0,12},{4,0},{8,4},{12,8},{1,13},{5,1},{9,5},{13,9},{2,14},{6,2},{... | collective-permute-start | bytes 540680 | tf_op jit(solution)/shard_map/ppermute | solution.py:193
  133.6 1.9 collective-permute-start.9
  135.6 1.3 copy_bitcast_fusion.caption
  136.9 1.2 copy-done.18
  138.2 2.7 query.1
  140.9 3.7 %collective-permute-done.9.e1 = bf16[64,1408]{1,0:T(8,128)(2,1)S(1)} collective-permute-done((bf16[64,1408]{1,0:T(8,128)(2,1)}, bf16[64,1408]{1,0:T(8,128)(2,1)S(1)}, u32[]{:S(2)}, u32[]{:S(2)}) %collective-permute-start.9) | collective-permute-done | bytes 180256 | tf_op jit(solution)/shard_map/ppermute | solution.py:193
  144.6 5.0 %attention.1 = (bf16[64,1408]{1,0:T(8,128)(2,1)S(1)}, bf16[64,1408]{1,0:T(8,128)(2,1)S(1)}, bf16[64,1408]{1,0:T(8,128)(2,1)S(1)}, bf16[64,1408]{1,0:T(8,128)(2,1...) custom-call(bf16[64,1408]{1,0:T(8,128)(2,1)S(1)} %copy-done.3, ...), custom_call_target="tpu_custom_call" | custom-call | tf_op jit(solution)/shard_map/attention/pallas_call | solution.py:307
  150.5 1.9 collective-permute-start.21
  152.4 3.2 %collective-permute-done.21 = bf16[1408,512]{1,0:T(8,128)(2,1)S(1)} collective-permute-done((bf16[1408,512]{1,0:T(8,128)(2,1)S(1)}, bf16[1408,512]{1,0:T(8,128)(2,1)S(1)}, u32[]{:S(2)}, u32[]{:S(2)}) %collective-permute-start.21) | collective-permute-done | bytes 1441824 | tf_op jit(solution)/shard_map/ppermute | solution.py:198
  155.6 1.7 fusion
  157.3 0.9 copy-done.14
  158.2 3.5 %collective-permute-start.15 = (bf16[64,1408]{1,0:T(8,128)(2,1)S(1)}, bf16[64,1408]{1,0:T(8,128)(2,1)S(1)}, u32[]{:S(2)}, u32[]{:S(2)}) collective-permute-start(bf16[64,1408]{1,0:T(8,128)(2,1)S(1)} %copy-done.14), channel_id=1, source_target_pairs={{0,4},{4,8},{8,12},{12,0},{1,5},{5,9},{9,13},{13,1},{2,6},{6,10},{... | collective-permute-start | bytes 540680 | tf_op jit(solution)/shard_map/ppermute | solution.py:193
  161.7 5.3 %collective-permute-start.16 = (bf16[64,1408]{1,0:T(8,128)(2,1)S(1)}, bf16[64,1408]{1,0:T(8,128)(2,1)S(1)}, u32[]{:S(2)}, u32[]{:S(2)}) collective-permute-start(bf16[64,1408]{1,0:T(8,128)(2,1)S(1)} %copy-done.12), channel_id=1, source_target_pairs={{0,8},{4,12},{8,0},{12,4},{1,9},{5,13},{9,1},{13,5},{2,10},{6,14},... | collective-permute-start | bytes 540680 | tf_op jit(solution)/shard_map/ppermute | solution.py:193
  167.1 3.4 %collective-permute-start.17 = (bf16[64,1408]{1,0:T(8,128)(2,1)S(1)}, bf16[64,1408]{1,0:T(8,128)(2,1)S(1)}, u32[]{:S(2)}, u32[]{:S(2)}) collective-permute-start(bf16[64,1408]{1,0:T(8,128)(2,1)S(1)} %copy-done.10), channel_id=1, source_target_pairs={{0,12},{4,0},{8,4},{12,8},{1,13},{5,1},{9,5},{13,9},{2,14},{6,2},{... | collective-permute-start | bytes 540680 | tf_op jit(solution)/shard_map/ppermute | solution.py:193
  170.5 6.6 %collective-permute-done.16 = bf16[64,1408]{1,0:T(8,128)(2,1)S(1)} collective-permute-done((bf16[64,1408]{1,0:T(8,128)(2,1)S(1)}, bf16[64,1408]{1,0:T(8,128)(2,1)S(1)}, u32[]{:S(2)}, u32[]{:S(2)}) %collective-permute-start.16) | collective-permute-done | bytes 180256 | tf_op jit(solution)/shard_map/ppermute | solution.py:193
  177.1 1.7 collective-permute-done.17
  178.9 4.6 %collective-permute-start.18 = (bf16[64,1408]{1,0:T(8,128)(2,1)S(1)}, bf16[64,1408]{1,0:T(8,128)(2,1)S(1)}, u32[]{:S(2)}, u32[]{:S(2)}) collective-permute-start(bf16[64,1408]{1,0:T(8,128)(2,1)S(1)} %add_convert_fusion.g0), channel_id=1, source_target_pairs={{0,4},{4,8},{8,12},{12,0},{1,5},{5,9},{9,13},{13,1},{2,6},{6,10},{... | collective-permute-start | bytes 540680 | tf_op jit(solution)/shard_map/ppermute | solution.py:193
  183.4 3.6 %collective-permute-start.19 = (bf16[64,1408]{1,0:T(8,128)(2,1)S(1)}, bf16[64,1408]{1,0:T(8,128)(2,1)S(1)}, u32[]{:S(2)}, u32[]{:S(2)}) collective-permute-start(bf16[64,1408]{1,0:T(8,128)(2,1)S(1)} %add_convert_fusion.g0), channel_id=1, source_target_pairs={{0,8},{4,12},{8,0},{12,4},{1,9},{5,13},{9,1},{13,5},{2,10},{6,14},... | collective-permute-start | bytes 540680 | tf_op jit(solution)/shard_map/ppermute | solution.py:193
  187.1 2.5 collective-permute-start.20
  189.7 0.9 slice.33
  190.6 7.1 %collective-permute-start.22 = (bf16[352,256]{1,0:T(8,128)(2,1)S(1)}, bf16[352,256]{1,0:T(8,128)(2,1)S(1)}, u32[]{:S(2)}, u32[]{:S(2)}) collective-permute-start(bf16[352,256]{1,0:T(8,128)(2,1)S(1)} %slice.33), channel_id=1, source_target_pairs={{0,2},{2,0},{1,3},{3,1},{4,6},{6,4},{5,7},{7,5},{8,10},{10,8},{9,1... | collective-permute-start | bytes 540680 | tf_op jit(solution)/shard_map/ppermute | solution.py:198
  198.0 1.3 collective-permute-done.20.g3
  199.9 0.9 copy-done.8
  200.9 5.3 %encoder_back.1 = (bf16[64,1408]{1,0:T(8,128)(2,1)S(1)}, bf16[64,1408]{1,0:T(8,128)(2,1)}, bf16[64,1408]{1,0:T(8,128)(2,1)}, bf16[64,1408]{1,0:T(8,128)(2,1)}) custom-call(s32[3]{0:T(128)S(1)} %pad_add_fusion.place, bf16[64,1408]{1,0:T(8,128)(2,1)S(1)} %add_convert_fusion.g0, bf16[64,1408]{1,0:T(8,128)(2,1)S(1)} %collective-permute-done.18.g1, ...), custom_call_target="tpu_custom_call" | custom-call | tf_op jit(solution)/shard_map/encoder_back/pallas_call | solution.py:333
  206.3 11.2 %collective-permute-start.23 = (bf16[64,1408]{1,0:T(8,128)(2,1)}, bf16[64,1408]{1,0:T(8,128)(2,1)S(1)}, u32[]{:S(2)}, u32[]{:S(2)}) collective-permute-start(bf16[64,1408]{1,0:T(8,128)(2,1)} %get-tuple-element.69), channel_id=1, source_target_pairs={{0,4},{4,8},{8,12},{12,0},{1,5},{5,9},{9,13},{13,1},{2,6},{6,10},{... | collective-permute-start | bytes 540680 | tf_op jit(solution)/shard_map/ppermute | solution.py:193
  217.5 3.9 %collective-permute-start.24 = (bf16[64,1408]{1,0:T(8,128)(2,1)}, bf16[64,1408]{1,0:T(8,128)(2,1)S(1)}, u32[]{:S(2)}, u32[]{:S(2)}) collective-permute-start(bf16[64,1408]{1,0:T(8,128)(2,1)} %get-tuple-element.70), channel_id=1, source_target_pairs={{0,8},{4,12},{8,0},{12,4},{1,9},{5,13},{9,1},{13,5},{2,10},{6,14},... | collective-permute-start | bytes 540680 | tf_op jit(solution)/shard_map/ppermute | solution.py:193
  221.4 2.3 collective-permute-start.25
  224.4 10.3 %all-to-all-start.1 = ((bf16[8,44,256]{2,1,0:T(8,128)(2,1)}), bf16[8,44,256]{2,1,0:T(8,128)(2,1)S(1)}, u32[]{:S(2)}, u32[]{:S(2)}) async-start(bf16[8,44,256]{2,1,0:T(8,128)(2,1)} %reshape.62), calls=%async_computation.2 | async-start | bytes 393216 | tf_op jit(solution)/shard_map/all_to_all | solution.py:351
  235.2 9.6 %all-to-all-done.1 = bf16[8,44,256]{2,1,0:T(8,128)(2,1)S(1)} async-done(((bf16[8,44,256]{2,1,0:T(8,128)(2,1)}), bf16[8,44,256]{2,1,0:T(8,128)(2,1)S(1)}, u32[]{:S(2)}, u32[]{:S(2)}) %all-to-all-start.1) | async-done | bytes 180256 | tf_op jit(solution)/shard_map/all_to_all | solution.py:351
  244.8 17.0 %all_gather.7 = bf16[256,1408]{1,0:T(8,128)(2,1)S(1)} all-gather(bf16[64,1408]{1,0:T(8,128)(2,1)S(1)} %fusion.9), channel_id=1, replica_groups=mesh['x'=4,'zh'=2,'zl'=4,'tensor'=4,'yh'=2,'core'=2] {'tensor'}, dimensions={0}, use_global_device_ids=true | all-gather | bytes 901120 | tf_op jit(solution)/shard_map/all_gather | solution.py:364
  262.5 0.9 copy.30
  (102 shorter events, 10.5 us)
Async XLA Ops:
  7.2 10.6 %copy-start.19 = (bf16[4,8,2048]{2,1,0:T(8,128)(2,1)S(1)}, bf16[4,8,2048]{2,1,0:T(8,128)(2,1)}, u32[]{:S(2)}) copy-start(bf16[4,8,2048]{2,1,0:T(8,128)(2,1)} %param.15) | copy-start | bytes 393220
  7.2 10.7 %copy-start.22 = (bf16[1408,128]{1,0:T(8,128)(2,1)S(1)}, bf16[1408,128]{1,0:T(8,128)(2,1)}, u32[]{:S(2)}) copy-start(bf16[1408,128]{1,0:T(8,128)(2,1)} %param.18) | copy-start | bytes 1081348
  7.2 10.9 %copy-start.23 = (bf16[1408,128]{1,0:T(8,128)(2,1)S(1)}, bf16[1408,128]{1,0:T(8,128)(2,1)}, u32[]{:S(2)}) copy-start(bf16[1408,128]{1,0:T(8,128)(2,1)} %param.19) | copy-start | bytes 1081348
  7.2 114.1 %all-gather.2.cloned.1.call-start = ((), (), s32[]{:S(2)}) async-start(), calls=%async_computation.3 | async-start | bytes 2211840 | tf_op jit(solution)/shard_map/all_gather | solution.py:294
  7.3 11.0 %copy-start.20 = (bf16[2048,128]{1,0:T(8,128)(2,1)S(1)}, bf16[2048,128]{1,0:T(8,128)(2,1)}, u32[]{:S(2)}) copy-start(bf16[2048,128]{1,0:T(8,128)(2,1)} %param.17) | copy-start | bytes 1572868
  10.0 20.1 %collective-permute-start.1 = (bf16[704,256]{1,0:T(8,128)(2,1)}, bf16[704,256]{1,0:T(8,128)(2,1)}, u32[]{:S(2)}, u32[]{:S(2)}) collective-permute-start(bf16[704,256]{1,0:T(8,128)(2,1)} %pad_maximum_fusion.1), channel_id=1, source_target_pairs={{0,2},{2,0},{1,3},{3,1},{4,6},{6,4},{5,7},{7,5},{8,10},{10,8},{9,1... | collective-permute-start | bytes 1081352 | tf_op jit(solution)/shard_map/ppermute | solution.py:198
  30.1 24.9 %collective-permute-start.2 = (bf16[704,256]{1,0:T(8,128)(2,1)}, bf16[704,256]{1,0:T(8,128)(2,1)S(1)}, u32[]{:S(2)}, u32[]{:S(2)}) collective-permute-start(bf16[704,256]{1,0:T(8,128)(2,1)} %collective-permute-done.1), channel_id=1, source_target_pairs={{0,384},{128,0},{256,128},{384,256},{1,385},{129,1},{257,129},{385... | collective-permute-start | bytes 1081352 | tf_op jit(solution)/shard_map/ppermute | solution.py:193
  32.5 23.3 %collective-permute-start.3 = (bf16[704,256]{1,0:T(8,128)(2,1)}, bf16[704,256]{1,0:T(8,128)(2,1)S(1)}, u32[]{:S(2)}, u32[]{:S(2)}) collective-permute-start(bf16[704,256]{1,0:T(8,128)(2,1)} %collective-permute-done.1), channel_id=1, source_target_pairs={{0,256},{128,384},{256,0},{384,128},{1,257},{129,385},{257,1},{385... | collective-permute-start | bytes 1081352 | tf_op jit(solution)/shard_map/ppermute | solution.py:193
  37.2 29.0 %collective-permute-start.13 = (bf16[64,3456]{1,0:T(8,128)(2,1)S(1)}, bf16[64,3456]{1,0:T(8,128)(2,1)S(1)}, u32[]{:S(2)}, u32[]{:S(2)}) collective-permute-start(bf16[64,3456]{1,0:T(8,128)(2,1)S(1)} %constant_dynamic-slice_fusion), channel_id=1, source_target_pairs={{0,2},{2,0},{1,3},{3,1},{4,6},{6,4},{5,7},{7,5},{8,10},{10,8},{9,1... | collective-permute-start | bytes 1327112 | tf_op jit(solution)/shard_map/ppermute | solution.py:198
  48.9 16.6 %collective-permute-start.4 = (bf16[704,256]{1,0:T(8,128)(2,1)}, bf16[704,256]{1,0:T(8,128)(2,1)S(1)}, u32[]{:S(2)}, u32[]{:S(2)}) collective-permute-start(bf16[704,256]{1,0:T(8,128)(2,1)} %collective-permute-done.1), channel_id=1, source_target_pairs={{0,16},{16,32},{32,48},{48,64},{64,80},{80,96},{96,112},{112,0},{1... | collective-permute-start | bytes 1081352 | tf_op jit(solution)/shard_map/ppermute | solution.py:193
  55.0 12.1 %copy-start.27 = (f32[2048]{0:T(1024)S(1)}, f32[2048]{0:T(1024)}, u32[]{:S(2)}) copy-start(f32[2048]{0:T(1024)} %param.16) | copy-start | bytes 24580
  55.0 12.2 %copy-start.25 = (bf16[4,8,2048]{2,1,0:T(8,128)(2,1)S(1)}, bf16[4,8,2048]{2,1,0:T(8,128)(2,1)}, u32[]{:S(2)}) copy-start(bf16[4,8,2048]{2,1,0:T(8,128)(2,1)} %param.21) | copy-start | bytes 393220
  66.2 0.8 copy-start.21
  68.3 32.4 %all-to-all-start = ((bf16[16,2,8,2048]{3,2,1,0:T(8,128)(2,1)}), bf16[16,2,8,2048]{3,2,1,0:T(8,128)(2,1)}, u32[]{:S(2)}, u32[]{:S(2)}) async-start(bf16[16,2,8,2048]{3,2,1,0:T(8,128)(2,1)} %bitcast.8), calls=%async_computation | async-start | bytes 2097152 | tf_op jit(solution)/shard_map/all_to_all | solution.py:264
  73.0 116.7 %reduce-scatter.2.cloned.1.call-start = ((), (), s32[]{:S(2)}) async-start(), calls=%async_computation.4 | async-start | bytes 1802240 | tf_op jit(solution)/shard_map/reduce_scatter | solution.py:330
  73.1 5.8 %copy-start.26 = (f32[1408]{0:T(1024)S(1)}, f32[1408]{0:T(1024)}, u32[]{:S(2)}) copy-start(f32[1408]{0:T(1024)} %param.12) | copy-start | bytes 16900
  74.5 5.2 %collective-permute-start = (bf16[704,1024]{1,0:T(8,128)(2,1)S(1)}, bf16[704,1024]{1,0:T(8,128)(2,1)}, u32[]{:S(2)}, u32[]{:S(2)}) collective-permute-start(bf16[704,1024]{1,0:T(8,128)(2,1)S(1)} %pad_maximum_fusion.w0), channel_id=1, source_target_pairs={{0,1},{1,0},{2,3},{3,2},{4,5},{5,4},{6,7},{7,6},{8,9},{9,8},{10,11... | collective-permute-start | bytes 4325384 | tf_op jit(solution)/shard_map/ppermute | solution.py:198
  76.8 5.5 %collective-permute-start.5 = (bf16[704,1024]{1,0:T(8,128)(2,1)}, bf16[704,1024]{1,0:T(8,128)(2,1)}, u32[]{:S(2)}, u32[]{:S(2)}) collective-permute-start(bf16[704,1024]{1,0:T(8,128)(2,1)} %constant_dynamic-update-slice_fusion.w2), channel_id=1, source_target_pairs={{0,1},{1,0},{2,3},{3,2},{4,5},{5,4},{6,7},{7,6},{8,9},{9,8},{10,11... | collective-permute-start | bytes 4325384 | tf_op jit(solution)/shard_map/ppermute | solution.py:198
  82.2 1.1 copy-start.2
  88.4 1.0 copy-start
  92.9 0.7 copy-start.6
  93.5 0.7 copy-start.15
  94.2 0.7 copy-start.16
  94.9 0.7 copy-start.17
  100.7 13.0 %collective-permute-start.6 = (bf16[64,1408]{1,0:T(8,128)(2,1)}, bf16[64,1408]{1,0:T(8,128)(2,1)S(1)}, u32[]{:S(2)}, u32[]{:S(2)}) collective-permute-start(bf16[64,1408]{1,0:T(8,128)(2,1)} %copy-done.17), channel_id=1, source_target_pairs={{0,4},{4,8},{8,12},{12,0},{1,5},{5,9},{9,13},{13,1},{2,6},{6,10},{... | collective-permute-start | bytes 540680 | tf_op jit(solution)/shard_map/ppermute | solution.py:193
  102.6 16.5 %collective-permute-start.7 = (bf16[64,1408]{1,0:T(8,128)(2,1)}, bf16[64,1408]{1,0:T(8,128)(2,1)S(1)}, u32[]{:S(2)}, u32[]{:S(2)}) collective-permute-start(bf16[64,1408]{1,0:T(8,128)(2,1)} %copy-done.16), channel_id=1, source_target_pairs={{0,8},{4,12},{8,0},{12,4},{1,9},{5,13},{9,1},{13,5},{2,10},{6,14},... | collective-permute-start | bytes 540680 | tf_op jit(solution)/shard_map/ppermute | solution.py:193
  107.0 12.5 %collective-permute-start.8 = (bf16[64,1408]{1,0:T(8,128)(2,1)}, bf16[64,1408]{1,0:T(8,128)(2,1)S(1)}, u32[]{:S(2)}, u32[]{:S(2)}) collective-permute-start(bf16[64,1408]{1,0:T(8,128)(2,1)} %copy-done.15), channel_id=1, source_target_pairs={{0,12},{4,0},{8,4},{12,8},{1,13},{5,1},{9,5},{13,9},{2,14},{6,2},{... | collective-permute-start | bytes 540680 | tf_op jit(solution)/shard_map/ppermute | solution.py:193
  111.8 25.1 %collective-permute-start.12 = (bf16[256,3456]{1,0:T(8,128)(2,1)S(1)}, bf16[256,3456]{1,0:T(8,128)(2,1)}, u32[]{:S(2)}, u32[]{:S(2)}) collective-permute-start(bf16[256,3456]{1,0:T(8,128)(2,1)S(1)} %maximum_maximum_fusion.p0), channel_id=1, source_target_pairs={{0,1},{1,0},{2,3},{3,2},{4,5},{5,4},{6,7},{7,6},{8,9},{9,8},{10,11... | collective-permute-start | bytes 5308424 | tf_op jit(solution)/shard_map/ppermute | solution.py:198
  121.3 15.6 %collective-permute-start.14 = (bf16[256,3456]{1,0:T(8,128)(2,1)}, bf16[256,3456]{1,0:T(8,128)(2,1)S(1)}, u32[]{:S(2)}, u32[]{:S(2)}) collective-permute-start(bf16[256,3456]{1,0:T(8,128)(2,1)} %all-gather.2.cloned.1.call-done.p2), channel_id=1, source_target_pairs={{0,1},{1,0},{2,3},{3,2},{4,5},{5,4},{6,7},{7,6},{8,9},{9,8},{10,11... | collective-permute-start | bytes 5308424 | tf_op jit(solution)/shard_map/ppermute | solution.py:198
  123.2 17.6 %collective-permute-start.10 = (bf16[64,1408]{1,0:T(8,128)(2,1)}, bf16[64,1408]{1,0:T(8,128)(2,1)S(1)}, u32[]{:S(2)}, u32[]{:S(2)}) collective-permute-start(bf16[64,1408]{1,0:T(8,128)(2,1)} %get-tuple-element.82.e0), channel_id=1, source_target_pairs={{0,8},{4,12},{8,0},{12,4},{1,9},{5,13},{9,1},{13,5},{2,10},{6,14},... | collective-permute-start | bytes 540680 | tf_op jit(solution)/shard_map/ppermute | solution.py:193
  128.4 12.4 %collective-permute-start.11 = (bf16[64,1408]{1,0:T(8,128)(2,1)}, bf16[64,1408]{1,0:T(8,128)(2,1)S(1)}, u32[]{:S(2)}, u32[]{:S(2)}) collective-permute-start(bf16[64,1408]{1,0:T(8,128)(2,1)} %get-tuple-element.82.e0), channel_id=1, source_target_pairs={{0,12},{4,0},{8,4},{12,8},{1,13},{5,1},{9,5},{13,9},{2,14},{6,2},{... | collective-permute-start | bytes 540680 | tf_op jit(solution)/shard_map/ppermute | solution.py:193
  133.6 10.9 %collective-permute-start.9 = (bf16[64,1408]{1,0:T(8,128)(2,1)}, bf16[64,1408]{1,0:T(8,128)(2,1)S(1)}, u32[]{:S(2)}, u32[]{:S(2)}) collective-permute-start(bf16[64,1408]{1,0:T(8,128)(2,1)} %get-tuple-element.82.e0), channel_id=1, source_target_pairs={{0,4},{4,8},{8,12},{12,0},{1,5},{5,9},{9,13},{13,1},{2,6},{6,10},{... | collective-permute-start | bytes 540680 | tf_op jit(solution)/shard_map/ppermute | solution.py:193
  136.9 7.7 %copy-start.3 = (bf16[64,1408]{1,0:T(8,128)(2,1)S(1)}, bf16[64,1408]{1,0:T(8,128)(2,1)}, u32[]{:S(2)}) copy-start(bf16[64,1408]{1,0:T(8,128)(2,1)} %get-tuple-element.82.e0) | copy-start | bytes 540676
  136.9 1.2 copy-start.18
  149.6 0.7 copy-start.4
  149.6 0.7 copy-start.9
  149.6 0.8 copy-start.11
  149.7 0.8 copy-start.13
  150.5 5.1 %collective-permute-start.21 = (bf16[1408,512]{1,0:T(8,128)(2,1)S(1)}, bf16[1408,512]{1,0:T(8,128)(2,1)S(1)}, u32[]{:S(2)}, u32[]{:S(2)}) collective-permute-start(bf16[1408,512]{1,0:T(8,128)(2,1)S(1)} %convolution_convert_fusion), channel_id=1, source_target_pairs={{0,1},{1,0},{2,3},{3,2},{4,5},{5,4},{6,7},{7,6},{8,9},{9,8},{10,11... | collective-permute-start | bytes 4325384 | tf_op jit(solution)/shard_map/ppermute | solution.py:198
  157.3 0.9 copy-start.14
  157.3 4.4 %copy-start.12 = (bf16[64,1408]{1,0:T(8,128)(2,1)S(1)}, bf16[64,1408]{1,0:T(8,128)(2,1)}, u32[]{:S(2)}) copy-start(bf16[64,1408]{1,0:T(8,128)(2,1)} %copy-done.11) | copy-start | bytes 540676
  157.3 9.8 %copy-start.10 = (bf16[64,1408]{1,0:T(8,128)(2,1)S(1)}, bf16[64,1408]{1,0:T(8,128)(2,1)}, u32[]{:S(2)}) copy-start(bf16[64,1408]{1,0:T(8,128)(2,1)} %copy-done.9) | copy-start | bytes 540676
  157.3 21.5 %copy-start.5 = (bf16[64,1408]{1,0:T(8,128)(2,1)S(1)}, bf16[64,1408]{1,0:T(8,128)(2,1)}, u32[]{:S(2)}) copy-start(bf16[64,1408]{1,0:T(8,128)(2,1)} %copy-done.4) | copy-start | bytes 540676
  157.3 42.6 %copy-start.1 = (f32[256,1024]{1,0:T(8,128)S(1)}, f32[256,1024]{1,0:T(8,128)}, u32[]{:S(2)}) copy-start(f32[256,1024]{1,0:T(8,128)} %copy-done) | copy-start | bytes 3145732
  158.2 12.3 %collective-permute-start.15 = (bf16[64,1408]{1,0:T(8,128)(2,1)S(1)}, bf16[64,1408]{1,0:T(8,128)(2,1)S(1)}, u32[]{:S(2)}, u32[]{:S(2)}) collective-permute-start(bf16[64,1408]{1,0:T(8,128)(2,1)S(1)} %copy-done.14), channel_id=1, source_target_pairs={{0,4},{4,8},{8,12},{12,0},{1,5},{5,9},{9,13},{13,1},{2,6},{6,10},{... | collective-permute-start | bytes 540680 | tf_op jit(solution)/shard_map/ppermute | solution.py:193
  161.7 15.3 %collective-permute-start.16 = (bf16[64,1408]{1,0:T(8,128)(2,1)S(1)}, bf16[64,1408]{1,0:T(8,128)(2,1)S(1)}, u32[]{:S(2)}, u32[]{:S(2)}) collective-permute-start(bf16[64,1408]{1,0:T(8,128)(2,1)S(1)} %copy-done.12), channel_id=1, source_target_pairs={{0,8},{4,12},{8,0},{12,4},{1,9},{5,13},{9,1},{13,5},{2,10},{6,14},... | collective-permute-start | bytes 540680 | tf_op jit(solution)/shard_map/ppermute | solution.py:193
  167.1 11.7 %collective-permute-start.17 = (bf16[64,1408]{1,0:T(8,128)(2,1)S(1)}, bf16[64,1408]{1,0:T(8,128)(2,1)S(1)}, u32[]{:S(2)}, u32[]{:S(2)}) collective-permute-start(bf16[64,1408]{1,0:T(8,128)(2,1)S(1)} %copy-done.10), channel_id=1, source_target_pairs={{0,12},{4,0},{8,4},{12,8},{1,13},{5,1},{9,5},{13,9},{2,14},{6,2},{... | collective-permute-start | bytes 540680 | tf_op jit(solution)/shard_map/ppermute | solution.py:193
  178.9 19.1 %collective-permute-start.18 = (bf16[64,1408]{1,0:T(8,128)(2,1)S(1)}, bf16[64,1408]{1,0:T(8,128)(2,1)S(1)}, u32[]{:S(2)}, u32[]{:S(2)}) collective-permute-start(bf16[64,1408]{1,0:T(8,128)(2,1)S(1)} %add_convert_fusion.g0), channel_id=1, source_target_pairs={{0,4},{4,8},{8,12},{12,0},{1,5},{5,9},{9,13},{13,1},{2,6},{6,10},{... | collective-permute-start | bytes 540680 | tf_op jit(solution)/shard_map/ppermute | solution.py:193
  183.4 14.5 %collective-permute-start.19 = (bf16[64,1408]{1,0:T(8,128)(2,1)S(1)}, bf16[64,1408]{1,0:T(8,128)(2,1)S(1)}, u32[]{:S(2)}, u32[]{:S(2)}) collective-permute-start(bf16[64,1408]{1,0:T(8,128)(2,1)S(1)} %add_convert_fusion.g0), channel_id=1, source_target_pairs={{0,8},{4,12},{8,0},{12,4},{1,9},{5,13},{9,1},{13,5},{2,10},{6,14},... | collective-permute-start | bytes 540680 | tf_op jit(solution)/shard_map/ppermute | solution.py:193
  187.1 12.2 %collective-permute-start.20 = (bf16[64,1408]{1,0:T(8,128)(2,1)S(1)}, bf16[64,1408]{1,0:T(8,128)(2,1)S(1)}, u32[]{:S(2)}, u32[]{:S(2)}) collective-permute-start(bf16[64,1408]{1,0:T(8,128)(2,1)S(1)} %add_convert_fusion.g0), channel_id=1, source_target_pairs={{0,12},{4,0},{8,4},{12,8},{1,13},{5,1},{9,5},{13,9},{2,14},{6,2},{... | collective-permute-start | bytes 540680 | tf_op jit(solution)/shard_map/ppermute | solution.py:193
  190.6 15.6 %collective-permute-start.22 = (bf16[352,256]{1,0:T(8,128)(2,1)S(1)}, bf16[352,256]{1,0:T(8,128)(2,1)S(1)}, u32[]{:S(2)}, u32[]{:S(2)}) collective-permute-start(bf16[352,256]{1,0:T(8,128)(2,1)S(1)} %slice.33), channel_id=1, source_target_pairs={{0,2},{2,0},{1,3},{3,1},{4,6},{6,4},{5,7},{7,5},{8,10},{10,8},{9,1... | collective-permute-start | bytes 540680 | tf_op jit(solution)/shard_map/ppermute | solution.py:198
  199.3 0.7 copy-start.7
  199.9 0.9 copy-start.8
  200.9 5.4 %copy-start.24 = (bf16[352,512]{1,0:T(8,128)(2,1)S(1)}, bf16[352,512]{1,0:T(8,128)(2,1)}, u32[]{:S(2)}) copy-start(bf16[352,512]{1,0:T(8,128)(2,1)} %reduce-scatter.2.cloned.1.call-done) | copy-start | bytes 1081348
  206.3 28.4 %collective-permute-start.23 = (bf16[64,1408]{1,0:T(8,128)(2,1)}, bf16[64,1408]{1,0:T(8,128)(2,1)S(1)}, u32[]{:S(2)}, u32[]{:S(2)}) collective-permute-start(bf16[64,1408]{1,0:T(8,128)(2,1)} %get-tuple-element.69), channel_id=1, source_target_pairs={{0,4},{4,8},{8,12},{12,0},{1,5},{5,9},{9,13},{13,1},{2,6},{6,10},{... | collective-permute-start | bytes 540680 | tf_op jit(solution)/shard_map/ppermute | solution.py:193
  217.5 17.3 %collective-permute-start.24 = (bf16[64,1408]{1,0:T(8,128)(2,1)}, bf16[64,1408]{1,0:T(8,128)(2,1)S(1)}, u32[]{:S(2)}, u32[]{:S(2)}) collective-permute-start(bf16[64,1408]{1,0:T(8,128)(2,1)} %get-tuple-element.70), channel_id=1, source_target_pairs={{0,8},{4,12},{8,0},{12,4},{1,9},{5,13},{9,1},{13,5},{2,10},{6,14},... | collective-permute-start | bytes 540680 | tf_op jit(solution)/shard_map/ppermute | solution.py:193
  221.4 13.3 %collective-permute-start.25 = (bf16[64,1408]{1,0:T(8,128)(2,1)}, bf16[64,1408]{1,0:T(8,128)(2,1)S(1)}, u32[]{:S(2)}, u32[]{:S(2)}) collective-permute-start(bf16[64,1408]{1,0:T(8,128)(2,1)} %get-tuple-element.71), channel_id=1, source_target_pairs={{0,12},{4,0},{8,4},{12,8},{1,13},{5,1},{9,5},{13,9},{2,14},{6,2},{... | collective-permute-start | bytes 540680 | tf_op jit(solution)/shard_map/ppermute | solution.py:193
  224.4 20.4 %all-to-all-start.1 = ((bf16[8,44,256]{2,1,0:T(8,128)(2,1)}), bf16[8,44,256]{2,1,0:T(8,128)(2,1)S(1)}, u32[]{:S(2)}, u32[]{:S(2)}) async-start(bf16[8,44,256]{2,1,0:T(8,128)(2,1)} %reshape.62), calls=%async_computation.2 | async-start | bytes 393216 | tf_op jit(solution)/shard_map/all_to_all | solution.py:351
Sparse Core Ops, SparseCore 0:
  67.2 34.1 all-gather.1
  157.5 31.9 reduce-scatter.1

commit v5 on v4

--- a/solution.py
+++ b/solution.py
@@ -286,7 +286,8 @@
         scratch_shapes=[pltpu.VMEM((width, hidden), BF), dma((COPIES,))],
         compiler_params=PARAMS,
     )(place, act, *weights)
-    *branch, caption = lax.optimization_barrier((*branch, caption))
+    branch = list(branch)
+    branch[1], caption = lax.optimization_barrier((branch[1], caption))
     caption = jnp.swapaxes(caption, 0, 1).reshape(2, -1, dec)
     encoded_rows = (in_rows.astype(F32) + add_blocks(send_blocks(branch))).astype(BF)
     encoded_blocks = gather_blocks(encoded_rows)
@@ -323,12 +324,12 @@
     give = lax.dot_general(
         encoded, jnp.concatenate([cols[1], cols[3]], axis=1), contract, preferred_element_type=F32
     ).astype(BF)
+    later = [after(cols[0], grad_rows), after(cols[2], grad_rows)]
     keep = lax.dot_general(
-        encoded, jnp.concatenate([cols[0], cols[2]], axis=1), contract, preferred_element_type=F32
+        encoded, jnp.concatenate(later, axis=1), contract, preferred_element_type=F32
     )
     sums = (keep + swap(give, "core").astype(F32)).astype(BF)
     sums = lax.psum_scatter(sums, "x", scatter_dimension=0, tiled=True)
-    sums = sums[:, :pair_cols].astype(F32) + swap(sums[:, pair_cols:], "yh").astype(F32)
 
     d_norm = pl.pallas_call(
         back_kernel,
@@ -346,9 +347,9 @@
         ],
         compiler_params=PARAMS,
     )(place, *grad_blocks, slope, *weights)
-    *d_norm, sums = lax.optimization_barrier((*d_norm, sums))
-    sums = sums.astype(BF).reshape(8, -1, pair_cols)
-    sums = lax.all_to_all(sums, ("zh", "zl"), 0, 0, tiled=True)
+    d_norm = list(d_norm)
+    d_norm[1], sums = lax.optimization_barrier((d_norm[1], sums))
+    sums = lax.all_to_all(sums.reshape(8, -1, 2 * pair_cols), ("zh", "zl"), 0, 0, tiled=True)
     d_normed = add_blocks(send_blocks(d_norm))
     _, normal, inverse = layer_norm(in_rows, enc_gain)
     scaled_grad = d_normed * enc_gain
@@ -358,10 +359,11 @@
         - normal * jnp.mean(scaled_grad * normal, axis=-1, keepdims=True)
     )
     image_rows = (grad_rows.astype(F32) + d_input).astype(BF)
-    image_rows, sums = lax.optimization_barrier((image_rows, sums))
+    image_grad = lax.all_gather(image_rows, "tensor", axis=0, tiled=True).reshape(1, patches, width)
+    image_grad, sums = lax.optimization_barrier((image_grad, sums))
     sums = jnp.sum(sums.astype(F32), axis=0)
+    sums = sums[:, :pair_cols] + swap(sums[:, pair_cols:].astype(BF), "yh").astype(F32)
     key_grad, value_grad = sums[:, :HEAD_DIM], sums[:, HEAD_DIM:]
-    image_grad = lax.all_gather(image_rows, "tensor", axis=0, tiled=True).reshape(1, patches, width)
     return (image_grad, key_grad, value_grad)
 
 

time: 272 us -> 256 us (0.941)
  the two profiles are of different devices: /device:TPU:4 before, /device:TPU:56 now
where the time goes in v5:
time: 256 us; the launch traced here: 254 us
  starting transfers between devices  95.7 us (37%)
  waiting for transfers between devices  79 us (31%)
  Pallas kernels  22.2 us (9%)
  local copies, waits for them, and re-layouts  18.2 us (7%)
  blocking collectives  16.6 us (6%)
  between operations  14.7 us (6%)
  other arithmetic  5.77 us (2%)
    ppermute x18, starting transfers between devices, shift(): lax.ppermute(value, axis, [(i, (i + by) % size) for i in range(size)])  59.5 us
    ppermute x18, waiting for transfers between devices, shift(): lax.ppermute(value, axis, [(i, (i + by) % size) for i in range(size)])  48.4 us
    ppermute x8, waiting for transfers between devices, swap(): return lax.ppermute(value, axis, [(i, i ^ bit) for i in range(size)])  28.9 us
    ppermute x8, starting transfers between devices, swap(): return lax.ppermute(value, axis, [(i, i ^ bit) for i in range(size)])  21.1 us
    all_gather x1, blocking collectives, local(): lax.all_gather(image_rows, 'tensor', axis=0, tiled=True)  16.6 us
    unnamed x43, local copies, waits for them, and re-layouts  10.5 us
    all_to_all x1, starting transfers between devices, local(): lax.all_to_all(sums.reshape(8, -1, 2 * pair_cols), ('zh', 'zl'), 0, 0, ti...  9.47 us
    all_to_all x1, starting transfers between devices, local(): caption = lax.all_to_all(sent, ('tensor', 'yh', 'core'), 0, 0, tiled=True)  5.58 us
  transfers between devices with their start and end apart: 30, of which 14 were waited for; matrix products, arithmetic and copies ran while one was open for 5% of the time, Pallas kernels for 7%

profile of v5, /device:TPU:56, one launch (start us, length us, event | category | flops | bytes accessed | tf_op | source)
XLA Modules:
  0.0 254.4 jit_solution(9953475133355096623)
XLA Ops:
  7.3 1.0 constant_dynamic-slice_fusion.1
  8.3 0.9 dynamic-slice_bitcast_fusion
  9.2 0.8 pad_maximum_fusion.1
  10.0 4.7 %collective-permute-start.1 = (bf16[704,256]{1,0:T(8,128)(2,1)}, bf16[704,256]{1,0:T(8,128)(2,1)S(1)}, u32[]{:S(2)}, u32[]{:S(2)}) collective-permute-start(bf16[704,256]{1,0:T(8,128)(2,1)} %pad_maximum_fusion.1), channel_id=1, source_target_pairs={{0,2},{2,0},{1,3},{3,1},{4,6},{6,4},{5,7},{7,5},{8,10},{10,8},{9,1... | collective-permute-start | bytes 1081352 | tf_op jit(solution)/shard_map/ppermute | solution.py:198
  16.5 16.6 %collective-permute-done.1 = bf16[704,256]{1,0:T(8,128)(2,1)S(1)} collective-permute-done((bf16[704,256]{1,0:T(8,128)(2,1)}, bf16[704,256]{1,0:T(8,128)(2,1)S(1)}, u32[]{:S(2)}, u32[]{:S(2)}) %collective-permute-start.1) | collective-permute-done | bytes 360480 | tf_op jit(solution)/shard_map/ppermute | solution.py:198
  33.1 4.7 %collective-permute-start.2 = (bf16[704,256]{1,0:T(8,128)(2,1)S(1)}, bf16[704,256]{1,0:T(8,128)(2,1)S(1)}, u32[]{:S(2)}, u32[]{:S(2)}) collective-permute-start(bf16[704,256]{1,0:T(8,128)(2,1)S(1)} %collective-permute-done.1), channel_id=1, source_target_pairs={{0,384},{128,0},{256,128},{384,256},{1,385},{129,1},{257,129},{385... | collective-permute-start | bytes 1081352 | tf_op jit(solution)/shard_map/ppermute | solution.py:193
  37.7 2.7 %collective-permute-start.3 = (bf16[704,256]{1,0:T(8,128)(2,1)S(1)}, bf16[704,256]{1,0:T(8,128)(2,1)S(1)}, u32[]{:S(2)}, u32[]{:S(2)}) collective-permute-start(bf16[704,256]{1,0:T(8,128)(2,1)S(1)} %collective-permute-done.1), channel_id=1, source_target_pairs={{0,256},{128,384},{256,0},{384,128},{1,257},{129,385},{257,1},{385... | collective-permute-start | bytes 1081352 | tf_op jit(solution)/shard_map/ppermute | solution.py:193
  40.5 2.7 %collective-permute-start.13 = (bf16[64,3456]{1,0:T(8,128)(2,1)S(1)}, bf16[64,3456]{1,0:T(8,128)(2,1)S(1)}, u32[]{:S(2)}, u32[]{:S(2)}) collective-permute-start(bf16[64,3456]{1,0:T(8,128)(2,1)S(1)} %constant_dynamic-slice_fusion), channel_id=1, source_target_pairs={{0,2},{2,0},{1,3},{3,1},{4,6},{6,4},{5,7},{7,5},{8,10},{10,8},{9,1... | collective-permute-start | bytes 1327112 | tf_op jit(solution)/shard_map/ppermute | solution.py:198
  43.2 4.3 %collective-permute-start.4 = (bf16[704,256]{1,0:T(8,128)(2,1)S(1)}, bf16[704,256]{1,0:T(8,128)(2,1)S(1)}, u32[]{:S(2)}, u32[]{:S(2)}) collective-permute-start(bf16[704,256]{1,0:T(8,128)(2,1)S(1)} %collective-permute-done.1), channel_id=1, source_target_pairs={{0,16},{16,32},{32,48},{48,64},{64,80},{80,96},{96,112},{112,0},{1... | collective-permute-start | bytes 1081352 | tf_op jit(solution)/shard_map/ppermute | solution.py:193
  47.5 0.8 constant_dynamic-update-slice_fusion.3
  48.3 4.8 %collective-permute-done.2 = bf16[704,256]{1,0:T(8,128)(2,1)S(1)} collective-permute-done((bf16[704,256]{1,0:T(8,128)(2,1)S(1)}, bf16[704,256]{1,0:T(8,128)(2,1)S(1)}, u32[]{:S(2)}, u32[]{:S(2)}) %collective-permute-start.2) | collective-permute-done | bytes 360480 | tf_op jit(solution)/shard_map/ppermute | solution.py:193
  53.1 0.8 constant_dynamic-update-slice_fusion.2
  53.9 0.8 constant_dynamic-update-slice_fusion.1
  54.6 6.5 %collective-permute-done.4 = bf16[704,256]{1,0:T(8,128)(2,1)S(1)} collective-permute-done((bf16[704,256]{1,0:T(8,128)(2,1)S(1)}, bf16[704,256]{1,0:T(8,128)(2,1)S(1)}, u32[]{:S(2)}, u32[]{:S(2)}) %collective-permute-start.4) | collective-permute-done | bytes 360480 | tf_op jit(solution)/shard_map/ppermute | solution.py:193
  61.1 0.8 constant_dynamic-update-slice_fusion.w2
  62.0 3.2 %collective-permute-done.13 = bf16[64,3456]{1,0:T(8,128)(2,1)S(1)} collective-permute-done((bf16[64,3456]{1,0:T(8,128)(2,1)S(1)}, bf16[64,3456]{1,0:T(8,128)(2,1)S(1)}, u32[]{:S(2)}, u32[]{:S(2)}) %collective-permute-start.13) | collective-permute-done | bytes 442400 | tf_op jit(solution)/shard_map/ppermute | solution.py:198
  66.1 1.1 broadcast_in_dim.2
  67.2 5.6 %all-to-all-start = ((bf16[16,2,8,2048]{3,2,1,0:T(8,128)(2,1)}), bf16[16,2,8,2048]{3,2,1,0:T(8,128)(2,1)}, u32[]{:S(2)}, u32[]{:S(2)}) async-start(bf16[16,2,8,2048]{3,2,1,0:T(8,128)(2,1)} %bitcast.8), calls=%async_computation | async-start | bytes 2097152 | tf_op jit(solution)/shard_map/all_to_all | solution.py:264
  72.9 1.4 pad_maximum_fusion.w0
  74.3 2.1 collective-permute-start
  76.4 2.3 collective-permute-start.5
  78.8 0.8 collective-permute-done.w1
  79.6 2.3 collective-permute-done.5.w3
  81.9 1.1 copy-done.2
  83.0 5.0 %encoder_up.1 = (bf16[256,1024]{1,0:T(8,128)(2,1)S(1)}, f32[256,1024]{1,0:T(8,128)S(1)}, bf16[64,1408]{1,0:T(8,128)(2,1)S(1)}) custom-call(s32[3]{0:T(128)S(1)} %pad_add_fusion.place, bf16[256,1408]{1,0:T(8,128)(2,1)S(1)} %bitcast.22, f32[1,1408]{1,0:T(1,128)S(1)} %reshape.59.gain, bf16[704,1024]{1,0:T(8,128)(2,1)S(1)} %pad_maximum_fusion.w0, ...), custom_call_target="tpu_custom_call" | custom-call | tf_op jit(solution)/shard_map/encoder_up/pallas_call | solution.py:266
  88.0 1.0 copy-done
  88.9 4.2 %encoder_down.1 = (bf16[64,1408]{1,0:T(8,128)(2,1)S(1)}, bf16[64,1408]{1,0:T(8,128)(2,1)S(1)}, bf16[64,1408]{1,0:T(8,128)(2,1)}, bf16[64,1408]{1,0:T(8,128)(2,1)}) custom-call(s32[3]{0:T(128)S(1)} %pad_add_fusion.place, bf16[256,1024]{1,0:T(8,128)(2,1)S(1)} %get-tuple-element.36.act, bf16[704,1024]{1,0:T(8,128)(2,1)S(1)} %pad_maximum_fusion.w0, ...), custom_call_target="tpu_custom_call" | custom-call | tf_op jit(solution)/shard_map/encoder_down/pallas_call | solution.py:280
  94.5 5.2 %collective-permute-start.6 = (bf16[64,1408]{1,0:T(8,128)(2,1)}, bf16[64,1408]{1,0:T(8,128)(2,1)}, u32[]{:S(2)}, u32[]{:S(2)}) collective-permute-start(bf16[64,1408]{1,0:T(8,128)(2,1)} %get-tuple-element.38), channel_id=1, source_target_pairs={{0,4},{4,8},{8,12},{12,0},{1,5},{5,9},{9,13},{13,1},{2,6},{6,10},{... | collective-permute-start | bytes 540680 | tf_op jit(solution)/shard_map/ppermute | solution.py:193
  99.7 1.9 collective-permute-start.7
  101.6 3.0 %collective-permute-start.8 = (bf16[64,1408]{1,0:T(8,128)(2,1)}, bf16[64,1408]{1,0:T(8,128)(2,1)S(1)}, u32[]{:S(2)}, u32[]{:S(2)}) collective-permute-start(bf16[64,1408]{1,0:T(8,128)(2,1)} %copy-done.7), channel_id=1, source_target_pairs={{0,12},{4,0},{8,4},{12,8},{1,13},{5,1},{9,5},{13,9},{2,14},{6,2},{... | collective-permute-start | bytes 540680 | tf_op jit(solution)/shard_map/ppermute | solution.py:193
  104.6 1.9 collective-permute-start.12
  106.6 10.1 %collective-permute-done.7 = bf16[64,1408]{1,0:T(8,128)(2,1)} collective-permute-done((bf16[64,1408]{1,0:T(8,128)(2,1)}, bf16[64,1408]{1,0:T(8,128)(2,1)}, u32[]{:S(2)}, u32[]{:S(2)}) %collective-permute-start.7) | collective-permute-done | bytes 180256 | tf_op jit(solution)/shard_map/ppermute | solution.py:193
  116.7 2.0 fusion.11
  118.7 1.9 collective-permute-start.14
  120.7 4.4 %collective-permute-start.10 = (bf16[64,1408]{1,0:T(8,128)(2,1)}, bf16[64,1408]{1,0:T(8,128)(2,1)S(1)}, u32[]{:S(2)}, u32[]{:S(2)}) collective-permute-start(bf16[64,1408]{1,0:T(8,128)(2,1)} %get-tuple-element.74.e0), channel_id=1, source_target_pairs={{0,8},{4,12},{8,0},{12,4},{1,9},{5,13},{9,1},{13,5},{2,10},{6,14},... | collective-permute-start | bytes 540680 | tf_op jit(solution)/shard_map/ppermute | solution.py:193
  125.1 1.9 collective-permute-start.11
  127.0 5.7 %collective-permute-start.9 = (bf16[64,1408]{1,0:T(8,128)(2,1)}, bf16[64,1408]{1,0:T(8,128)(2,1)S(1)}, u32[]{:S(2)}, u32[]{:S(2)}) collective-permute-start(bf16[64,1408]{1,0:T(8,128)(2,1)} %get-tuple-element.74.e0), channel_id=1, source_target_pairs={{0,4},{4,8},{8,12},{12,0},{1,5},{5,9},{9,13},{13,1},{2,6},{6,10},{... | collective-permute-start | bytes 540680 | tf_op jit(solution)/shard_map/ppermute | solution.py:193
  132.7 1.3 copy_bitcast_fusion.caption
  134.1 1.2 copy-done.8
  135.3 2.6 %query.1 = (bf16[4,128,128]{2,1,0:T(8,128)(2,1)S(1)}, bf16[4,128,128]{2,1,0:T(8,128)(2,1)S(1)}) custom-call(bf16[2,128,2048]{2,1,0:T(8,128)(2,1)S(1)} %copy_bitcast_fusion.caption, bf16[256,3456]{1,0:T(8,128)(2,1)S(1)} %maximum_maximum_fusion.p0, bf16[256,3456]{1,0:T(8,128)(2,1)} %collective-permute-done.12.p1, ...), custom_call_target="tpu_custom_call" | custom-call | tf_op jit(solution)/shard_map/query/pallas_call | solution.py:299
  138.6 3.6 %collective-permute-done.9.e1 = bf16[64,1408]{1,0:T(8,128)(2,1)S(1)} collective-permute-done((bf16[64,1408]{1,0:T(8,128)(2,1)}, bf16[64,1408]{1,0:T(8,128)(2,1)S(1)}, u32[]{:S(2)}, u32[]{:S(2)}) %collective-permute-start.9) | collective-permute-done | bytes 180256 | tf_op jit(solution)/shard_map/ppermute | solution.py:193
  142.2 5.0 %attention.1 = (bf16[64,1408]{1,0:T(8,128)(2,1)S(1)}, bf16[64,1408]{1,0:T(8,128)(2,1)S(1)}, bf16[64,1408]{1,0:T(8,128)(2,1)S(1)}, bf16[64,1408]{1,0:T(8,128)(2,1...) custom-call(bf16[64,1408]{1,0:T(8,128)(2,1)S(1)} %copy-done.3, ...), custom_call_target="tpu_custom_call" | custom-call | tf_op jit(solution)/shard_map/attention/pallas_call | solution.py:308
  147.9 2.0 collective-permute-start.23
  149.8 1.9 collective-permute-start.15
  151.7 3.9 %collective-permute-start.16 = (bf16[64,1408]{1,0:T(8,128)(2,1)S(1)}, bf16[64,1408]{1,0:T(8,128)(2,1)S(1)}, u32[]{:S(2)}, u32[]{:S(2)}) collective-permute-start(bf16[64,1408]{1,0:T(8,128)(2,1)S(1)} %get-tuple-element.52), channel_id=1, source_target_pairs={{0,8},{4,12},{8,0},{12,4},{1,9},{5,13},{9,1},{13,5},{2,10},{6,14},... | collective-permute-start | bytes 540680 | tf_op jit(solution)/shard_map/ppermute | solution.py:193
  155.7 2.1 collective-permute-start.17
  157.8 1.1 collective-permute-done.15
  158.9 11.3 %collective-permute-done.16 = bf16[64,1408]{1,0:T(8,128)(2,1)S(1)} collective-permute-done((bf16[64,1408]{1,0:T(8,128)(2,1)S(1)}, bf16[64,1408]{1,0:T(8,128)(2,1)S(1)}, u32[]{:S(2)}, u32[]{:S(2)}) %collective-permute-start.16) | collective-permute-done | bytes 180256 | tf_op jit(solution)/shard_map/ppermute | solution.py:193
  170.4 1.7 fusion
  172.1 2.1 collective-permute-start.18
  174.2 3.1 %collective-permute-start.19 = (bf16[64,1408]{1,0:T(8,128)(2,1)S(1)}, bf16[64,1408]{1,0:T(8,128)(2,1)S(1)}, u32[]{:S(2)}, u32[]{:S(2)}) collective-permute-start(bf16[64,1408]{1,0:T(8,128)(2,1)S(1)} %add_convert_fusion.g0), channel_id=1, source_target_pairs={{0,8},{4,12},{8,0},{12,4},{1,9},{5,13},{9,1},{13,5},{2,10},{6,14},... | collective-permute-start | bytes 540680 | tf_op jit(solution)/shard_map/ppermute | solution.py:193
  177.3 3.9 %collective-permute-start.20 = (bf16[64,1408]{1,0:T(8,128)(2,1)S(1)}, bf16[64,1408]{1,0:T(8,128)(2,1)S(1)}, u32[]{:S(2)}, u32[]{:S(2)}) collective-permute-start(bf16[64,1408]{1,0:T(8,128)(2,1)S(1)} %add_convert_fusion.g0), channel_id=1, source_target_pairs={{0,12},{4,0},{8,4},{12,8},{1,13},{5,1},{9,5},{13,9},{2,14},{6,2},{... | collective-permute-start | bytes 540680 | tf_op jit(solution)/shard_map/ppermute | solution.py:193
  181.4 10.3 %collective-permute-done.19.g2 = bf16[64,1408]{1,0:T(8,128)(2,1)S(1)} collective-permute-done((bf16[64,1408]{1,0:T(8,128)(2,1)S(1)}, bf16[64,1408]{1,0:T(8,128)(2,1)S(1)}, u32[]{:S(2)}, u32[]{:S(2)}) %collective-permute-start.19) | collective-permute-done | bytes 180256 | tf_op jit(solution)/shard_map/ppermute | solution.py:193
  191.7 5.3 %encoder_back.1 = (bf16[64,1408]{1,0:T(8,128)(2,1)S(1)}, bf16[64,1408]{1,0:T(8,128)(2,1)S(1)}, bf16[64,1408]{1,0:T(8,128)(2,1)}, bf16[64,1408]{1,0:T(8,128)(2,1)}) custom-call(s32[3]{0:T(128)S(1)} %pad_add_fusion.place, bf16[64,1408]{1,0:T(8,128)(2,1)S(1)} %add_convert_fusion.g0, bf16[64,1408]{1,0:T(8,128)(2,1)S(1)} %collective-permute-done.18.g1, ...), custom_call_target="tpu_custom_call" | custom-call | tf_op jit(solution)/shard_map/encoder_back/pallas_call | solution.py:334
  197.7 2.0 collective-permute-start.21
  199.8 3.3 %collective-permute-start.22 = (bf16[64,1408]{1,0:T(8,128)(2,1)}, bf16[64,1408]{1,0:T(8,128)(2,1)S(1)}, u32[]{:S(2)}, u32[]{:S(2)}) collective-permute-start(bf16[64,1408]{1,0:T(8,128)(2,1)} %get-tuple-element.57), channel_id=1, source_target_pairs={{0,8},{4,12},{8,0},{12,4},{1,9},{5,13},{9,1},{13,5},{2,10},{6,14},... | collective-permute-start | bytes 540680 | tf_op jit(solution)/shard_map/ppermute | solution.py:193
  203.1 1.6 reduce-scatter.2.cloned.1.call-done
  204.7 3.3 %collective-permute-start.24 = (bf16[64,1408]{1,0:T(8,128)(2,1)S(1)}, bf16[64,1408]{1,0:T(8,128)(2,1)S(1)}, u32[]{:S(2)}, u32[]{:S(2)}) collective-permute-start(bf16[64,1408]{1,0:T(8,128)(2,1)S(1)} %get-tuple-element.63), channel_id=1, source_target_pairs={{0,12},{4,0},{8,4},{12,8},{1,13},{5,1},{9,5},{13,9},{2,14},{6,2},{... | collective-permute-start | bytes 540680 | tf_op jit(solution)/shard_map/ppermute | solution.py:193
  208.0 1.8 reshape.63
  209.8 9.5 %all-to-all-start.1 = ((bf16[8,44,512]{2,1,0:T(8,128)(2,1)}), bf16[8,44,512]{2,1,0:T(8,128)(2,1)S(1)}, u32[]{:S(2)}, u32[]{:S(2)}) async-start(bf16[8,44,512]{2,1,0:T(8,128)(2,1)} %reshape.63), calls=%async_computation.2 | async-start | bytes 786432 | tf_op jit(solution)/shard_map/all_to_all | solution.py:352
  219.8 16.6 %all_gather.7 = bf16[256,1408]{1,0:T(8,128)(2,1)S(1)} all-gather(bf16[64,1408]{1,0:T(8,128)(2,1)S(1)} %fusion.9), channel_id=1, replica_groups=mesh['x'=4,'zh'=2,'zl'=4,'tensor'=4,'yh'=2,'core'=2] {'tensor'}, dimensions={0}, use_global_device_ids=true | all-gather | bytes 901120 | tf_op jit(solution)/shard_map/all_gather | solution.py:362
  236.4 3.6 %collective-permute-start.25 = (bf16[44,256]{1,0:T(8,128)(2,1)S(1)}, bf16[44,256]{1,0:T(8,128)(2,1)S(1)}, u32[]{:S(2)}, u32[]{:S(2)}) collective-permute-start(bf16[44,256]{1,0:T(8,128)(2,1)S(1)} %slice.39), channel_id=1, source_target_pairs={{0,2},{2,0},{1,3},{3,1},{4,6},{6,4},{5,7},{7,5},{8,10},{10,8},{9,1... | collective-permute-start | bytes 67592 | tf_op jit(solution)/shard_map/ppermute | solution.py:198
  240.0 6.0 %collective-permute-done.25 = bf16[44,256]{1,0:T(8,128)(2,1)S(1)} collective-permute-done((bf16[44,256]{1,0:T(8,128)(2,1)S(1)}, bf16[44,256]{1,0:T(8,128)(2,1)S(1)}, u32[]{:S(2)}, u32[]{:S(2)}) %collective-permute-start.25) | collective-permute-done | bytes 22560 | tf_op jit(solution)/shard_map/ppermute | solution.py:198
  246.7 0.9 copy.30
  (82 shorter events, 7.6 us)
Async XLA Ops:
  7.2 7.6 %copy-start.9 = (bf16[4,8,2048]{2,1,0:T(8,128)(2,1)S(1)}, bf16[4,8,2048]{2,1,0:T(8,128)(2,1)}, u32[]{:S(2)}) copy-start(bf16[4,8,2048]{2,1,0:T(8,128)(2,1)} %param.15) | copy-start | bytes 393220
  7.2 7.7 %copy-start.13 = (bf16[1408,128]{1,0:T(8,128)(2,1)S(1)}, bf16[1408,128]{1,0:T(8,128)(2,1)}, u32[]{:S(2)}) copy-start(bf16[1408,128]{1,0:T(8,128)(2,1)} %param.18) | copy-start | bytes 1081348
  7.2 7.9 %copy-start.14 = (bf16[1408,128]{1,0:T(8,128)(2,1)S(1)}, bf16[1408,128]{1,0:T(8,128)(2,1)}, u32[]{:S(2)}) copy-start(bf16[1408,128]{1,0:T(8,128)(2,1)} %param.19) | copy-start | bytes 1081348
  7.2 111.5 %all-gather.2.cloned.1.call-start = ((), (), s32[]{:S(2)}) async-start(), calls=%async_computation.3 | async-start | bytes 2211840 | tf_op jit(solution)/shard_map/all_gather | solution.py:295
  7.3 8.0 %copy-start.11 = (bf16[2048,128]{1,0:T(8,128)(2,1)S(1)}, bf16[2048,128]{1,0:T(8,128)(2,1)}, u32[]{:S(2)}) copy-start(bf16[2048,128]{1,0:T(8,128)(2,1)} %param.17) | copy-start | bytes 1572868
  10.0 23.1 %collective-permute-start.1 = (bf16[704,256]{1,0:T(8,128)(2,1)}, bf16[704,256]{1,0:T(8,128)(2,1)S(1)}, u32[]{:S(2)}, u32[]{:S(2)}) collective-permute-start(bf16[704,256]{1,0:T(8,128)(2,1)} %pad_maximum_fusion.1), channel_id=1, source_target_pairs={{0,2},{2,0},{1,3},{3,1},{4,6},{6,4},{5,7},{7,5},{8,10},{10,8},{9,1... | collective-permute-start | bytes 1081352 | tf_op jit(solution)/shard_map/ppermute | solution.py:198
  15.1 1.0 copy-start.10
  33.1 20.0 %collective-permute-start.2 = (bf16[704,256]{1,0:T(8,128)(2,1)S(1)}, bf16[704,256]{1,0:T(8,128)(2,1)S(1)}, u32[]{:S(2)}, u32[]{:S(2)}) collective-permute-start(bf16[704,256]{1,0:T(8,128)(2,1)S(1)} %collective-permute-done.1), channel_id=1, source_target_pairs={{0,384},{128,0},{256,128},{384,256},{1,385},{129,1},{257,129},{385... | collective-permute-start | bytes 1081352 | tf_op jit(solution)/shard_map/ppermute | solution.py:193
  37.7 16.1 %collective-permute-start.3 = (bf16[704,256]{1,0:T(8,128)(2,1)S(1)}, bf16[704,256]{1,0:T(8,128)(2,1)S(1)}, u32[]{:S(2)}, u32[]{:S(2)}) collective-permute-start(bf16[704,256]{1,0:T(8,128)(2,1)S(1)} %collective-permute-done.1), channel_id=1, source_target_pairs={{0,256},{128,384},{256,0},{384,128},{1,257},{129,385},{257,1},{385... | collective-permute-start | bytes 1081352 | tf_op jit(solution)/shard_map/ppermute | solution.py:193
  40.5 24.6 %collective-permute-start.13 = (bf16[64,3456]{1,0:T(8,128)(2,1)S(1)}, bf16[64,3456]{1,0:T(8,128)(2,1)S(1)}, u32[]{:S(2)}, u32[]{:S(2)}) collective-permute-start(bf16[64,3456]{1,0:T(8,128)(2,1)S(1)} %constant_dynamic-slice_fusion), channel_id=1, source_target_pairs={{0,2},{2,0},{1,3},{3,1},{4,6},{6,4},{5,7},{7,5},{8,10},{10,8},{9,1... | collective-permute-start | bytes 1327112 | tf_op jit(solution)/shard_map/ppermute | solution.py:198
  43.2 18.0 %collective-permute-start.4 = (bf16[704,256]{1,0:T(8,128)(2,1)S(1)}, bf16[704,256]{1,0:T(8,128)(2,1)S(1)}, u32[]{:S(2)}, u32[]{:S(2)}) collective-permute-start(bf16[704,256]{1,0:T(8,128)(2,1)S(1)} %collective-permute-done.1), channel_id=1, source_target_pairs={{0,16},{16,32},{32,48},{48,64},{64,80},{80,96},{96,112},{112,0},{1... | collective-permute-start | bytes 1081352 | tf_op jit(solution)/shard_map/ppermute | solution.py:193
  48.3 17.7 %copy-start.17 = (f32[2048]{0:T(1024)S(1)}, f32[2048]{0:T(1024)}, u32[]{:S(2)}) copy-start(f32[2048]{0:T(1024)} %param.16) | copy-start | bytes 24580
  48.3 17.8 %copy-start.15 = (bf16[4,8,2048]{2,1,0:T(8,128)(2,1)S(1)}, bf16[4,8,2048]{2,1,0:T(8,128)(2,1)}, u32[]{:S(2)}) copy-start(bf16[4,8,2048]{2,1,0:T(8,128)(2,1)} %param.21) | copy-start | bytes 393220
  65.2 0.8 copy-start.12
  67.2 34.3 %all-to-all-start = ((bf16[16,2,8,2048]{3,2,1,0:T(8,128)(2,1)}), bf16[16,2,8,2048]{3,2,1,0:T(8,128)(2,1)}, u32[]{:S(2)}, u32[]{:S(2)}) async-start(bf16[16,2,8,2048]{3,2,1,0:T(8,128)(2,1)} %bitcast.8), calls=%async_computation | async-start | bytes 2097152 | tf_op jit(solution)/shard_map/all_to_all | solution.py:264
  72.8 131.8 %reduce-scatter.2.cloned.1.call-start = ((), (), s32[]{:S(2)}) async-start(), calls=%async_computation.4 | async-start | bytes 1802240 | tf_op jit(solution)/shard_map/reduce_scatter | solution.py:332
  72.9 5.8 %copy-start.16 = (f32[1408]{0:T(1024)S(1)}, f32[1408]{0:T(1024)}, u32[]{:S(2)}) copy-start(f32[1408]{0:T(1024)} %param.12) | copy-start | bytes 16900
  74.3 5.2 %collective-permute-start = (bf16[704,1024]{1,0:T(8,128)(2,1)S(1)}, bf16[704,1024]{1,0:T(8,128)(2,1)}, u32[]{:S(2)}, u32[]{:S(2)}) collective-permute-start(bf16[704,1024]{1,0:T(8,128)(2,1)S(1)} %pad_maximum_fusion.w0), channel_id=1, source_target_pairs={{0,1},{1,0},{2,3},{3,2},{4,5},{5,4},{6,7},{7,6},{8,9},{9,8},{10,11... | collective-permute-start | bytes 4325384 | tf_op jit(solution)/shard_map/ppermute | solution.py:198
  76.4 5.5 %collective-permute-start.5 = (bf16[704,1024]{1,0:T(8,128)(2,1)}, bf16[704,1024]{1,0:T(8,128)(2,1)}, u32[]{:S(2)}, u32[]{:S(2)}) collective-permute-start(bf16[704,1024]{1,0:T(8,128)(2,1)} %constant_dynamic-update-slice_fusion.w2), channel_id=1, source_target_pairs={{0,1},{1,0},{2,3},{3,2},{4,5},{5,4},{6,7},{7,6},{8,9},{9,8},{10,11... | collective-permute-start | bytes 4325384 | tf_op jit(solution)/shard_map/ppermute | solution.py:198
  81.8 1.1 copy-start.2
  88.0 1.0 copy-start
  93.1 0.7 copy-start.6
  93.8 0.7 copy-start.7
  94.5 12.1 %collective-permute-start.6 = (bf16[64,1408]{1,0:T(8,128)(2,1)}, bf16[64,1408]{1,0:T(8,128)(2,1)}, u32[]{:S(2)}, u32[]{:S(2)}) collective-permute-start(bf16[64,1408]{1,0:T(8,128)(2,1)} %get-tuple-element.38), channel_id=1, source_target_pairs={{0,4},{4,8},{8,12},{12,0},{1,5},{5,9},{9,13},{13,1},{2,6},{6,10},{... | collective-permute-start | bytes 540680 | tf_op jit(solution)/shard_map/ppermute | solution.py:193
  99.7 17.0 %collective-permute-start.7 = (bf16[64,1408]{1,0:T(8,128)(2,1)}, bf16[64,1408]{1,0:T(8,128)(2,1)}, u32[]{:S(2)}, u32[]{:S(2)}) collective-permute-start(bf16[64,1408]{1,0:T(8,128)(2,1)} %get-tuple-element.39), channel_id=1, source_target_pairs={{0,8},{4,12},{8,0},{12,4},{1,9},{5,13},{9,1},{13,5},{2,10},{6,14},... | collective-permute-start | bytes 540680 | tf_op jit(solution)/shard_map/ppermute | solution.py:193
  101.6 15.1 %collective-permute-start.8 = (bf16[64,1408]{1,0:T(8,128)(2,1)}, bf16[64,1408]{1,0:T(8,128)(2,1)S(1)}, u32[]{:S(2)}, u32[]{:S(2)}) collective-permute-start(bf16[64,1408]{1,0:T(8,128)(2,1)} %copy-done.7), channel_id=1, source_target_pairs={{0,12},{4,0},{8,4},{12,8},{1,13},{5,1},{9,5},{13,9},{2,14},{6,2},{... | collective-permute-start | bytes 540680 | tf_op jit(solution)/shard_map/ppermute | solution.py:193
  104.6 29.4 %collective-permute-start.12 = (bf16[256,3456]{1,0:T(8,128)(2,1)S(1)}, bf16[256,3456]{1,0:T(8,128)(2,1)}, u32[]{:S(2)}, u32[]{:S(2)}) collective-permute-start(bf16[256,3456]{1,0:T(8,128)(2,1)S(1)} %maximum_maximum_fusion.p0), channel_id=1, source_target_pairs={{0,1},{1,0},{2,3},{3,2},{4,5},{5,4},{6,7},{7,6},{8,9},{9,8},{10,11... | collective-permute-start | bytes 5308424 | tf_op jit(solution)/shard_map/ppermute | solution.py:198
  118.7 15.4 %collective-permute-start.14 = (bf16[256,3456]{1,0:T(8,128)(2,1)}, bf16[256,3456]{1,0:T(8,128)(2,1)S(1)}, u32[]{:S(2)}, u32[]{:S(2)}) collective-permute-start(bf16[256,3456]{1,0:T(8,128)(2,1)} %all-gather.2.cloned.1.call-done.p2), channel_id=1, source_target_pairs={{0,1},{1,0},{2,3},{3,2},{4,5},{5,4},{6,7},{7,6},{8,9},{9,8},{10,11... | collective-permute-start | bytes 5308424 | tf_op jit(solution)/shard_map/ppermute | solution.py:198
  120.7 17.9 %collective-permute-start.10 = (bf16[64,1408]{1,0:T(8,128)(2,1)}, bf16[64,1408]{1,0:T(8,128)(2,1)S(1)}, u32[]{:S(2)}, u32[]{:S(2)}) collective-permute-start(bf16[64,1408]{1,0:T(8,128)(2,1)} %get-tuple-element.74.e0), channel_id=1, source_target_pairs={{0,8},{4,12},{8,0},{12,4},{1,9},{5,13},{9,1},{13,5},{2,10},{6,14},... | collective-permute-start | bytes 540680 | tf_op jit(solution)/shard_map/ppermute | solution.py:193
  125.1 13.5 %collective-permute-start.11 = (bf16[64,1408]{1,0:T(8,128)(2,1)}, bf16[64,1408]{1,0:T(8,128)(2,1)S(1)}, u32[]{:S(2)}, u32[]{:S(2)}) collective-permute-start(bf16[64,1408]{1,0:T(8,128)(2,1)} %get-tuple-element.74.e0), channel_id=1, source_target_pairs={{0,12},{4,0},{8,4},{12,8},{1,13},{5,1},{9,5},{13,9},{2,14},{6,2},{... | collective-permute-start | bytes 540680 | tf_op jit(solution)/shard_map/ppermute | solution.py:193
  127.0 15.2 %collective-permute-start.9 = (bf16[64,1408]{1,0:T(8,128)(2,1)}, bf16[64,1408]{1,0:T(8,128)(2,1)S(1)}, u32[]{:S(2)}, u32[]{:S(2)}) collective-permute-start(bf16[64,1408]{1,0:T(8,128)(2,1)} %get-tuple-element.74.e0), channel_id=1, source_target_pairs={{0,4},{4,8},{8,12},{12,0},{1,5},{5,9},{9,13},{13,1},{2,6},{6,10},{... | collective-permute-start | bytes 540680 | tf_op jit(solution)/shard_map/ppermute | solution.py:193
  134.1 8.1 %copy-start.3 = (bf16[64,1408]{1,0:T(8,128)(2,1)S(1)}, bf16[64,1408]{1,0:T(8,128)(2,1)}, u32[]{:S(2)}) copy-start(bf16[64,1408]{1,0:T(8,128)(2,1)} %get-tuple-element.74.e0) | copy-start | bytes 540676
  134.1 1.2 copy-start.8
  147.9 22.5 %collective-permute-start.23 = (bf16[1408,512]{1,0:T(8,128)(2,1)S(1)}, bf16[1408,512]{1,0:T(8,128)(2,1)S(1)}, u32[]{:S(2)}, u32[]{:S(2)}) collective-permute-start(bf16[1408,512]{1,0:T(8,128)(2,1)S(1)} %convolution_convert_fusion), channel_id=1, source_target_pairs={{0,1},{1,0},{2,3},{3,2},{4,5},{5,4},{6,7},{7,6},{8,9},{9,8},{10,11... | collective-permute-start | bytes 4325384 | tf_op jit(solution)/shard_map/ppermute | solution.py:198
  149.8 9.1 %collective-permute-start.15 = (bf16[64,1408]{1,0:T(8,128)(2,1)S(1)}, bf16[64,1408]{1,0:T(8,128)(2,1)S(1)}, u32[]{:S(2)}, u32[]{:S(2)}) collective-permute-start(bf16[64,1408]{1,0:T(8,128)(2,1)S(1)} %get-tuple-element.51), channel_id=1, source_target_pairs={{0,4},{4,8},{8,12},{12,0},{1,5},{5,9},{9,13},{13,1},{2,6},{6,10},{... | collective-permute-start | bytes 540680 | tf_op jit(solution)/shard_map/ppermute | solution.py:193
  151.7 18.5 %collective-permute-start.16 = (bf16[64,1408]{1,0:T(8,128)(2,1)S(1)}, bf16[64,1408]{1,0:T(8,128)(2,1)S(1)}, u32[]{:S(2)}, u32[]{:S(2)}) collective-permute-start(bf16[64,1408]{1,0:T(8,128)(2,1)S(1)} %get-tuple-element.52), channel_id=1, source_target_pairs={{0,8},{4,12},{8,0},{12,4},{1,9},{5,13},{9,1},{13,5},{2,10},{6,14},... | collective-permute-start | bytes 540680 | tf_op jit(solution)/shard_map/ppermute | solution.py:193
  155.7 14.6 %collective-permute-start.17 = (bf16[64,1408]{1,0:T(8,128)(2,1)S(1)}, bf16[64,1408]{1,0:T(8,128)(2,1)S(1)}, u32[]{:S(2)}, u32[]{:S(2)}) collective-permute-start(bf16[64,1408]{1,0:T(8,128)(2,1)S(1)} %get-tuple-element.53), channel_id=1, source_target_pairs={{0,12},{4,0},{8,4},{12,8},{1,13},{5,1},{9,5},{13,9},{2,14},{6,2},{... | collective-permute-start | bytes 540680 | tf_op jit(solution)/shard_map/ppermute | solution.py:193
  172.1 19.6 %copy-start.1 = (f32[256,1024]{1,0:T(8,128)S(1)}, f32[256,1024]{1,0:T(8,128)}, u32[]{:S(2)}) copy-start(f32[256,1024]{1,0:T(8,128)} %copy-done) | copy-start | bytes 3145732
  172.1 9.3 %collective-permute-start.18 = (bf16[64,1408]{1,0:T(8,128)(2,1)S(1)}, bf16[64,1408]{1,0:T(8,128)(2,1)S(1)}, u32[]{:S(2)}, u32[]{:S(2)}) collective-permute-start(bf16[64,1408]{1,0:T(8,128)(2,1)S(1)} %add_convert_fusion.g0), channel_id=1, source_target_pairs={{0,4},{4,8},{8,12},{12,0},{1,5},{5,9},{9,13},{13,1},{2,6},{6,10},{... | collective-permute-start | bytes 540680 | tf_op jit(solution)/shard_map/ppermute | solution.py:193
  174.2 17.5 %collective-permute-start.19 = (bf16[64,1408]{1,0:T(8,128)(2,1)S(1)}, bf16[64,1408]{1,0:T(8,128)(2,1)S(1)}, u32[]{:S(2)}, u32[]{:S(2)}) collective-permute-start(bf16[64,1408]{1,0:T(8,128)(2,1)S(1)} %add_convert_fusion.g0), channel_id=1, source_target_pairs={{0,8},{4,12},{8,0},{12,4},{1,9},{5,13},{9,1},{13,5},{2,10},{6,14},... | collective-permute-start | bytes 540680 | tf_op jit(solution)/shard_map/ppermute | solution.py:193
  177.3 14.4 %collective-permute-start.20 = (bf16[64,1408]{1,0:T(8,128)(2,1)S(1)}, bf16[64,1408]{1,0:T(8,128)(2,1)S(1)}, u32[]{:S(2)}, u32[]{:S(2)}) collective-permute-start(bf16[64,1408]{1,0:T(8,128)(2,1)S(1)} %add_convert_fusion.g0), channel_id=1, source_target_pairs={{0,12},{4,0},{8,4},{12,8},{1,13},{5,1},{9,5},{13,9},{2,14},{6,2},{... | collective-permute-start | bytes 540680 | tf_op jit(solution)/shard_map/ppermute | solution.py:193
  197.0 0.7 copy-start.4
  197.7 21.6 %copy-start.5 = (bf16[64,1408]{1,0:T(8,128)(2,1)S(1)}, bf16[64,1408]{1,0:T(8,128)(2,1)}, u32[]{:S(2)}) copy-start(bf16[64,1408]{1,0:T(8,128)(2,1)} %copy-done.4) | copy-start | bytes 540676
  197.7 21.5 %collective-permute-start.21 = (bf16[64,1408]{1,0:T(8,128)(2,1)}, bf16[64,1408]{1,0:T(8,128)(2,1)S(1)}, u32[]{:S(2)}, u32[]{:S(2)}) collective-permute-start(bf16[64,1408]{1,0:T(8,128)(2,1)} %get-tuple-element.56), channel_id=1, source_target_pairs={{0,4},{4,8},{8,12},{12,0},{1,5},{5,9},{9,13},{13,1},{2,6},{6,10},{... | collective-permute-start | bytes 540680 | tf_op jit(solution)/shard_map/ppermute | solution.py:193
  199.8 19.5 %collective-permute-start.22 = (bf16[64,1408]{1,0:T(8,128)(2,1)}, bf16[64,1408]{1,0:T(8,128)(2,1)S(1)}, u32[]{:S(2)}, u32[]{:S(2)}) collective-permute-start(bf16[64,1408]{1,0:T(8,128)(2,1)} %get-tuple-element.57), channel_id=1, source_target_pairs={{0,8},{4,12},{8,0},{12,4},{1,9},{5,13},{9,1},{13,5},{2,10},{6,14},... | collective-permute-start | bytes 540680 | tf_op jit(solution)/shard_map/ppermute | solution.py:193
  204.7 14.6 %collective-permute-start.24 = (bf16[64,1408]{1,0:T(8,128)(2,1)S(1)}, bf16[64,1408]{1,0:T(8,128)(2,1)S(1)}, u32[]{:S(2)}, u32[]{:S(2)}) collective-permute-start(bf16[64,1408]{1,0:T(8,128)(2,1)S(1)} %get-tuple-element.63), channel_id=1, source_target_pairs={{0,12},{4,0},{8,4},{12,8},{1,13},{5,1},{9,5},{13,9},{2,14},{6,2},{... | collective-permute-start | bytes 540680 | tf_op jit(solution)/shard_map/ppermute | solution.py:193
  209.8 26.6 %all-to-all-start.1 = ((bf16[8,44,512]{2,1,0:T(8,128)(2,1)}), bf16[8,44,512]{2,1,0:T(8,128)(2,1)S(1)}, u32[]{:S(2)}, u32[]{:S(2)}) async-start(bf16[8,44,512]{2,1,0:T(8,128)(2,1)} %reshape.63), calls=%async_computation.2 | async-start | bytes 786432 | tf_op jit(solution)/shard_map/all_to_all | solution.py:352
  236.4 9.6 %collective-permute-start.25 = (bf16[44,256]{1,0:T(8,128)(2,1)S(1)}, bf16[44,256]{1,0:T(8,128)(2,1)S(1)}, u32[]{:S(2)}, u32[]{:S(2)}) collective-permute-start(bf16[44,256]{1,0:T(8,128)(2,1)S(1)} %slice.39), channel_id=1, source_target_pairs={{0,2},{2,0},{1,3},{3,1},{4,6},{6,4},{5,7},{7,5},{8,10},{10,8},{9,1... | collective-permute-start | bytes 67592 | tf_op jit(solution)/shard_map/ppermute | solution.py:198
Sparse Core Ops, SparseCore 0:
  66.1 35.8 all-gather.1
  172.2 32.3 reduce-scatter.1

commit v6 on v5

--- a/solution.py
+++ b/solution.py
@@ -255,7 +255,7 @@
     text_own = jnp.concatenate([w_query.T, w_out], axis=0)
     heads_own = jnp.concatenate([pair_own, text_own], axis=1)
 
-    heads_piece = swap(quarter_of(after(heads_own, piece), lax.axis_index("x"), 0), "yh")
+    heads_piece = swap(quarter_of(after(heads_own, *pieces), lax.axis_index("x"), 0), "yh")
     heads_near = swap(after(heads_own, far), "core")
 
     text_normed = layer_norm(text_in, query_gain)[0].astype(BF)
@@ -286,13 +286,13 @@
         scratch_shapes=[pltpu.VMEM((width, hidden), BF), dma((COPIES,))],
         compiler_params=PARAMS,
     )(place, act, *weights)
+    heads_far = lax.all_gather(after(heads_piece, act), "x", axis=0, tiled=True)
     branch = list(branch)
     branch[1], caption = lax.optimization_barrier((branch[1], caption))
     caption = jnp.swapaxes(caption, 0, 1).reshape(2, -1, dec)
     encoded_rows = (in_rows.astype(F32) + add_blocks(send_blocks(branch))).astype(BF)
     encoded_blocks = gather_blocks(encoded_rows)
 
-    heads_far = lax.all_gather(after(heads_piece, far), "x", axis=0, tiled=True)
     heads = (heads_own, heads_near, heads_far, swap(after(heads_far, encoded_rows), "core"))
 
     head_shape = shape((4, caption.shape[1], HEAD_DIM), BF)

time: 256 us -> 281 us (1.098)
  waiting for transfers between devices: 79 us -> 102 us
  starting transfers between devices: 95.7 us -> 90.7 us
    all_to_all x1, waiting for transfers between devices: 0.01 us -> 12.3 us  [local(): caption = lax.all_to_all(sent, ('tensor', 'yh', 'core'), 0, 0, tiled=True)]
    ppermute x8, waiting for transfers between devices: 28.9 us -> 37.2 us  [swap(): return lax.ppermute(value, axis, [(i, i ^ bit) for i in range(size)])]
    all_to_all x1, starting transfers between devices: 9.47 us -> 4.47 us  [local(): lax.all_to_all(sums.reshape(8, -1, 2 * pair_cols), ('zh', 'zl'), 0, 0, ti...]
    ppermute x18, waiting for transfers between devices: 48.4 us -> 52.3 us  [shift(): lax.ppermute(value, axis, [(i, (i + by) % size) for i in range(size)])]
    unnamed x43 -> x35, local copies, waits for them, and re-layouts: 10.5 us -> 13 us
  transfers between devices with their start and end apart: 30 -> 30, of which waited for: 14 -> 13; matrix products, arithmetic and copies ran while one was open for 5% -> 7% of each run, Pallas kernels for 7% -> 6%
where the time goes in v6:
time: 281 us; the launch traced here: 279 us
  waiting for transfers between devices  102 us (36%)
  starting transfers between devices  90.7 us (32%)
  Pallas kernels  22.3 us (8%)
  local copies, waits for them, and re-layouts  20.7 us (7%)
  blocking collectives  17.7 us (6%)
  between operations  14.6 us (5%)
  other arithmetic  8.4 us (3%)
    ppermute x18, starting transfers between devices, shift(): lax.ppermute(value, axis, [(i, (i + by) % size) for i in range(size)])  58.8 us
    ppermute x18, waiting for transfers between devices, shift(): lax.ppermute(value, axis, [(i, (i + by) % size) for i in range(size)])  52.3 us
    ppermute x8, waiting for transfers between devices, swap(): return lax.ppermute(value, axis, [(i, i ^ bit) for i in range(size)])  37.2 us
    ppermute x8, starting transfers between devices, swap(): return lax.ppermute(value, axis, [(i, i ^ bit) for i in range(size)])  20.9 us
    all_gather x1, blocking collectives, local(): lax.all_gather(image_rows, 'tensor', axis=0, tiled=True)  17.7 us
    unnamed x35, local copies, waits for them, and re-layouts  13 us
    all_to_all x1, waiting for transfers between devices, local(): caption = lax.all_to_all(sent, ('tensor', 'yh', 'core'), 0, 0, tiled=True)  12.3 us
    all_to_all x1, starting transfers between devices, local(): caption = lax.all_to_all(sent, ('tensor', 'yh', 'core'), 0, 0, tiled=True)  6.44 us
  transfers between devices with their start and end apart: 30, of which 13 were waited for; matrix products, arithmetic and copies ran while one was open for 7% of the time, Pallas kernels for 6%

profile of v6, /device:TPU:56, one launch (start us, length us, event | category | flops | bytes accessed | tf_op | source)
XLA Modules:
  0.0 278.6 jit_solution(16367236660126889709)
XLA Ops:
  7.2 1.0 constant_dynamic-slice_fusion.1
  8.3 0.9 dynamic-slice_bitcast_fusion
  10.0 4.7 %collective-permute-start.1 = (bf16[704,256]{1,0:T(8,128)(2,1)}, bf16[704,256]{1,0:T(8,128)(2,1)}, u32[]{:S(2)}, u32[]{:S(2)}) collective-permute-start(bf16[704,256]{1,0:T(8,128)(2,1)} %pad_maximum_fusion.1), channel_id=1, source_target_pairs={{0,2},{2,0},{1,3},{3,1},{4,6},{6,4},{5,7},{7,5},{8,10},{10,8},{9,1... | collective-permute-start | bytes 1081352 | tf_op jit(solution)/shard_map/ppermute | solution.py:198
  14.8 2.1 collective-permute-start
  16.9 1.2 copy.22
  18.1 1.2 copy.23
  19.3 13.9 %collective-permute-done.1 = bf16[704,256]{1,0:T(8,128)(2,1)} collective-permute-done((bf16[704,256]{1,0:T(8,128)(2,1)}, bf16[704,256]{1,0:T(8,128)(2,1)}, u32[]{:S(2)}, u32[]{:S(2)}) %collective-permute-start.1) | collective-permute-done | bytes 360480 | tf_op jit(solution)/shard_map/ppermute | solution.py:198
  33.2 4.7 %collective-permute-start.2 = (bf16[704,256]{1,0:T(8,128)(2,1)}, bf16[704,256]{1,0:T(8,128)(2,1)S(1)}, u32[]{:S(2)}, u32[]{:S(2)}) collective-permute-start(bf16[704,256]{1,0:T(8,128)(2,1)} %collective-permute-done.1), channel_id=1, source_target_pairs={{0,384},{128,0},{256,128},{384,256},{1,385},{129,1},{257,129},{385... | collective-permute-start | bytes 1081352 | tf_op jit(solution)/shard_map/ppermute | solution.py:193
  37.8 0.9 maximum_bitcast_fusion
  38.7 2.7 collective-permute-start.3
  41.6 4.4 %collective-permute-start.4 = (bf16[704,256]{1,0:T(8,128)(2,1)}, bf16[704,256]{1,0:T(8,128)(2,1)S(1)}, u32[]{:S(2)}, u32[]{:S(2)}) collective-permute-start(bf16[704,256]{1,0:T(8,128)(2,1)} %collective-permute-done.1), channel_id=1, source_target_pairs={{0,16},{16,32},{32,48},{48,64},{64,80},{80,96},{96,112},{112,0},{1... | collective-permute-start | bytes 1081352 | tf_op jit(solution)/shard_map/ppermute | solution.py:193
  46.0 1.8 constant_dynamic-update-slice_fusion.3
  47.8 5.7 %collective-permute-done.2 = bf16[704,256]{1,0:T(8,128)(2,1)S(1)} collective-permute-done((bf16[704,256]{1,0:T(8,128)(2,1)}, bf16[704,256]{1,0:T(8,128)(2,1)S(1)}, u32[]{:S(2)}, u32[]{:S(2)}) %collective-permute-start.2) | collective-permute-done | bytes 360480 | tf_op jit(solution)/shard_map/ppermute | solution.py:193
  55.1 5.6 %collective-permute-done.4 = bf16[704,256]{1,0:T(8,128)(2,1)S(1)} collective-permute-done((bf16[704,256]{1,0:T(8,128)(2,1)}, bf16[704,256]{1,0:T(8,128)(2,1)S(1)}, u32[]{:S(2)}, u32[]{:S(2)}) %collective-permute-start.4) | collective-permute-done | bytes 360480 | tf_op jit(solution)/shard_map/ppermute | solution.py:193
  61.4 1.9 collective-permute-start.5
  63.4 1.0 copy.24
  64.4 1.6 maximum_maximum_fusion.p0
  66.1 1.9 collective-permute-start.13
  68.3 5.0 %encoder_up.1 = (bf16[256,1024]{1,0:T(8,128)(2,1)S(1)}, f32[256,1024]{1,0:T(8,128)S(1)}, bf16[64,1408]{1,0:T(8,128)(2,1)S(1)}) custom-call(s32[3]{0:T(128)S(1)} %pad_add_fusion.place, bf16[256,1408]{1,0:T(8,128)(2,1)S(1)} %bitcast.22, f32[1,1408]{1,0:T(1,128)S(1)} %reshape.59.gain, bf16[704,1024]{1,0:T(8,128)(2,1)S(1)} %pad_maximum_fusion.w0, ...), custom_call_target="tpu_custom_call" | custom-call | tf_op jit(solution)/shard_map/encoder_up/pallas_call | solution.py:266
  73.3 1.0 copy-done
  75.0 17.9 %collective-permute-done.13 = bf16[64,3456]{1,0:T(8,128)(2,1)} collective-permute-done((bf16[64,3456]{1,0:T(8,128)(2,1)S(1)}, bf16[64,3456]{1,0:T(8,128)(2,1)}, u32[]{:S(2)}, u32[]{:S(2)}) %collective-permute-start.13) | collective-permute-done | bytes 442400 | tf_op jit(solution)/shard_map/ppermute | solution.py:198
  93.8 0.9 pad_maximum_fusion.2
  94.8 1.1 broadcast_in_dim.2
  95.9 6.4 %all-to-all-start = ((bf16[16,2,8,2048]{3,2,1,0:T(8,128)(2,1)}), bf16[16,2,8,2048]{3,2,1,0:T(8,128)(2,1)}, u32[]{:S(2)}, u32[]{:S(2)}) async-start(bf16[16,2,8,2048]{3,2,1,0:T(8,128)(2,1)} %bitcast.23), calls=%async_computation | async-start | bytes 2097152 | tf_op jit(solution)/shard_map/all_to_all | solution.py:264
  102.4 1.0 copy-done.5
  103.4 4.3 %encoder_down.1 = (bf16[64,1408]{1,0:T(8,128)(2,1)S(1)}, bf16[64,1408]{1,0:T(8,128)(2,1)S(1)}, bf16[64,1408]{1,0:T(8,128)(2,1)}, bf16[64,1408]{1,0:T(8,128)(2,1)}) custom-call(s32[3]{0:T(128)S(1)} %pad_add_fusion.place, bf16[256,1024]{1,0:T(8,128)(2,1)S(1)} %copy-done.5, bf16[704,1024]{1,0:T(8,128)(2,1)S(1)} %pad_maximum_fusion.w0, ...), custom_call_target="tpu_custom_call" | custom-call | tf_op jit(solution)/shard_map/encoder_down/pallas_call | solution.py:280
  109.1 5.2 %collective-permute-start.6 = (bf16[64,1408]{1,0:T(8,128)(2,1)}, bf16[64,1408]{1,0:T(8,128)(2,1)}, u32[]{:S(2)}, u32[]{:S(2)}) collective-permute-start(bf16[64,1408]{1,0:T(8,128)(2,1)} %get-tuple-element.38), channel_id=1, source_target_pairs={{0,4},{4,8},{8,12},{12,0},{1,5},{5,9},{9,13},{13,1},{2,6},{6,10},{... | collective-permute-start | bytes 540680 | tf_op jit(solution)/shard_map/ppermute | solution.py:193
  114.2 1.9 collective-permute-start.7
  116.2 12.3 %all-to-all-done = bf16[16,2,8,2048]{3,2,1,0:T(8,128)(2,1)} async-done(((bf16[16,2,8,2048]{3,2,1,0:T(8,128)(2,1)}), bf16[16,2,8,2048]{3,2,1,0:T(8,128)(2,1)}, u32[]{:S(2)}, u32[]{:S(2)}) %all-to-all-start) | async-done | bytes 1048608 | tf_op jit(solution)/shard_map/all_to_all | solution.py:264
  128.5 3.8 %collective-permute-start.8 = (bf16[64,1408]{1,0:T(8,128)(2,1)}, bf16[64,1408]{1,0:T(8,128)(2,1)S(1)}, u32[]{:S(2)}, u32[]{:S(2)}) collective-permute-start(bf16[64,1408]{1,0:T(8,128)(2,1)} %copy-done.7), channel_id=1, source_target_pairs={{0,12},{4,0},{8,4},{12,8},{1,13},{5,1},{9,5},{13,9},{2,14},{6,2},{... | collective-permute-start | bytes 540680 | tf_op jit(solution)/shard_map/ppermute | solution.py:193
  132.3 1.9 collective-permute-start.12
  134.2 9.7 %collective-permute-done.7 = bf16[64,1408]{1,0:T(8,128)(2,1)} collective-permute-done((bf16[64,1408]{1,0:T(8,128)(2,1)}, bf16[64,1408]{1,0:T(8,128)(2,1)}, u32[]{:S(2)}, u32[]{:S(2)}) %collective-permute-start.7) | collective-permute-done | bytes 180256 | tf_op jit(solution)/shard_map/ppermute | solution.py:193
  143.9 2.0 fusion.11
  145.9 1.9 collective-permute-start.14
  147.9 2.3 collective-permute-start.10
  150.2 1.9 collective-permute-start.11
  152.2 5.7 %collective-permute-start.9 = (bf16[64,1408]{1,0:T(8,128)(2,1)}, bf16[64,1408]{1,0:T(8,128)(2,1)S(1)}, u32[]{:S(2)}, u32[]{:S(2)}) collective-permute-start(bf16[64,1408]{1,0:T(8,128)(2,1)} %get-tuple-element.74.e0), channel_id=1, source_target_pairs={{0,4},{4,8},{8,12},{12,0},{1,5},{5,9},{9,13},{13,1},{2,6},{6,10},{... | collective-permute-start | bytes 540680 | tf_op jit(solution)/shard_map/ppermute | solution.py:193
  157.9 1.3 copy_bitcast_fusion.caption
  159.3 1.2 copy-done.8
  160.5 2.6 query.1
  163.7 3.8 %collective-permute-done.9.e1 = bf16[64,1408]{1,0:T(8,128)(2,1)S(1)} collective-permute-done((bf16[64,1408]{1,0:T(8,128)(2,1)}, bf16[64,1408]{1,0:T(8,128)(2,1)S(1)}, u32[]{:S(2)}, u32[]{:S(2)}) %collective-permute-start.9) | collective-permute-done | bytes 180256 | tf_op jit(solution)/shard_map/ppermute | solution.py:193
  167.4 5.0 %attention.1 = (bf16[64,1408]{1,0:T(8,128)(2,1)S(1)}, bf16[64,1408]{1,0:T(8,128)(2,1)S(1)}, bf16[64,1408]{1,0:T(8,128)(2,1)S(1)}, bf16[64,1408]{1,0:T(8,128)(2,1...) custom-call(bf16[64,1408]{1,0:T(8,128)(2,1)S(1)} %copy-done.3, ...), custom_call_target="tpu_custom_call" | custom-call | tf_op jit(solution)/shard_map/attention/pallas_call | solution.py:308
  173.1 2.0 collective-permute-start.23
  175.0 1.9 collective-permute-start.15
  177.0 4.0 %collective-permute-start.16 = (bf16[64,1408]{1,0:T(8,128)(2,1)S(1)}, bf16[64,1408]{1,0:T(8,128)(2,1)S(1)}, u32[]{:S(2)}, u32[]{:S(2)}) collective-permute-start(bf16[64,1408]{1,0:T(8,128)(2,1)S(1)} %get-tuple-element.52), channel_id=1, source_target_pairs={{0,8},{4,12},{8,0},{12,4},{1,9},{5,13},{9,1},{13,5},{2,10},{6,14},... | collective-permute-start | bytes 540680 | tf_op jit(solution)/shard_map/ppermute | solution.py:193
  181.0 2.1 collective-permute-start.17
  183.1 1.1 collective-permute-done.15
  184.2 11.3 %collective-permute-done.16 = bf16[64,1408]{1,0:T(8,128)(2,1)S(1)} collective-permute-done((bf16[64,1408]{1,0:T(8,128)(2,1)S(1)}, bf16[64,1408]{1,0:T(8,128)(2,1)S(1)}, u32[]{:S(2)}, u32[]{:S(2)}) %collective-permute-start.16) | collective-permute-done | bytes 180256 | tf_op jit(solution)/shard_map/ppermute | solution.py:193
  195.6 1.7 fusion
  197.3 2.1 collective-permute-start.18
  199.4 3.1 %collective-permute-start.19 = (bf16[64,1408]{1,0:T(8,128)(2,1)S(1)}, bf16[64,1408]{1,0:T(8,128)(2,1)S(1)}, u32[]{:S(2)}, u32[]{:S(2)}) collective-permute-start(bf16[64,1408]{1,0:T(8,128)(2,1)S(1)} %add_convert_fusion.g0), channel_id=1, source_target_pairs={{0,8},{4,12},{8,0},{12,4},{1,9},{5,13},{9,1},{13,5},{2,10},{6,14},... | collective-permute-start | bytes 540680 | tf_op jit(solution)/shard_map/ppermute | solution.py:193
  202.5 3.9 %collective-permute-start.20 = (bf16[64,1408]{1,0:T(8,128)(2,1)S(1)}, bf16[64,1408]{1,0:T(8,128)(2,1)S(1)}, u32[]{:S(2)}, u32[]{:S(2)}) collective-permute-start(bf16[64,1408]{1,0:T(8,128)(2,1)S(1)} %add_convert_fusion.g0), channel_id=1, source_target_pairs={{0,12},{4,0},{8,4},{12,8},{1,13},{5,1},{9,5},{13,9},{2,14},{6,2},{... | collective-permute-start | bytes 540680 | tf_op jit(solution)/shard_map/ppermute | solution.py:193
  206.7 10.3 %collective-permute-done.19.g2 = bf16[64,1408]{1,0:T(8,128)(2,1)S(1)} collective-permute-done((bf16[64,1408]{1,0:T(8,128)(2,1)S(1)}, bf16[64,1408]{1,0:T(8,128)(2,1)S(1)}, u32[]{:S(2)}, u32[]{:S(2)}) %collective-permute-start.19) | collective-permute-done | bytes 180256 | tf_op jit(solution)/shard_map/ppermute | solution.py:193
  216.9 5.3 %encoder_back.1 = (bf16[64,1408]{1,0:T(8,128)(2,1)S(1)}, bf16[64,1408]{1,0:T(8,128)(2,1)S(1)}, bf16[64,1408]{1,0:T(8,128)(2,1)S(1)}, bf16[64,1408]{1,0:T(8,128)(2,1)}) custom-call(s32[3]{0:T(128)S(1)} %pad_add_fusion.place, bf16[64,1408]{1,0:T(8,128)(2,1)S(1)} %add_convert_fusion.g0, bf16[64,1408]{1,0:T(8,128)(2,1)S(1)} %collective-permute-done.18.g1, ...), custom_call_target="tpu_custom_call" | custom-call | tf_op jit(solution)/shard_map/encoder_back/pallas_call | solution.py:334
  222.2 1.9 collective-permute-start.21
  224.1 3.3 %collective-permute-start.22 = (bf16[64,1408]{1,0:T(8,128)(2,1)S(1)}, bf16[64,1408]{1,0:T(8,128)(2,1)S(1)}, u32[]{:S(2)}, u32[]{:S(2)}) collective-permute-start(bf16[64,1408]{1,0:T(8,128)(2,1)S(1)} %get-tuple-element.57), channel_id=1, source_target_pairs={{0,8},{4,12},{8,0},{12,4},{1,9},{5,13},{9,1},{13,5},{2,10},{6,14},... | collective-permute-start | bytes 540680 | tf_op jit(solution)/shard_map/ppermute | solution.py:193
  227.4 3.9 %collective-permute-start.24 = (bf16[64,1408]{1,0:T(8,128)(2,1)S(1)}, bf16[64,1408]{1,0:T(8,128)(2,1)S(1)}, u32[]{:S(2)}, u32[]{:S(2)}) collective-permute-start(bf16[64,1408]{1,0:T(8,128)(2,1)S(1)} %get-tuple-element.63), channel_id=1, source_target_pairs={{0,12},{4,0},{8,4},{12,8},{1,13},{5,1},{9,5},{13,9},{2,14},{6,2},{... | collective-permute-start | bytes 540680 | tf_op jit(solution)/shard_map/ppermute | solution.py:193
  231.4 1.8 reshape.63
  233.2 4.5 %all-to-all-start.1 = ((bf16[8,44,512]{2,1,0:T(8,128)(2,1)}), bf16[8,44,512]{2,1,0:T(8,128)(2,1)S(1)}, u32[]{:S(2)}, u32[]{:S(2)}) async-start(bf16[8,44,512]{2,1,0:T(8,128)(2,1)} %reshape.63), calls=%async_computation.2 | async-start | bytes 786432 | tf_op jit(solution)/shard_map/all_to_all | solution.py:352
  237.7 4.4 %collective-permute-done.22 = bf16[64,1408]{1,0:T(8,128)(2,1)S(1)} collective-permute-done((bf16[64,1408]{1,0:T(8,128)(2,1)S(1)}, bf16[64,1408]{1,0:T(8,128)(2,1)S(1)}, u32[]{:S(2)}, u32[]{:S(2)}) %collective-permute-start.22) | collective-permute-done | bytes 180256 | tf_op jit(solution)/shard_map/ppermute | solution.py:193
  242.6 17.7 %all_gather.7 = bf16[256,1408]{1,0:T(8,128)(2,1)S(1)} all-gather(bf16[64,1408]{1,0:T(8,128)(2,1)S(1)} %fusion.9), channel_id=1, replica_groups=mesh['x'=4,'zh'=2,'zl'=4,'tensor'=4,'yh'=2,'core'=2] {'tensor'}, dimensions={0}, use_global_device_ids=true | all-gather | bytes 901120 | tf_op jit(solution)/shard_map/all_gather | solution.py:362
  260.3 4.6 %collective-permute-start.25 = (bf16[44,256]{1,0:T(8,128)(2,1)S(1)}, bf16[44,256]{1,0:T(8,128)(2,1)S(1)}, u32[]{:S(2)}, u32[]{:S(2)}) collective-permute-start(bf16[44,256]{1,0:T(8,128)(2,1)S(1)} %slice.39), channel_id=1, source_target_pairs={{0,2},{2,0},{1,3},{3,1},{4,6},{6,4},{5,7},{7,5},{8,10},{10,8},{9,1... | collective-permute-start | bytes 67592 | tf_op jit(solution)/shard_map/ppermute | solution.py:198
  264.9 5.3 %collective-permute-done.25 = bf16[44,256]{1,0:T(8,128)(2,1)S(1)} collective-permute-done((bf16[44,256]{1,0:T(8,128)(2,1)S(1)}, bf16[44,256]{1,0:T(8,128)(2,1)S(1)}, u32[]{:S(2)}, u32[]{:S(2)}) %collective-permute-start.25) | collective-permute-done | bytes 22560 | tf_op jit(solution)/shard_map/ppermute | solution.py:198
  270.9 0.9 copy.30
  (74 shorter events, 9.5 us)
Async XLA Ops:
  7.2 7.5 %copy-start.11 = (bf16[352,1024]{1,0:T(8,128)(2,1)S(1)}, bf16[352,1024]{1,0:T(8,128)(2,1)}, u32[]{:S(2)}) copy-start(bf16[352,1024]{1,0:T(8,128)(2,1)} %param.13) | copy-start | bytes 2162692
  7.2 7.5 %copy-start.10 = (bf16[1024,352]{0,1:T(8,128)(2,1)S(1)}, bf16[1024,352]{0,1:T(8,128)(2,1)}, u32[]{:S(2)}) copy-start(bf16[1024,352]{0,1:T(8,128)(2,1)} %param.14) | copy-start | bytes 2162692
  7.2 138.8 %all-gather.2.cloned.1.call-start = ((), (), s32[]{:S(2)}) async-start(), calls=%async_computation.3 | async-start | bytes 2211840 | tf_op jit(solution)/shard_map/all_gather | solution.py:289
  10.0 23.2 %collective-permute-start.1 = (bf16[704,256]{1,0:T(8,128)(2,1)}, bf16[704,256]{1,0:T(8,128)(2,1)}, u32[]{:S(2)}, u32[]{:S(2)}) collective-permute-start(bf16[704,256]{1,0:T(8,128)(2,1)} %pad_maximum_fusion.1), channel_id=1, source_target_pairs={{0,2},{2,0},{1,3},{3,1},{4,6},{6,4},{5,7},{7,5},{8,10},{10,8},{9,1... | collective-permute-start | bytes 1081352 | tf_op jit(solution)/shard_map/ppermute | solution.py:198
  14.8 26.6 %copy-start.9 = (bf16[4,8,2048]{2,1,0:T(8,128)(2,1)S(1)}, bf16[4,8,2048]{2,1,0:T(8,128)(2,1)}, u32[]{:S(2)}) copy-start(bf16[4,8,2048]{2,1,0:T(8,128)(2,1)} %param.15) | copy-start | bytes 393220
  14.8 53.4 %collective-permute-start = (bf16[704,1024]{1,0:T(8,128)(2,1)S(1)}, bf16[704,1024]{1,0:T(8,128)(2,1)}, u32[]{:S(2)}, u32[]{:S(2)}) collective-permute-start(bf16[704,1024]{1,0:T(8,128)(2,1)S(1)} %pad_maximum_fusion.w0), channel_id=1, source_target_pairs={{0,1},{1,0},{2,3},{3,2},{4,5},{5,4},{6,7},{7,6},{8,9},{9,8},{10,11... | collective-permute-start | bytes 4325384 | tf_op jit(solution)/shard_map/ppermute | solution.py:198
  33.2 20.3 %collective-permute-start.2 = (bf16[704,256]{1,0:T(8,128)(2,1)}, bf16[704,256]{1,0:T(8,128)(2,1)S(1)}, u32[]{:S(2)}, u32[]{:S(2)}) collective-permute-start(bf16[704,256]{1,0:T(8,128)(2,1)} %collective-permute-done.1), channel_id=1, source_target_pairs={{0,384},{128,0},{256,128},{384,256},{1,385},{129,1},{257,129},{385... | collective-permute-start | bytes 1081352 | tf_op jit(solution)/shard_map/ppermute | solution.py:193
  38.7 15.5 %collective-permute-start.3 = (bf16[704,256]{1,0:T(8,128)(2,1)}, bf16[704,256]{1,0:T(8,128)(2,1)S(1)}, u32[]{:S(2)}, u32[]{:S(2)}) collective-permute-start(bf16[704,256]{1,0:T(8,128)(2,1)} %collective-permute-done.1), channel_id=1, source_target_pairs={{0,256},{128,384},{256,0},{384,128},{1,257},{129,385},{257,1},{385... | collective-permute-start | bytes 1081352 | tf_op jit(solution)/shard_map/ppermute | solution.py:193
  41.6 21.8 %copy-start.13 = (f32[1408]{0:T(1024)S(1)}, f32[1408]{0:T(1024)}, u32[]{:S(2)}) copy-start(f32[1408]{0:T(1024)} %param.12) | copy-start | bytes 16900
  41.6 21.8 %copy-start.12 = (bf16[2048,128]{1,0:T(8,128)(2,1)S(1)}, bf16[2048,128]{1,0:T(8,128)(2,1)}, u32[]{:S(2)}) copy-start(bf16[2048,128]{1,0:T(8,128)(2,1)} %param.17) | copy-start | bytes 1572868
  41.6 19.0 %collective-permute-start.4 = (bf16[704,256]{1,0:T(8,128)(2,1)}, bf16[704,256]{1,0:T(8,128)(2,1)S(1)}, u32[]{:S(2)}, u32[]{:S(2)}) collective-permute-start(bf16[704,256]{1,0:T(8,128)(2,1)} %collective-permute-done.1), channel_id=1, source_target_pairs={{0,16},{16,32},{32,48},{48,64},{64,80},{80,96},{96,112},{112,0},{1... | collective-permute-start | bytes 1081352 | tf_op jit(solution)/shard_map/ppermute | solution.py:193
  61.4 6.9 %collective-permute-start.5 = (bf16[704,1024]{1,0:T(8,128)(2,1)}, bf16[704,1024]{1,0:T(8,128)(2,1)}, u32[]{:S(2)}, u32[]{:S(2)}) collective-permute-start(bf16[704,1024]{1,0:T(8,128)(2,1)} %constant_dynamic-update-slice_fusion.w2), channel_id=1, source_target_pairs={{0,1},{1,0},{2,3},{3,2},{4,5},{5,4},{6,7},{7,6},{8,9},{9,8},{10,11... | collective-permute-start | bytes 4325384 | tf_op jit(solution)/shard_map/ppermute | solution.py:198
  64.4 3.9 %copy-start.2 = (bf16[1,256,1408]{2,1,0:T(8,128)(2,1)S(1)}, bf16[1,256,1408]{2,1,0:T(8,128)(2,1)}, u32[]{:S(2)}) copy-start(bf16[1,256,1408]{2,1,0:T(8,128)(2,1)} %param.11) | copy-start | bytes 2162692
  66.1 26.9 %collective-permute-start.13 = (bf16[64,3456]{1,0:T(8,128)(2,1)S(1)}, bf16[64,3456]{1,0:T(8,128)(2,1)}, u32[]{:S(2)}, u32[]{:S(2)}) collective-permute-start(bf16[64,3456]{1,0:T(8,128)(2,1)S(1)} %constant_dynamic-slice_fusion), channel_id=1, source_target_pairs={{0,2},{2,0},{1,3},{3,1},{4,6},{6,4},{5,7},{7,5},{8,10},{10,8},{9,1... | collective-permute-start | bytes 1327112 | tf_op jit(solution)/shard_map/ppermute | solution.py:198
  73.3 1.0 copy-start
  74.3 0.8 copy-start.4
  95.9 32.6 %all-to-all-start = ((bf16[16,2,8,2048]{3,2,1,0:T(8,128)(2,1)}), bf16[16,2,8,2048]{3,2,1,0:T(8,128)(2,1)}, u32[]{:S(2)}, u32[]{:S(2)}) async-start(bf16[16,2,8,2048]{3,2,1,0:T(8,128)(2,1)} %bitcast.23), calls=%async_computation | async-start | bytes 2097152 | tf_op jit(solution)/shard_map/all_to_all | solution.py:264
  102.3 125.1 %reduce-scatter.2.cloned.1.call-start = ((), (), s32[]{:S(2)}) async-start(), calls=%async_computation.4 | async-start | bytes 1802240 | tf_op jit(solution)/shard_map/reduce_scatter | solution.py:332
  102.4 1.0 copy-start.5
  107.7 0.7 copy-start.6
  108.4 0.7 copy-start.7
  109.1 25.1 %collective-permute-start.6 = (bf16[64,1408]{1,0:T(8,128)(2,1)}, bf16[64,1408]{1,0:T(8,128)(2,1)}, u32[]{:S(2)}, u32[]{:S(2)}) collective-permute-start(bf16[64,1408]{1,0:T(8,128)(2,1)} %get-tuple-element.38), channel_id=1, source_target_pairs={{0,4},{4,8},{8,12},{12,0},{1,5},{5,9},{9,13},{13,1},{2,6},{6,10},{... | collective-permute-start | bytes 540680 | tf_op jit(solution)/shard_map/ppermute | solution.py:193
  114.2 29.7 %collective-permute-start.7 = (bf16[64,1408]{1,0:T(8,128)(2,1)}, bf16[64,1408]{1,0:T(8,128)(2,1)}, u32[]{:S(2)}, u32[]{:S(2)}) collective-permute-start(bf16[64,1408]{1,0:T(8,128)(2,1)} %get-tuple-element.39), channel_id=1, source_target_pairs={{0,8},{4,12},{8,0},{12,4},{1,9},{5,13},{9,1},{13,5},{2,10},{6,14},... | collective-permute-start | bytes 540680 | tf_op jit(solution)/shard_map/ppermute | solution.py:193
  128.5 15.4 %collective-permute-start.8 = (bf16[64,1408]{1,0:T(8,128)(2,1)}, bf16[64,1408]{1,0:T(8,128)(2,1)S(1)}, u32[]{:S(2)}, u32[]{:S(2)}) collective-permute-start(bf16[64,1408]{1,0:T(8,128)(2,1)} %copy-done.7), channel_id=1, source_target_pairs={{0,12},{4,0},{8,4},{12,8},{1,13},{5,1},{9,5},{13,9},{2,14},{6,2},{... | collective-permute-start | bytes 540680 | tf_op jit(solution)/shard_map/ppermute | solution.py:193
  132.3 26.9 %collective-permute-start.12 = (bf16[256,3456]{1,0:T(8,128)(2,1)S(1)}, bf16[256,3456]{1,0:T(8,128)(2,1)}, u32[]{:S(2)}, u32[]{:S(2)}) collective-permute-start(bf16[256,3456]{1,0:T(8,128)(2,1)S(1)} %maximum_maximum_fusion.p0), channel_id=1, source_target_pairs={{0,1},{1,0},{2,3},{3,2},{4,5},{5,4},{6,7},{7,6},{8,9},{9,8},{10,11... | collective-permute-start | bytes 5308424 | tf_op jit(solution)/shard_map/ppermute | solution.py:198
  145.9 13.3 %collective-permute-start.14 = (bf16[256,3456]{1,0:T(8,128)(2,1)}, bf16[256,3456]{1,0:T(8,128)(2,1)S(1)}, u32[]{:S(2)}, u32[]{:S(2)}) collective-permute-start(bf16[256,3456]{1,0:T(8,128)(2,1)} %all-gather.2.cloned.1.call-done.p2), channel_id=1, source_target_pairs={{0,1},{1,0},{2,3},{3,2},{4,5},{5,4},{6,7},{7,6},{8,9},{9,8},{10,11... | collective-permute-start | bytes 5308424 | tf_op jit(solution)/shard_map/ppermute | solution.py:198
  147.9 15.8 %collective-permute-start.10 = (bf16[64,1408]{1,0:T(8,128)(2,1)}, bf16[64,1408]{1,0:T(8,128)(2,1)S(1)}, u32[]{:S(2)}, u32[]{:S(2)}) collective-permute-start(bf16[64,1408]{1,0:T(8,128)(2,1)} %get-tuple-element.74.e0), channel_id=1, source_target_pairs={{0,8},{4,12},{8,0},{12,4},{1,9},{5,13},{9,1},{13,5},{2,10},{6,14},... | collective-permute-start | bytes 540680 | tf_op jit(solution)/shard_map/ppermute | solution.py:193
  150.2 13.4 %collective-permute-start.11 = (bf16[64,1408]{1,0:T(8,128)(2,1)}, bf16[64,1408]{1,0:T(8,128)(2,1)S(1)}, u32[]{:S(2)}, u32[]{:S(2)}) collective-permute-start(bf16[64,1408]{1,0:T(8,128)(2,1)} %get-tuple-element.74.e0), channel_id=1, source_target_pairs={{0,12},{4,0},{8,4},{12,8},{1,13},{5,1},{9,5},{13,9},{2,14},{6,2},{... | collective-permute-start | bytes 540680 | tf_op jit(solution)/shard_map/ppermute | solution.py:193
  152.2 15.3 %collective-permute-start.9 = (bf16[64,1408]{1,0:T(8,128)(2,1)}, bf16[64,1408]{1,0:T(8,128)(2,1)S(1)}, u32[]{:S(2)}, u32[]{:S(2)}) collective-permute-start(bf16[64,1408]{1,0:T(8,128)(2,1)} %get-tuple-element.74.e0), channel_id=1, source_target_pairs={{0,4},{4,8},{8,12},{12,0},{1,5},{5,9},{9,13},{13,1},{2,6},{6,10},{... | collective-permute-start | bytes 540680 | tf_op jit(solution)/shard_map/ppermute | solution.py:193
  159.2 8.2 %copy-start.3 = (bf16[64,1408]{1,0:T(8,128)(2,1)S(1)}, bf16[64,1408]{1,0:T(8,128)(2,1)}, u32[]{:S(2)}) copy-start(bf16[64,1408]{1,0:T(8,128)(2,1)} %get-tuple-element.74.e0) | copy-start | bytes 540676
  159.2 1.2 copy-start.8
  173.1 22.5 %collective-permute-start.23 = (bf16[1408,512]{1,0:T(8,128)(2,1)S(1)}, bf16[1408,512]{1,0:T(8,128)(2,1)S(1)}, u32[]{:S(2)}, u32[]{:S(2)}) collective-permute-start(bf16[1408,512]{1,0:T(8,128)(2,1)S(1)} %convolution_convert_fusion), channel_id=1, source_target_pairs={{0,1},{1,0},{2,3},{3,2},{4,5},{5,4},{6,7},{7,6},{8,9},{9,8},{10,11... | collective-permute-start | bytes 4325384 | tf_op jit(solution)/shard_map/ppermute | solution.py:198
  175.0 9.1 %collective-permute-start.15 = (bf16[64,1408]{1,0:T(8,128)(2,1)S(1)}, bf16[64,1408]{1,0:T(8,128)(2,1)S(1)}, u32[]{:S(2)}, u32[]{:S(2)}) collective-permute-start(bf16[64,1408]{1,0:T(8,128)(2,1)S(1)} %get-tuple-element.51), channel_id=1, source_target_pairs={{0,4},{4,8},{8,12},{12,0},{1,5},{5,9},{9,13},{13,1},{2,6},{6,10},{... | collective-permute-start | bytes 540680 | tf_op jit(solution)/shard_map/ppermute | solution.py:193
  177.0 18.5 %collective-permute-start.16 = (bf16[64,1408]{1,0:T(8,128)(2,1)S(1)}, bf16[64,1408]{1,0:T(8,128)(2,1)S(1)}, u32[]{:S(2)}, u32[]{:S(2)}) collective-permute-start(bf16[64,1408]{1,0:T(8,128)(2,1)S(1)} %get-tuple-element.52), channel_id=1, source_target_pairs={{0,8},{4,12},{8,0},{12,4},{1,9},{5,13},{9,1},{13,5},{2,10},{6,14},... | collective-permute-start | bytes 540680 | tf_op jit(solution)/shard_map/ppermute | solution.py:193
  181.0 14.5 %collective-permute-start.17 = (bf16[64,1408]{1,0:T(8,128)(2,1)S(1)}, bf16[64,1408]{1,0:T(8,128)(2,1)S(1)}, u32[]{:S(2)}, u32[]{:S(2)}) collective-permute-start(bf16[64,1408]{1,0:T(8,128)(2,1)S(1)} %get-tuple-element.53), channel_id=1, source_target_pairs={{0,12},{4,0},{8,4},{12,8},{1,13},{5,1},{9,5},{13,9},{2,14},{6,2},{... | collective-permute-start | bytes 540680 | tf_op jit(solution)/shard_map/ppermute | solution.py:193
  197.3 19.6 %copy-start.1 = (f32[256,1024]{1,0:T(8,128)S(1)}, f32[256,1024]{1,0:T(8,128)}, u32[]{:S(2)}) copy-start(f32[256,1024]{1,0:T(8,128)} %copy-done) | copy-start | bytes 3145732
  197.3 9.3 %collective-permute-start.18 = (bf16[64,1408]{1,0:T(8,128)(2,1)S(1)}, bf16[64,1408]{1,0:T(8,128)(2,1)S(1)}, u32[]{:S(2)}, u32[]{:S(2)}) collective-permute-start(bf16[64,1408]{1,0:T(8,128)(2,1)S(1)} %add_convert_fusion.g0), channel_id=1, source_target_pairs={{0,4},{4,8},{8,12},{12,0},{1,5},{5,9},{9,13},{13,1},{2,6},{6,10},{... | collective-permute-start | bytes 540680 | tf_op jit(solution)/shard_map/ppermute | solution.py:193
  199.4 17.5 %collective-permute-start.19 = (bf16[64,1408]{1,0:T(8,128)(2,1)S(1)}, bf16[64,1408]{1,0:T(8,128)(2,1)S(1)}, u32[]{:S(2)}, u32[]{:S(2)}) collective-permute-start(bf16[64,1408]{1,0:T(8,128)(2,1)S(1)} %add_convert_fusion.g0), channel_id=1, source_target_pairs={{0,8},{4,12},{8,0},{12,4},{1,9},{5,13},{9,1},{13,5},{2,10},{6,14},... | collective-permute-start | bytes 540680 | tf_op jit(solution)/shard_map/ppermute | solution.py:193
  202.5 14.4 %collective-permute-start.20 = (bf16[64,1408]{1,0:T(8,128)(2,1)S(1)}, bf16[64,1408]{1,0:T(8,128)(2,1)S(1)}, u32[]{:S(2)}, u32[]{:S(2)}) collective-permute-start(bf16[64,1408]{1,0:T(8,128)(2,1)S(1)} %add_convert_fusion.g0), channel_id=1, source_target_pairs={{0,12},{4,0},{8,4},{12,8},{1,13},{5,1},{9,5},{13,9},{2,14},{6,2},{... | collective-permute-start | bytes 540680 | tf_op jit(solution)/shard_map/ppermute | solution.py:193
  222.2 15.5 %collective-permute-start.21 = (bf16[64,1408]{1,0:T(8,128)(2,1)}, bf16[64,1408]{1,0:T(8,128)(2,1)S(1)}, u32[]{:S(2)}, u32[]{:S(2)}) collective-permute-start(bf16[64,1408]{1,0:T(8,128)(2,1)} %get-tuple-element.56), channel_id=1, source_target_pairs={{0,4},{4,8},{8,12},{12,0},{1,5},{5,9},{9,13},{13,1},{2,6},{6,10},{... | collective-permute-start | bytes 540680 | tf_op jit(solution)/shard_map/ppermute | solution.py:193
  224.1 18.0 %collective-permute-start.22 = (bf16[64,1408]{1,0:T(8,128)(2,1)S(1)}, bf16[64,1408]{1,0:T(8,128)(2,1)S(1)}, u32[]{:S(2)}, u32[]{:S(2)}) collective-permute-start(bf16[64,1408]{1,0:T(8,128)(2,1)S(1)} %get-tuple-element.57), channel_id=1, source_target_pairs={{0,8},{4,12},{8,0},{12,4},{1,9},{5,13},{9,1},{13,5},{2,10},{6,14},... | collective-permute-start | bytes 540680 | tf_op jit(solution)/shard_map/ppermute | solution.py:193
  227.4 14.7 %collective-permute-start.24 = (bf16[64,1408]{1,0:T(8,128)(2,1)S(1)}, bf16[64,1408]{1,0:T(8,128)(2,1)S(1)}, u32[]{:S(2)}, u32[]{:S(2)}) collective-permute-start(bf16[64,1408]{1,0:T(8,128)(2,1)S(1)} %get-tuple-element.63), channel_id=1, source_target_pairs={{0,12},{4,0},{8,4},{12,8},{1,13},{5,1},{9,5},{13,9},{2,14},{6,2},{... | collective-permute-start | bytes 540680 | tf_op jit(solution)/shard_map/ppermute | solution.py:193
  233.2 27.1 %all-to-all-start.1 = ((bf16[8,44,512]{2,1,0:T(8,128)(2,1)}), bf16[8,44,512]{2,1,0:T(8,128)(2,1)S(1)}, u32[]{:S(2)}, u32[]{:S(2)}) async-start(bf16[8,44,512]{2,1,0:T(8,128)(2,1)} %reshape.63), calls=%async_computation.2 | async-start | bytes 786432 | tf_op jit(solution)/shard_map/all_to_all | solution.py:352
  260.3 9.9 %collective-permute-start.25 = (bf16[44,256]{1,0:T(8,128)(2,1)S(1)}, bf16[44,256]{1,0:T(8,128)(2,1)S(1)}, u32[]{:S(2)}, u32[]{:S(2)}) collective-permute-start(bf16[44,256]{1,0:T(8,128)(2,1)S(1)} %slice.39), channel_id=1, source_target_pairs={{0,2},{2,0},{1,3},{3,1},{4,6},{6,4},{5,7},{7,5},{8,10},{10,8},{9,1... | collective-permute-start | bytes 67592 | tf_op jit(solution)/shard_map/ppermute | solution.py:198
Sparse Core Ops, SparseCore 0:
  93.1 30.9 all-gather.1
  197.5 26.5 reduce-scatter.1
